TPU v7x, 32 devices: a whole 2x2x4 slice. The times are simulated.
32 devices in a mesh: dp: 4 (over z), fsdp: 8 (over y, x, core).
Axes of the slice: x: 2, y: 2, z: 4, core: 2. Of those that a mesh axis runs over, the one named last changes fastest.
Arguments:
- activations: bfloat16 [64, 1024, 512], P(('dp', 'fsdp')), may hold values from -6 to 6
- window_lengths: int32 [64, 4], P(('dp', 'fsdp')), may hold values from 0 to 512, as said below
- query_weight: bfloat16 [512, 512], P('fsdp', 'dp'), may hold values from -0.25 to 0.25
- key_weight: bfloat16 [512, 512], P('fsdp', 'dp'), may hold values from -0.25 to 0.25
- value_weight: bfloat16 [512, 512], P('fsdp', 'dp'), may hold values from -0.25 to 0.25
- output_weight: bfloat16 [512, 512], P('fsdp', 'dp'), may hold values from -1 to 1
- inner_weight: bfloat16 [512, 2048], P('fsdp', 'dp'), may hold values from -0.25 to 0.25
- outer_weight: bfloat16 [2048, 512], P('fsdp', 'dp'), may hold values from -0.1875 to 0.1875
- vectors: bfloat16 [8, 512], P('dp', 'fsdp')
- positions: bfloat16 [1024, 512], P('dp', 'fsdp'), may hold values from -3 to 3
- inner_bias: bfloat16 [2048], P(('dp', 'fsdp')), may hold values from -3 to 3
- output_cotangent: bfloat16 [64, 1024, 512], P(('dp', 'fsdp')), may hold values from -6 to 6
Outputs:
- block_out: bfloat16 [64, 1024, 512], P(('dp', 'fsdp'))
- input_grad: bfloat16 [64, 1024, 512], P(('dp', 'fsdp'))
- query_grad: float32 [512, 512], P('fsdp', 'dp')
- key_grad: float32 [512, 512], P('fsdp', 'dp')
- value_grad: float32 [512, 512], P('fsdp', 'dp')
- output_grad: float32 [512, 512], P('fsdp', 'dp')
- inner_grad: float32 [512, 2048], P('fsdp', 'dp')
- outer_grad: float32 [2048, 512], P('fsdp', 'dp')
- vectors_grad: float32 [8, 512], P('dp', 'fsdp')
- positions_grad: float32 [1024, 512], P('dp', 'fsdp')
- inner_bias_grad: float32 [2048], P(('dp', 'fsdp'))
Inputs may be any that keep to these rules, and one draw needn't show every extreme that they name: `window_lengths`: each row holds windows of 256 or 512 characters that sum to 1024, then zeros.
All inputs are finite; a program needn't handle non-finite values.
Results may differ from a plain program's by a relative error of at most 0.014.
The roundings to bfloat16 on the way count: a program that leaves them out, or rounds other values in their place, can miss the bound.
Values may be sent and summed in bfloat16 or wider, within the bound.
A program may use at most 192 MiB of HBM per device.

v0:
```python
import jax
import jax.numpy as jnp
from jax import lax
from jax.sharding import PartitionSpec as P

H = 8
HD = 64
WIN = 256


def gelu_tanh(value):
    return (
        0.5
        * value
        * (1.0 + jnp.tanh(0.7978845608028654 * (value + 0.044715 * value * value * value)))
    )


def layer_norm(value, gain, shift):
    center = value - jnp.mean(value, -1, keepdims=True)
    spread = jnp.mean(center * center, -1, keepdims=True)
    return center * lax.rsqrt(spread + 1e-05) * gain + shift


def window_ids(window_lengths, length):
    bounds = jnp.cumsum(window_lengths, -1)
    places = jnp.arange(length, dtype=jnp.int32)
    return jnp.sum((places[None, :, None] >= bounds[:, None, :]).astype(jnp.int32), -1)


def product(left, right):
    return jnp.dot(left, right, preferred_element_type=jnp.float32)


def left_product(left, right):
    return lax.dot_general(
        left, right, (((0,), (0,)), ((), ())), preferred_element_type=jnp.float32
    )


def right_product(left, right):
    return lax.dot_general(
        left, right, (((1,), (1,)), ((), ())), preferred_element_type=jnp.float32
    )


def column_sum(value):
    return jnp.sum(value.astype(jnp.float32), 0)


def bias_order(flat, first, second):
    return flat.reshape(first, second, -1).transpose(1, 0, 2).reshape(-1)


def fetch_params(
    query_weight,
    key_weight,
    value_weight,
    output_weight,
    inner_weight,
    outer_weight,
    vectors,
    positions,
    inner_bias,
):
    inner = (
        lax.all_gather(query_weight, "dp", axis=1, tiled=True),
        lax.all_gather(key_weight, "dp", axis=1, tiled=True),
        lax.all_gather(value_weight, "dp", axis=1, tiled=True),
        lax.all_gather(output_weight, "dp", axis=1, tiled=True),
        lax.all_gather(inner_weight, "dp", axis=1, tiled=True),
        lax.all_gather(outer_weight, "dp", axis=1, tiled=True),
        lax.all_gather(vectors, "dp", axis=0, tiled=True),
        lax.all_gather(positions, "dp", axis=0, tiled=True),
        lax.all_gather(inner_bias, "dp", axis=0, tiled=True),
    )
    whole = (
        lax.all_gather(inner[0], "fsdp", axis=0, tiled=True),
        lax.all_gather(inner[1], "fsdp", axis=0, tiled=True),
        lax.all_gather(inner[2], "fsdp", axis=0, tiled=True),
        lax.all_gather(inner[3], "fsdp", axis=0, tiled=True),
        lax.all_gather(inner[4], "fsdp", axis=0, tiled=True),
        lax.all_gather(inner[5], "fsdp", axis=0, tiled=True),
        lax.all_gather(inner[6], "fsdp", axis=1, tiled=True),
        lax.all_gather(inner[7], "fsdp", axis=1, tiled=True),
        lax.all_gather(inner[8], "fsdp", axis=0, tiled=True),
    )
    return whole[:8] + (bias_order(whole[8], lax.axis_size("fsdp"), lax.axis_size("dp")),)


def refetch_params(
    query_weight,
    key_weight,
    value_weight,
    output_weight,
    inner_weight,
    outer_weight,
    vectors,
    positions,
    inner_bias,
):
    inner = (
        lax.all_gather(query_weight, "dp", axis=1, tiled=True),
        lax.all_gather(key_weight, "dp", axis=1, tiled=True),
        lax.all_gather(value_weight, "dp", axis=1, tiled=True),
        lax.all_gather(output_weight, "dp", axis=1, tiled=True),
        lax.all_gather(inner_weight, "dp", axis=1, tiled=True),
        lax.all_gather(outer_weight, "dp", axis=1, tiled=True),
        lax.all_gather(vectors, "dp", axis=0, tiled=True),
        lax.all_gather(positions, "dp", axis=0, tiled=True),
        lax.all_gather(inner_bias, "dp", axis=0, tiled=True),
    )
    whole = (
        lax.all_gather(inner[0], "fsdp", axis=0, tiled=True),
        lax.all_gather(inner[1], "fsdp", axis=0, tiled=True),
        lax.all_gather(inner[2], "fsdp", axis=0, tiled=True),
        lax.all_gather(inner[3], "fsdp", axis=0, tiled=True),
        lax.all_gather(inner[4], "fsdp", axis=0, tiled=True),
        lax.all_gather(inner[5], "fsdp", axis=0, tiled=True),
        lax.all_gather(inner[6], "fsdp", axis=1, tiled=True),
        lax.all_gather(inner[7], "fsdp", axis=1, tiled=True),
        lax.all_gather(inner[8], "fsdp", axis=0, tiled=True),
    )
    return whole[:8] + (bias_order(whole[8], lax.axis_size("fsdp"), lax.axis_size("dp")),)


def block_pieces(queries, keys_pad, values_pad, window, window_pad, index, blocks):
    block = 2 * WIN
    row_index = index // blocks
    begin_at = index % blocks * block
    query_block = lax.dynamic_slice(queries, (row_index, begin_at, 0, 0), (1, block, H, HD))[0]
    key_block = lax.dynamic_slice(keys_pad, (row_index, begin_at, 0, 0), (1, 2 * block, H, HD))[0]
    value_block = lax.dynamic_slice(values_pad, (row_index, begin_at, 0, 0), (1, 2 * block, H, HD))[
        0
    ]
    query_ids = lax.dynamic_slice(window, (row_index, begin_at), (1, block))[0]
    key_ids = lax.dynamic_slice(window_pad, (row_index, begin_at), (1, 2 * block))[0]
    offsets = jnp.arange(block, dtype=jnp.int32)
    reaches = jnp.arange(2 * block, dtype=jnp.int32)
    allowed = (query_ids[:, None] == key_ids[None, :]) & (
        reaches[None, :] <= offsets[:, None] + block
    )
    scores = (
        jnp.einsum("qhd,khd->hqk", query_block, key_block, preferred_element_type=jnp.float32)
        * 0.125
    )
    scores = jnp.where(allowed[None], scores, -1e30)
    return (scores, query_block, key_block, value_block, row_index, begin_at)


def padded_inputs(keys_all, values_all, window):
    block = 2 * WIN
    keys_pad = jnp.pad(keys_all, ((0, 0), (block, 0), (0, 0), (0, 0)))
    values_pad = jnp.pad(values_all, ((0, 0), (block, 0), (0, 0), (0, 0)))
    window_pad = jnp.pad(window, ((0, 0), (block, 0)), constant_values=-1)
    return (keys_pad, values_pad, window_pad)


def attend_forward(queries, keys_all, values_all, window):
    row_count, length = window.shape
    blocks = length // (2 * WIN)
    keys_pad, values_pad, window_pad = padded_inputs(keys_all, values_all, window)

    def one_block(index):
        scores, query_block, key_block, value_block, row_index, begin_at = block_pieces(
            queries, keys_pad, values_pad, window, window_pad, index, blocks
        )
        peak = jnp.max(scores, -1, keepdims=True)
        expo = jnp.exp(scores - peak)
        total = jnp.sum(expo, -1, keepdims=True)
        probs_low = (expo / total).astype(jnp.bfloat16)
        context = jnp.einsum(
            "hqk,khd->qhd", probs_low, value_block, preferred_element_type=jnp.float32
        )
        return (context, peak[:, :, 0] + jnp.log(total[:, :, 0]))

    context, log_totals = lax.map(one_block, jnp.arange(row_count * blocks, dtype=jnp.int32))
    return (context.reshape(row_count, length, H * HD), log_totals)


def attend_backward(queries, keys_all, values_all, window, context_grad, log_totals):
    row_count, length = window.shape
    block = 2 * WIN
    blocks = length // block
    keys_pad, values_pad, window_pad = padded_inputs(keys_all, values_all, window)

    def one_step(carry, index):
        key_sums, value_sums = carry
        scores, query_block, key_block, value_block, row_index, begin_at = block_pieces(
            queries, keys_pad, values_pad, window, window_pad, index, blocks
        )
        grad_block = lax.dynamic_slice(
            context_grad, (row_index, begin_at, 0, 0), (1, block, H, HD)
        )[0]
        probs = jnp.exp(scores - log_totals[index][:, :, None])
        prob_grad = jnp.einsum(
            "qhd,khd->hqk", grad_block, value_block, preferred_element_type=jnp.float32
        )
        inner = jnp.sum(probs * prob_grad, -1, keepdims=True)
        score_grad = (probs * (prob_grad - inner)).astype(jnp.bfloat16)
        query_part = (
            jnp.einsum("hqk,khd->qhd", score_grad, key_block, preferred_element_type=jnp.float32)
            * 0.125
        )
        key_part = (
            jnp.einsum("hqk,qhd->khd", score_grad, query_block, preferred_element_type=jnp.float32)
            * 0.125
        )
        value_part = jnp.einsum(
            "hqk,qhd->khd",
            probs.astype(jnp.bfloat16),
            grad_block,
            preferred_element_type=jnp.float32,
        )
        place = (row_index, begin_at, 0, 0)
        key_sums = lax.dynamic_update_slice(
            key_sums,
            lax.dynamic_slice(key_sums, place, (1, 2 * block, H, HD)) + key_part[None],
            place,
        )
        value_sums = lax.dynamic_update_slice(
            value_sums,
            lax.dynamic_slice(value_sums, place, (1, 2 * block, H, HD)) + value_part[None],
            place,
        )
        return ((key_sums, value_sums), query_part)

    zeros = jnp.zeros((row_count, length + block, H, HD), jnp.float32)
    (key_sums, value_sums), query_parts = lax.scan(
        one_step, (zeros, zeros), jnp.arange(row_count * blocks, dtype=jnp.int32)
    )
    return (
        query_parts.reshape(row_count, length, H, HD),
        key_sums[:, block:],
        value_sums[:, block:],
    )


def shards(
    activations,
    window_lengths,
    query_weight,
    key_weight,
    value_weight,
    output_weight,
    inner_weight,
    outer_weight,
    vectors,
    positions,
    inner_bias,
    output_cotangent,
):
    row_count, length, width = activations.shape
    head_shape = (row_count, length, H, HD)
    params = fetch_params(
        query_weight,
        key_weight,
        value_weight,
        output_weight,
        inner_weight,
        outer_weight,
        vectors,
        positions,
        inner_bias,
    )
    (
        query_full,
        key_full,
        value_full,
        output_full,
        inner_full,
        outer_full,
        vector_full,
        position_full,
        bias_full,
    ) = params
    vector_rows = vector_full.astype(jnp.float32)
    window = window_ids(window_lengths, length)
    start_sum = (activations.astype(jnp.float32) + position_full.astype(jnp.float32)[None]).reshape(
        -1, width
    )
    start_low = start_sum.astype(jnp.bfloat16)
    queries = (
        (product(start_low, query_full) + vector_rows[0]).astype(jnp.bfloat16).reshape(head_shape)
    )
    keys_all = product(start_low, key_full).astype(jnp.bfloat16).reshape(head_shape)
    values_all = (
        (product(start_low, value_full) + vector_rows[1]).astype(jnp.bfloat16).reshape(head_shape)
    )
    context, log_totals = attend_forward(queries, keys_all, values_all, window)
    context_low = context.reshape(-1, width).astype(jnp.bfloat16)
    attn_out = product(context_low, output_full) + vector_rows[2]
    normed, first_pull = jax.vjp(layer_norm, start_sum + attn_out, vector_rows[3], vector_rows[4])
    normed_low = normed.astype(jnp.bfloat16)
    pre_act = product(normed_low, inner_full) + bias_full.astype(jnp.float32)
    act_value, act_pull = jax.vjp(gelu_tanh, pre_act)
    act_low = act_value.astype(jnp.bfloat16)
    branch = product(act_low, outer_full) + vector_rows[5]
    result, second_pull = jax.vjp(layer_norm, normed + branch, vector_rows[6], vector_rows[7])
    block_out = result.reshape(row_count, length, width).astype(jnp.bfloat16)
    back_params = refetch_params(
        query_weight,
        key_weight,
        value_weight,
        output_weight,
        inner_weight,
        outer_weight,
        vectors,
        positions,
        inner_bias,
    )
    back_query, back_key, back_value, back_output, back_inner, back_outer = back_params[:6]
    second_grad, gain_two, shift_two = second_pull(
        output_cotangent.reshape(-1, width).astype(jnp.float32)
    )
    branch_grad = second_grad.astype(jnp.bfloat16)
    outer_local = left_product(act_low, branch_grad)
    act_grad = right_product(branch_grad, back_outer)
    (pre_grad,) = act_pull(act_grad)
    pre_low = pre_grad.astype(jnp.bfloat16)
    inner_local = left_product(normed_low, pre_low)
    normed_grad = right_product(pre_low, back_inner) + second_grad
    first_grad, gain_one, shift_one = first_pull(normed_grad)
    attn_grad = first_grad.astype(jnp.bfloat16)
    output_local = left_product(context_low, attn_grad)
    context_grad = right_product(attn_grad, back_output).astype(jnp.bfloat16).reshape(head_shape)
    query_part, key_part, value_part = attend_backward(
        queries, keys_all, values_all, window, context_grad, log_totals
    )
    query_low = query_part.reshape(-1, width).astype(jnp.bfloat16)
    key_low = key_part.reshape(-1, width).astype(jnp.bfloat16)
    value_low = value_part.reshape(-1, width).astype(jnp.bfloat16)
    start_grad = (
        first_grad
        + right_product(query_low, back_query)
        + right_product(key_low, back_key)
        + right_product(value_low, back_value)
    )
    start_rows = start_grad.reshape(row_count, length, width)
    input_grad = start_rows.astype(jnp.bfloat16)
    position_local = jnp.sum(start_rows, 0)
    query_local = left_product(start_low, query_low)
    key_local = left_product(start_low, key_low)
    value_local = left_product(start_low, value_low)
    vector_local = jnp.stack(
        [
            column_sum(query_low),
            column_sum(value_low),
            column_sum(attn_grad),
            gain_one,
            shift_one,
            column_sum(branch_grad),
            gain_two,
            shift_two,
        ]
    )
    bias_sums = column_sum(pre_low)
    bias_local = bias_order(bias_sums, lax.axis_size("dp"), lax.axis_size("fsdp"))
    outer_sums = (
        lax.psum_scatter(query_local, "fsdp", scatter_dimension=0, tiled=True),
        lax.psum_scatter(key_local, "fsdp", scatter_dimension=0, tiled=True),
        lax.psum_scatter(value_local, "fsdp", scatter_dimension=0, tiled=True),
        lax.psum_scatter(output_local, "fsdp", scatter_dimension=0, tiled=True),
        lax.psum_scatter(inner_local, "fsdp", scatter_dimension=0, tiled=True),
        lax.psum_scatter(outer_local, "fsdp", scatter_dimension=0, tiled=True),
        lax.psum_scatter(vector_local, "fsdp", scatter_dimension=1, tiled=True),
        lax.psum_scatter(position_local, "fsdp", scatter_dimension=1, tiled=True),
        lax.psum_scatter(bias_local, "fsdp", scatter_dimension=0, tiled=True),
    )
    owned = (
        lax.psum_scatter(outer_sums[0], "dp", scatter_dimension=1, tiled=True),
        lax.psum_scatter(outer_sums[1], "dp", scatter_dimension=1, tiled=True),
        lax.psum_scatter(outer_sums[2], "dp", scatter_dimension=1, tiled=True),
        lax.psum_scatter(outer_sums[3], "dp", scatter_dimension=1, tiled=True),
        lax.psum_scatter(outer_sums[4], "dp", scatter_dimension=1, tiled=True),
        lax.psum_scatter(outer_sums[5], "dp", scatter_dimension=1, tiled=True),
        lax.psum_scatter(outer_sums[6], "dp", scatter_dimension=0, tiled=True),
        lax.psum_scatter(outer_sums[7], "dp", scatter_dimension=0, tiled=True),
        lax.psum_scatter(outer_sums[8], "dp", scatter_dimension=0, tiled=True),
    )
    return (
        block_out,
        input_grad,
        owned[0],
        owned[1],
        owned[2],
        owned[3],
        owned[4],
        owned[5],
        owned[6],
        owned[7],
        owned[8],
    )


def solution(mesh):
    placed = (
        P(("dp", "fsdp"), None, None),
        P(("dp", "fsdp"), None),
        P("fsdp", "dp"),
        P("fsdp", "dp"),
        P("fsdp", "dp"),
        P("fsdp", "dp"),
        P("fsdp", "dp"),
        P("fsdp", "dp"),
        P("dp", "fsdp"),
        P("dp", "fsdp"),
        P(("dp", "fsdp")),
        P(("dp", "fsdp"), None, None),
    )
    return jax.shard_map(
        shards,
        mesh=mesh,
        in_specs=placed,
        out_specs=(
            P(("dp", "fsdp"), None, None),
            P(("dp", "fsdp"), None, None),
            P("fsdp", "dp"),
            P("fsdp", "dp"),
            P("fsdp", "dp"),
            P("fsdp", "dp"),
            P("fsdp", "dp"),
            P("fsdp", "dp"),
            P("dp", "fsdp"),
            P("dp", "fsdp"),
            P(("dp", "fsdp")),
        ),
        check_vma=False,
    )
```

profile of v0, /device:TPU:0, one launch (start us, length us, event | category | flops | bytes accessed | tf_op | source)
XLA Modules:
  0.0 1168.2 jit_solution(9578939288833884458)
XLA Ops:
  7.2 16.9 %all_gather.66 = bf16[1024,64]{0,1:T(8,128)(2,1)} all-gather(bf16[256,64]{0,1:T(8,128)(2,1)} %param.25), channel_id=1, replica_groups=mesh['dp'=4,'fsdp'=8] {'dp'}, dimensions={0}, use_global_device_ids=true | all-gather | bytes 163840 | tf_op jit(solution)/shard_map/all_gather | solution.py:74
  24.2 15.1 %all_gather.78 = bf16[64,2048]{1,0:T(8,128)(2,1)} all-gather(bf16[64,512]{1,0:T(8,128)(2,1)} %param.22), channel_id=1, replica_groups=mesh['dp'=4,'fsdp'=8] {'dp'}, dimensions={1}, use_global_device_ids=true | all-gather | bytes 327680 | tf_op jit(solution)/shard_map/all_gather | solution.py:71
  39.4 14.0 %all_gather.82 = bf16[256,512]{1,0:T(8,128)(2,1)} all-gather(bf16[256,128]{1,0:T(8,128)(2,1)} %param.23), channel_id=1, replica_groups=mesh['dp'=4,'fsdp'=8] {'dp'}, dimensions={1}, use_global_device_ids=true | all-gather | bytes 327680 | tf_op jit(solution)/shard_map/all_gather | solution.py:72
  94.6 12.2 %all_gather.72 = bf16[64,512]{1,0:T(8,128)(2,1)S(1)} all-gather(bf16[64,128]{1,0:T(8,128)(2,1)} %param.18), channel_id=1, replica_groups=mesh['dp'=4,'fsdp'=8] {'dp'}, dimensions={1}, use_global_device_ids=true | all-gather | bytes 81920 | tf_op jit(solution)/shard_map/all_gather | solution.py:67
  106.8 12.2 %all_gather.74 = bf16[64,512]{1,0:T(8,128)(2,1)S(1)} all-gather(bf16[64,128]{1,0:T(8,128)(2,1)} %param.19), channel_id=1, replica_groups=mesh['dp'=4,'fsdp'=8] {'dp'}, dimensions={1}, use_global_device_ids=true | all-gather | bytes 81920 | tf_op jit(solution)/shard_map/all_gather | solution.py:68
  119.0 12.2 %all_gather.68 = bf16[64,512]{1,0:T(8,128)(2,1)S(1)} all-gather(bf16[64,128]{1,0:T(8,128)(2,1)} %param.20), channel_id=1, replica_groups=mesh['dp'=4,'fsdp'=8] {'dp'}, dimensions={1}, use_global_device_ids=true | all-gather | bytes 81920 | tf_op jit(solution)/shard_map/all_gather | solution.py:69
  131.2 12.2 %all_gather.76 = bf16[64,512]{1,0:T(8,128)(2,1)S(1)} all-gather(bf16[64,128]{1,0:T(8,128)(2,1)} %param.21), channel_id=1, replica_groups=mesh['dp'=4,'fsdp'=8] {'dp'}, dimensions={1}, use_global_device_ids=true | all-gather | bytes 81920 | tf_op jit(solution)/shard_map/all_gather | solution.py:70
  226.4 83.3 %while.30 = (s32[]{:T(128)}, bf16[4,512,8,64]{1,3,2,0:T(8,128)(2,1)}, f32[4,8,512]{2,1,0:T(8,128)S(1)}, s32[4]{0:T(128)S(1)}, bf16[2,1536,8,64]{1,3,2,0:T(8,128)...) while((s32[]{:T(128)}, ...), condition=%wide.region_5.6_spmd, body=%wide.region_2.5_spmd.sunk | while | flops 1125642752 | bytes 73032216 | solution.py:177
  318.0 14.7 %multiply_convert_fusion.1 = (bf16[2048,2048]{1,0:T(8,128)(2,1)}, f32[2048,2048]{1,0:T(8,128)}) fusion(f32[2048]{0:T(1024)S(1)} %copy-done.42, bf16[512,2048]{1,0:T(8,128)(2,1)} %all-gather.9.cloned.1.call-done, f32[2048,512]{1,0:T(8,128)} %copy-done.1, f32[512]{0:T(512)S(1)} %bitcast.268, f32[512]{0:T(512)S(1)} %bitcast.263, f32[2048]{0:T(1024)S(1)} %fusion.57, ...), kind=kOutput, calls=%fused_computation.70 | convolution fusion | flops 4342153216 | bytes 31485952 | tf_op jit(solution)/shard_map/dot_general | solution.py:32
  352.2 22.7 %convert_reduce_fusion = (f32[2048]{0:T(1024)}, bf16[2048,2048]{1,0:T(8,128)(2,1)}) fusion(bf16[2048,512]{1,0:T(8,128)(2,1)S(1)} %get-tuple-element.496, bf16[2048,512]{1,0:T(8,128)(2,1)S(1)} %copy-done.51, f32[2048,2048]{1,0:T(8,128)} %get-tuple-element.525, f32[2048]{0:T(1024)S(1)} %copy-done.42), kind=kOutput, calls=%fused_computation.69 | convolution fusion | flops 4408211456 | bytes 29376512 | tf_op jit(solution)/shard_map/dot_general | solution.py:42
  412.2 228.8 %while.31 = (s32[]{:T(128)}, f32[2,1536,8,64]{1,3,2,0:T(8,128)}, f32[2,1536,8,64]{1,3,2,0:T(8,128)}, bf16[4,512,8,64]{1,3,2,0:T(8,128)(2,1)}, s32[4]{0:T(128)S(1...) while((s32[]{:T(128)}, f32[2,1536,8,64]{1,3,2,0:T(8,128)}, ...), condition=%wide.region_16.17_spmd, body=%wide.region_14.16_spmd.sunk | while | flops 2725507584 | bytes 225557120 | solution.py:229
  427.5 12.8 %multiply_reduce_fusion.6 = (f32[8,512]{1,0:T(8,128)S(1)}, f32[8,512,1024]{2,1,0:T(8,128)}) fusion(f32[8,512,1024]{2,1,0:T(8,128)} %fusion.144, f32[8,512]{1,0:T(8,128)S(1)} %dynamic-slice_bitcast_fusion.2, bf16[2,1536,8,64]{1,3,2,0:T(8,128)(2,1)} %get-tuple-element.765, s32[]{:T(128)S(6)} %select_n.151, s32[]{:T(128)S(6)} %select_n.153, ...), kind=kOutput, calls=%fused_computation.24.clone.1 | convolution fusion | flops 557838336 | bytes 35686400 | tf_op jit(solution)/shard_map/while/body/eval_jaxpr/qhd,khd->hqk/dot_general | solution.py:144
  440.3 11.5 multiply_convert_fusion.3
  484.5 12.8 %multiply_reduce_fusion.6 = (f32[8,512]{1,0:T(8,128)S(1)}, f32[8,512,1024]{2,1,0:T(8,128)}) fusion(f32[8,512,1024]{2,1,0:T(8,128)} %fusion.144, f32[8,512]{1,0:T(8,128)S(1)} %dynamic-slice_bitcast_fusion.2, bf16[2,1536,8,64]{1,3,2,0:T(8,128)(2,1)} %get-tuple-element.765, s32[]{:T(128)S(6)} %select_n.151, s32[]{:T(128)S(6)} %select_n.153, ...), kind=kOutput, calls=%fused_computation.24.clone.1 | convolution fusion | flops 557838336 | bytes 35686400 | tf_op jit(solution)/shard_map/while/body/eval_jaxpr/qhd,khd->hqk/dot_general | solution.py:144
  497.3 11.5 multiply_convert_fusion.3
  541.6 12.8 %multiply_reduce_fusion.6 = (f32[8,512]{1,0:T(8,128)S(1)}, f32[8,512,1024]{2,1,0:T(8,128)}) fusion(f32[8,512,1024]{2,1,0:T(8,128)} %fusion.144, f32[8,512]{1,0:T(8,128)S(1)} %dynamic-slice_bitcast_fusion.2, bf16[2,1536,8,64]{1,3,2,0:T(8,128)(2,1)} %get-tuple-element.765, s32[]{:T(128)S(6)} %select_n.151, s32[]{:T(128)S(6)} %select_n.153, ...), kind=kOutput, calls=%fused_computation.24.clone.1 | convolution fusion | flops 557838336 | bytes 35686400 | tf_op jit(solution)/shard_map/while/body/eval_jaxpr/qhd,khd->hqk/dot_general | solution.py:144
  598.7 12.8 %multiply_reduce_fusion.6 = (f32[8,512]{1,0:T(8,128)S(1)}, f32[8,512,1024]{2,1,0:T(8,128)}) fusion(f32[8,512,1024]{2,1,0:T(8,128)} %fusion.144, f32[8,512]{1,0:T(8,128)S(1)} %dynamic-slice_bitcast_fusion.2, bf16[2,1536,8,64]{1,3,2,0:T(8,128)(2,1)} %get-tuple-element.765, s32[]{:T(128)S(6)} %select_n.151, s32[]{:T(128)S(6)} %select_n.153, ...), kind=kOutput, calls=%fused_computation.24.clone.1 | convolution fusion | flops 557838336 | bytes 35686400 | tf_op jit(solution)/shard_map/while/body/eval_jaxpr/qhd,khd->hqk/dot_general | solution.py:144
  714.7 31.6 %reduce-scatter.32.cloned.1.call-done = f32[64,512]{1,0:T(8,128)} async-done(((f32[512,512]{1,0:T(8,128)}), f32[64,512]{1,0:T(8,128)}) %reduce-scatter.32.cloned.1.call-update) | async-done | bytes 131088 | tf_op jit(solution)/shard_map/reduce_scatter | solution.py:363
  746.4 39.3 %reduce-scatter.20.cloned.1.call-done = f32[64,512]{1,0:T(8,128)} async-done(((f32[512,512]{1,0:T(8,128)}), f32[64,512]{1,0:T(8,128)}) %reduce-scatter.20.cloned.1.call-update) | async-done | bytes 131088 | tf_op jit(solution)/shard_map/reduce_scatter | solution.py:360
  785.8 39.5 %reduce-scatter.24.cloned.1.call-done = f32[64,512]{1,0:T(8,128)} async-done(((f32[512,512]{1,0:T(8,128)}), f32[64,512]{1,0:T(8,128)}) %reduce-scatter.24.cloned.1.call-update) | async-done | bytes 131088 | tf_op jit(solution)/shard_map/reduce_scatter | solution.py:361
  825.4 39.5 %reduce-scatter.28.cloned.1.call-done = f32[64,512]{1,0:T(8,128)} async-done(((f32[512,512]{1,0:T(8,128)}), f32[64,512]{1,0:T(8,128)}) %reduce-scatter.28.cloned.1.call-update) | async-done | bytes 131088 | tf_op jit(solution)/shard_map/reduce_scatter | solution.py:362
  864.9 55.0 %reduce-scatter.36.cloned.1.call-done = f32[64,2048]{1,0:T(8,128)} async-done(((f32[512,2048]{1,0:T(8,128)}), f32[64,2048]{1,0:T(8,128)}) %reduce-scatter.36.cloned.1.call-update) | async-done | bytes 524304 | tf_op jit(solution)/shard_map/reduce_scatter | solution.py:364
  920.0 54.5 %reduce-scatter.40.cloned.1.call-done = f32[256,512]{1,0:T(8,128)} async-done(((f32[2048,512]{1,0:T(8,128)}), f32[256,512]{1,0:T(8,128)}) %reduce-scatter.40.cloned.1.call-update) | async-done | bytes 524304 | tf_op jit(solution)/shard_map/reduce_scatter | solution.py:365
  977.2 12.9 %all-reduce.5 = f32[2048]{0:T(1024)S(1)} all-reduce(f32[2048]{0:T(1024)S(1)} %reshape.311), channel_id=18, replica_groups=mesh['dp'=4,'fsdp'=8] {'fsdp'}, use_global_device_ids=true, to_apply=%region_43.44.clone | all-reduce | flops 2048 | bytes 16384
  990.3 21.2 %reduce-scatter.46.cloned.1.call-done = f32[64,8]{1,0:T(8,128)} async-done(((f32[512,8]{1,0:T(8,128)}), f32[64,8]{1,0:T(8,128)}) %reduce-scatter.46.cloned.1.call-update) | async-done | bytes 2064
  1012.3 11.9 %all-reduce.7 = (f32[8,64]{1,0:T(8,128)S(1)}, f32[256]{0:T(256)S(1)}) all-reduce(f32[8,64]{1,0:T(8,128)S(1)} %copy.127, f32[256]{0:T(256)S(1)} %dynamic-slice.4), channel_id=15, replica_groups=mesh['dp'=4,'fsdp'=8] {'dp'}, use_global_device_ids=true, to_apply=%region_38.39.clone | all-reduce | flops 768 | bytes 6144
  1036.8 18.7 %reduce-scatter.34.cloned.1.call-done = f32[64,128]{1,0:T(8,128)} async-done(((f32[64,512]{1,0:T(8,128)}), f32[64,128]{1,0:T(8,128)}) %reduce-scatter.34.cloned.1.call-update) | async-done | bytes 32784 | tf_op jit(solution)/shard_map/reduce_scatter | solution.py:374
  1055.6 20.1 %reduce-scatter.22.cloned.1.call-done = f32[64,128]{1,0:T(8,128)} async-done(((f32[64,512]{1,0:T(8,128)}), f32[64,128]{1,0:T(8,128)}) %reduce-scatter.22.cloned.1.call-update) | async-done | bytes 32784 | tf_op jit(solution)/shard_map/reduce_scatter | solution.py:371
  1075.7 20.0 %reduce-scatter.26.cloned.1.call-done = f32[64,128]{1,0:T(8,128)} async-done(((f32[64,512]{1,0:T(8,128)}), f32[64,128]{1,0:T(8,128)}) %reduce-scatter.26.cloned.1.call-update) | async-done | bytes 32784 | tf_op jit(solution)/shard_map/reduce_scatter | solution.py:372
  1095.8 20.1 %reduce-scatter.30.cloned.1.call-done = f32[64,128]{1,0:T(8,128)} async-done(((f32[64,512]{1,0:T(8,128)}), f32[64,128]{1,0:T(8,128)}) %reduce-scatter.30.cloned.1.call-update) | async-done | bytes 32784 | tf_op jit(solution)/shard_map/reduce_scatter | solution.py:373
  1115.9 22.5 %reduce-scatter.38.cloned.1.call-done = f32[64,512]{1,0:T(8,128)} async-done(((f32[64,2048]{1,0:T(8,128)}), f32[64,512]{1,0:T(8,128)}) %reduce-scatter.38.cloned.1.call-update) | async-done | bytes 131088 | tf_op jit(solution)/shard_map/reduce_scatter | solution.py:375
  1138.4 22.7 %reduce-scatter.42.cloned.1.call-done = f32[256,128]{1,0:T(8,128)} async-done(((f32[256,512]{1,0:T(8,128)}), f32[256,128]{1,0:T(8,128)}) %reduce-scatter.42.cloned.1.call-update) | async-done | bytes 131088 | tf_op jit(solution)/shard_map/reduce_scatter | solution.py:376
  (356 shorter events, 486.6 us)
Async XLA Ops:
  7.2 175.8 %all-gather.7.cloned.1.call-start = ((), (), s32[]{:S(2)}) async-start(), calls=%async_computation.15 | async-start | bytes 1179648 | tf_op jit(solution)/shard_map/all_gather | solution.py:85
  24.2 293.8 %all-gather.9.cloned.1.call-start = ((), (), s32[]{:S(2)}) async-start(), calls=%async_computation.16 | async-start | bytes 2359296 | tf_op jit(solution)/shard_map/all_gather | solution.py:82
  39.3 293.4 %all-gather.11.cloned.1.call-start = ((), (), s32[]{:S(2)}) async-start(), calls=%async_computation.17 | async-start | bytes 2359296 | tf_op jit(solution)/shard_map/all_gather | solution.py:83
  53.4 659.3 %reduce-scatter.48.cloned.1.call-start = ((), (), s32[]{:S(2)}) async-start(), calls=%async_computation.32 | async-start | bytes 2359296
  163.0 40.0 %copy-start.22 = (bf16[512,512]{1,0:T(8,128)(2,1)}, bf16[512,512]{1,0:T(8,128)(2,1)S(1)}, u32[]{:S(2)}) copy-start(bf16[512,512]{1,0:T(8,128)(2,1)S(1)} %all_gather.69) | copy-start | bytes 1572868
  172.0 18.4 %copy-start.24 = (bf16[512,512]{1,0:T(8,128)(2,1)}, bf16[512,512]{1,0:T(8,128)(2,1)S(1)}, u32[]{:S(2)}) copy-start(bf16[512,512]{1,0:T(8,128)(2,1)S(1)} %all_gather.75) | copy-start | bytes 1572868
  315.2 68.4 %copy-start.31 = (f32[2048]{0:T(1024)}, f32[2048]{0:T(1024)S(1)}, u32[]{:S(2)}) copy-start(f32[2048]{0:T(1024)S(1)} %broadcast_multiply_fusion.1) | copy-start | bytes 24580
  317.9 65.7 %copy-start.33 = (f32[2048]{0:T(1024)}, f32[2048]{0:T(1024)S(1)}, u32[]{:S(2)}) copy-start(f32[2048]{0:T(1024)S(1)} %fusion.57) | copy-start | bytes 24580
  351.7 23.2 %copy-start.17 = (bf16[2048,512]{1,0:T(8,128)(2,1)}, bf16[2048,512]{1,0:T(8,128)(2,1)S(1)}, u32[]{:S(2)}) copy-start(bf16[2048,512]{1,0:T(8,128)(2,1)S(1)} %get-tuple-element.496) | copy-start | bytes 6291460
  352.2 22.7 %copy-start.2 = (f32[2048,512]{1,0:T(8,128)S(1)}, f32[2048,512]{1,0:T(8,128)}, u32[]{:S(2)}) copy-start(f32[2048,512]{1,0:T(8,128)} %copy-done.1) | copy-start | bytes 12582916
  352.2 22.7 %copy-start.50 = (bf16[512,2048]{1,0:T(8,128)(2,1)S(1)}, bf16[512,2048]{1,0:T(8,128)(2,1)}, u32[]{:S(2)}) copy-start(bf16[512,2048]{1,0:T(8,128)(2,1)} %all-gather.9.cloned.1.call-done) | copy-start | bytes 6291460
  412.6 14.9 %copy-start.5 = (bf16[2,1024,8,64]{1,3,2,0:T(8,128)(2,1)}, bf16[2,1024,8,64]{1,3,2,0:T(8,128)(2,1)S(1)}, u32[]{:S(2)}) copy-start(bf16[2,1024,8,64]{1,3,2,0:T(8,128)(2,1)S(1)} %get-tuple-element.762) | copy-start | bytes 6291460 | tf_op jit(solution)/shard_map/while
  440.3 15.4 %copy-start = (f32[8,512,1024]{2,1,0:T(8,128)S(1)}, f32[8,512,1024]{2,1,0:T(8,128)}, u32[]{:S(2)}) copy-start(f32[8,512,1024]{2,1,0:T(8,128)} %get-tuple-element.667) | copy-start | bytes 50331652 | tf_op jit(solution)/shard_map/while
  497.3 15.4 %copy-start = (f32[8,512,1024]{2,1,0:T(8,128)S(1)}, f32[8,512,1024]{2,1,0:T(8,128)}, u32[]{:S(2)}) copy-start(f32[8,512,1024]{2,1,0:T(8,128)} %get-tuple-element.667) | copy-start | bytes 50331652 | tf_op jit(solution)/shard_map/while
  554.4 15.4 %copy-start = (f32[8,512,1024]{2,1,0:T(8,128)S(1)}, f32[8,512,1024]{2,1,0:T(8,128)}, u32[]{:S(2)}) copy-start(f32[8,512,1024]{2,1,0:T(8,128)} %get-tuple-element.667) | copy-start | bytes 50331652 | tf_op jit(solution)/shard_map/while
  611.5 15.4 %copy-start = (f32[8,512,1024]{2,1,0:T(8,128)S(1)}, f32[8,512,1024]{2,1,0:T(8,128)}, u32[]{:S(2)}) copy-start(f32[8,512,1024]{2,1,0:T(8,128)} %get-tuple-element.667) | copy-start | bytes 50331652 | tf_op jit(solution)/shard_map/while
  668.0 78.4 %reduce-scatter.32.cloned.1.call-start = ((), (), s32[]{:S(2)}) async-start(), calls=%async_computation.24 | async-start | bytes 1179648 | tf_op jit(solution)/shard_map/reduce_scatter | solution.py:363
  672.5 113.3 %reduce-scatter.20.cloned.1.call-start = ((), (), s32[]{:S(2)}) async-start(), calls=%async_computation.18 | async-start | bytes 1179648 | tf_op jit(solution)/shard_map/reduce_scatter | solution.py:360
  677.3 148.0 %reduce-scatter.24.cloned.1.call-start = ((), (), s32[]{:S(2)}) async-start(), calls=%async_computation.20 | async-start | bytes 1179648 | tf_op jit(solution)/shard_map/reduce_scatter | solution.py:361
  682.0 182.8 %reduce-scatter.28.cloned.1.call-start = ((), (), s32[]{:S(2)}) async-start(), calls=%async_computation.22 | async-start | bytes 1179648 | tf_op jit(solution)/shard_map/reduce_scatter | solution.py:362
  686.6 233.3 %reduce-scatter.36.cloned.1.call-start = ((), (), s32[]{:S(2)}) async-start(), calls=%async_computation.26 | async-start | bytes 4718592 | tf_op jit(solution)/shard_map/reduce_scatter | solution.py:364
  698.2 276.3 %reduce-scatter.40.cloned.1.call-start = ((), (), s32[]{:S(2)}) async-start(), calls=%async_computation.28 | async-start | bytes 4718592 | tf_op jit(solution)/shard_map/reduce_scatter | solution.py:365
  709.2 265.3 %copy-start.52 = (u32[32]{0:T(128)S(1)}, u32[32]{0:T(128)}, u32[]{:S(2)}) copy-start(u32[32]{0:T(128)} %constant.227) | copy-start | bytes 388
  709.2 267.8 %copy-start.41 = (f32[2048]{0:T(1024)S(1)}, f32[2048]{0:T(1024)}, u32[]{:S(2)}) copy-start(f32[2048]{0:T(1024)} %get-tuple-element.531) | copy-start | bytes 24580
  709.2 302.2 %reduce-scatter.46.cloned.1.call-start = ((), (), s32[]{:S(2)}) async-start(), calls=%async_computation.31 | async-start | bytes 294912
  712.7 322.6 %reduce-scatter.44.cloned.1.call-start = ((), (), s32[]{:S(2)}) async-start(), calls=%async_computation.30 | async-start | bytes 655360 | tf_op jit(solution)/shard_map/reduce_scatter | solution.py:378
  714.7 340.9 %reduce-scatter.34.cloned.1.call-start = ((), (), s32[]{:S(2)}) async-start(), calls=%async_computation.25 | async-start | bytes 163840 | tf_op jit(solution)/shard_map/reduce_scatter | solution.py:374
  746.4 329.4 %reduce-scatter.22.cloned.1.call-start = ((), (), s32[]{:S(2)}) async-start(), calls=%async_computation.19 | async-start | bytes 163840 | tf_op jit(solution)/shard_map/reduce_scatter | solution.py:371
  785.8 310.0 %reduce-scatter.26.cloned.1.call-start = ((), (), s32[]{:S(2)}) async-start(), calls=%async_computation.21 | async-start | bytes 163840 | tf_op jit(solution)/shard_map/reduce_scatter | solution.py:372
  825.3 290.6 %reduce-scatter.30.cloned.1.call-start = ((), (), s32[]{:S(2)}) async-start(), calls=%async_computation.23 | async-start | bytes 163840 | tf_op jit(solution)/shard_map/reduce_scatter | solution.py:373
  864.9 273.5 %reduce-scatter.38.cloned.1.call-start = ((), (), s32[]{:S(2)}) async-start(), calls=%async_computation.27 | async-start | bytes 655360 | tf_op jit(solution)/shard_map/reduce_scatter | solution.py:375
  920.0 241.2 %reduce-scatter.42.cloned.1.call-start = ((), (), s32[]{:S(2)}) async-start(), calls=%async_computation.29 | async-start | bytes 655360 | tf_op jit(solution)/shard_map/reduce_scatter | solution.py:376
  (54 other events, 208.7 us)
Sparse Core Ops, SparseCore 0:
  24.3 23.6 all-gather.6
  49.9 27.8 all-gather.8
  79.7 27.8 all-gather.10
  668.1 38.7 reduce-scatter.47
  710.2 36.0 reduce-scatter.31
  749.7 36.0 reduce-scatter.19
  789.2 36.0 reduce-scatter.23
  828.8 35.9 reduce-scatter.27
  868.6 51.3 reduce-scatter.35
  923.1 51.3 reduce-scatter.39
  977.8 33.5 reduce-scatter.45
  1013.6 21.6 reduce-scatter.43
  1038.0 17.4 reduce-scatter.33
  1058.4 17.3 reduce-scatter.21
  1078.4 17.3 reduce-scatter.25
  1098.5 17.3 reduce-scatter.29
  1118.6 19.7 reduce-scatter.37
  1141.1 19.9 reduce-scatter.41
where the time goes:
time: 1170 us
  waiting for transfers between devices  415 us (35%)
  matrix products  301 us (26%)
  blocking collectives  195 us (17%)
  local copies, waits for them, and re-layouts  118 us (10%)
  other arithmetic  92.8 us (8%)
  loops' own time  27.7 us (2%)
  between operations  18 us (2%)
    dot_general x8, matrix products, block_pieces(): jnp.einsum('qhd,khd->hqk', query_block, key_block, preferred_element_type...  70 us
    reduce_scatter x1, waiting for transfers between devices, shards(): lax.psum_scatter(inner_local, 'fsdp', scatter_dimension=0, tiled=True)  55 us
    reduce_scatter x1, waiting for transfers between devices, shards(): lax.psum_scatter(outer_local, 'fsdp', scatter_dimension=0, tiled=True)  54.5 us
    convert_element_type x4, other arithmetic, one_step(): score_grad = (probs * (prob_grad - inner)).astype(jnp.bfloat16)  45.9 us
    dot_general x6, matrix products, right_product(): lax.dot_general(left, right, (((1,), (1,)), ((), ())), preferred_element_...  40.8 us
    dot_general x6, matrix products, left_product(): lax.dot_general(left, right, (((0,), (0,)), ((), ())), preferred_element_...  40.4 us
    reduce_scatter x1, waiting for transfers between devices, shards(): lax.psum_scatter(key_local, 'fsdp', scatter_dimension=0, tiled=True)  39.5 us
    reduce_scatter x1, waiting for transfers between devices, shards(): lax.psum_scatter(value_local, 'fsdp', scatter_dimension=0, tiled=True)  39.5 us
  transfers between devices with their start and end apart: 18, of which 14 were waited for; matrix products, arithmetic and copies ran while one was open for 16% of the time, Pallas kernels for 0%

commit v1 on v0

v1 whole, which is shorter than its diff:
```python
import functools

import jax
import jax.numpy as jnp
from jax import lax
from jax.experimental import pallas as pl
from jax.experimental.pallas import tpu as pltpu
from jax.sharding import PartitionSpec as P

H = 8
HD = 64
WIN = 256
PAIR = 2 * HD
VMEM_LIMIT = 60 * 1024 * 1024
F32 = jnp.float32
BF16 = jnp.bfloat16
MESH = pl.DeviceIdType.MESH
SMALL = 16


def nn(left, right):
    return lax.dot_general(left, right, (((1,), (0,)), ((), ())), preferred_element_type=F32)


def nt(left, right):
    return lax.dot_general(left, right, (((1,), (1,)), ((), ())), preferred_element_type=F32)


def tn(left, right):
    return lax.dot_general(left, right, (((0,), (0,)), ((), ())), preferred_element_type=F32)


def column_sum(value):
    return jnp.sum(value.astype(F32), 0, keepdims=True)


def head_rows(pair, which):
    zeros = jnp.zeros((HD, pair.shape[1]), pair.dtype)
    if which == 0:
        return jnp.concatenate([pair[:HD], zeros], 0)
    return jnp.concatenate([zeros, pair[HD:]], 0)


def head_lanes(pair, which):
    lane = lax.broadcasted_iota(jnp.int32, pair.shape, 1)
    keep = (lane < HD) if which == 0 else (lane >= HD)
    return jnp.where(keep, pair, jnp.zeros_like(pair))


def causal(scores):
    key = lax.broadcasted_iota(jnp.int32, scores.shape, 0)
    query = lax.broadcasted_iota(jnp.int32, scores.shape, 1)
    return jnp.where(key <= query, scores, -1e30)


def mesh_place():
    fsdp = lax.axis_index("fsdp")
    return lax.axis_index("dp"), fsdp // 2, lax.rem(fsdp, 2), lax.axis_size("dp"), lax.axis_size("fsdp") // 2


def remote(src, dst, send, recv, device):
    return pltpu.make_async_remote_copy(
        src_ref=src, dst_ref=dst, send_sem=send, recv_sem=recv, device_id=device, device_id_type=MESH
    )


def meet():
    d, chip, core, dp, chips = mesh_place()
    barrier = pltpu.get_barrier_semaphore()
    for n in range(1, dp):
        pl.semaphore_signal(barrier, inc=1, device_id={"dp": lax.rem(d + n, dp)}, device_id_type=MESH)
    for n in range(1, chips):
        other = lax.rem(chip + n, chips) * 2 + core
        pl.semaphore_signal(barrier, inc=1, device_id={"fsdp": other}, device_id_type=MESH)
    pl.semaphore_signal(barrier, inc=1, device_id={"fsdp": chip * 2 + 1 - core}, device_id_type=MESH)
    pl.semaphore_wait(barrier, dp + chips - 1)


class Gather:
    def __init__(self, buf, sems):
        self.buf = buf
        self.zs, self.zr, self.xs, self.xr, self.cs, self.cr = sems
        self.d, self.chip, self.core, self.dp, self.chips = mesh_place()

    @staticmethod
    def semaphores(dp, chips):
        dma = pltpu.SemaphoreType.DMA
        return [dma((dp,)), dma((dp,)), dma((dp, chips)), dma((dp, chips)), dma((chips,)), dma((chips,))]

    def source(self, o):
        return lax.rem(self.d - o + self.dp, self.dp)

    def chip_at(self, p):
        return lax.rem(self.chip + p + self.chips, self.chips)

    def along_dp(self, o):
        block = self.buf.at[self.d, self.chip, self.core]
        to = {"dp": lax.rem(self.d + o, self.dp)}
        return remote(block, block, self.zs.at[o], self.zr.at[o], to)

    def to_chip(self, o, p):
        block = self.buf.at[self.source(o), self.chip, self.core]
        to = {"fsdp": self.chip_at(p) * 2 + self.core}
        return remote(block, block, self.xs.at[o, p], self.xr.at[o, p], to)

    def to_core(self, p):
        block = self.buf.at[:, self.chip_at(-p), self.core]
        return remote(block, block, self.cs.at[p], self.cr.at[p], {"fsdp": self.chip * 2 + 1 - self.core})

    def begin(self):
        for o in range(1, self.dp):
            self.along_dp(o).start()
        for p in range(1, self.chips):
            self.to_chip(0, p).start()

    def spread(self):
        for o in range(1, self.dp):
            self.along_dp(o).wait_recv()
            for p in range(1, self.chips):
                self.to_chip(o, p).start()
        self.to_core(0).start()

    def share(self):
        for p in range(1, self.chips):
            for o in range(self.dp):
                self.to_chip(o, p).wait_recv()
            self.to_core(p).start()

    def arrive(self):
        for p in range(self.chips):
            self.to_core(p).wait_recv()

    def close(self):
        for o in range(1, self.dp):
            self.along_dp(o).wait_send()
        for p in range(1, self.chips):
            for o in range(self.dp):
                self.to_chip(o, p).wait_send()
        for p in range(self.chips):
            self.to_core(p).wait_send()


def forward_attention(
    joined_ref, act_ref, wq_ref, wk_ref, wv_ref, wo_ref, wi_ref, w2_ref, table_ref, place_ref, line_ref,
    q_ref, qt_ref, k_ref, kt_ref, v_ref, ctx_ref, lse_ref, weight_ref, pos_ref, vec_ref, bias_ref, late_ref,
    vt_ref, ctxt_ref, early_ref, own_ref, own_sem, *sems,
):
    row = pl.program_id(0)
    rows = pl.num_programs(0)
    width = act_ref.shape[2]
    blocks = act_ref.shape[1] // WIN
    d, chip, core, dp, chips = mesh_place()
    r, c = wq_ref.shape
    held, narrow = place_ref.shape
    folds = c // narrow
    per = held // folds
    early = Gather(early_ref, sems[:6])
    late = Gather(late_ref, sems[6:])

    def own_copy():
        return pltpu.make_async_copy(own_ref, late_ref.at[d, chip, core], own_sem)

    @pl.when(row == 0)
    def _():
        for n, ref in enumerate((wq_ref, wk_ref, wv_ref)):
            early_ref[d, chip, core, n * r : (n + 1) * r, :] = ref[...]
        place = place_ref[...]
        early_ref[d, chip, core, 3 * r : 3 * r + per, :] = jnp.concatenate(
            [place[n * per : (n + 1) * per] for n in range(folds)], 1
        )
        wide = lambda x: jnp.concatenate([x, jnp.zeros((x.shape[0], c - x.shape[1]), F32)], 1)
        table = wide(table_ref[...].astype(F32))
        line = wide(line_ref[...].astype(F32))
        few = table.shape[0]
        small = jnp.concatenate([table, line, jnp.zeros((SMALL - few - 1, c), F32)], 0)
        early_ref[d, chip, core, 3 * r + per :, :] = small.astype(BF16)
        own_ref[:r, :] = wo_ref[...]
        wide_parts = wi_ref.shape[1] // c
        for n in range(wide_parts):
            own_ref[(1 + n) * r : (2 + n) * r, :] = wi_ref[:, n * c : (n + 1) * c]
        own_ref[(1 + wide_parts) * r :, :] = w2_ref[...]
        own_copy().start()
        meet()
        early.begin()
        early.spread()
        early.share()
        own_copy().wait()
        early.arrive()
        late.begin()
        for a in range(chips):
            for b in range(2):
                f = 2 * a + b
                for n in range(3):
                    weight_ref[f * r : (f + 1) * r, n * width : (n + 1) * width] = jnp.concatenate(
                        [early_ref[e, a, b, n * r : (n + 1) * r, :] for e in range(dp)], 1
                    )
        members = [(a, b) for a in range(chips) for b in range(2)]
        tables = []
        lines = []
        for e in range(dp):
            for n in range(folds):
                at = slice(e * held + n * per, e * held + (n + 1) * per)
                pos_ref[at, :] = jnp.concatenate(
                    [
                        early_ref[e, a, b, 3 * r : 3 * r + per, :][:, n * narrow : (n + 1) * narrow]
                        for a, b in members
                    ],
                    1,
                )
            smalls = [early_ref[e, a, b, 3 * r + per :, :].astype(F32) for a, b in members]
            tables.append(jnp.concatenate([x[:few, :narrow] for x in smalls], 1))
            lines.extend(x[few : few + 1, : line_ref.shape[1]] for x in smalls)
        vec_ref[...] = jnp.concatenate(tables, 0)
        bias_ref[...] = jnp.concatenate(lines, 1)

    def project(step, carry):
        at = pl.ds(pl.multiple_of(step * WIN, WIN), WIN)
        low = (act_ref[0, at, :].astype(F32) + pos_ref[at, :].astype(F32)).astype(BF16)
        every = nn(low, weight_ref[...])
        q = (every[:, :width] + vec_ref[0:1, :]).astype(BF16)
        q = (q.astype(F32) * 0.125).astype(BF16)
        k = every[:, width : 2 * width].astype(BF16)
        v = (every[:, 2 * width :] + vec_ref[1:2, :]).astype(BF16)
        q_ref[0, at, :] = q
        k_ref[0, at, :] = k
        v_ref[0, at, :] = v
        qt_ref[0, :, at] = q.T
        kt_ref[0, :, at] = k.T
        vt_ref[:, at] = v.T
        return carry

    lax.fori_loop(0, blocks, project, 0)

    @pl.when(row == 0)
    def _():
        late.spread()

    @pl.when(row == rows - 1)
    def _():
        late.share()

    def attend(block, pair, joined):
        at = pl.ds(pl.multiple_of(block * WIN, WIN), WIN)
        feats = pl.ds(pl.multiple_of(pair * PAIR, PAIR), PAIR)
        qt = qt_ref[0, feats, at]
        k_own = k_ref[0, at, feats]
        vt_own = vt_ref[feats, at]
        if joined:
            before = pl.ds(pl.multiple_of((block - 1) * WIN, WIN), WIN)
            k_prev = k_ref[0, before, feats]
            vt_prev = vt_ref[feats, before]
            apart = joined_ref[row, block]
        for which in range(2):
            half = slice(which * HD, (which + 1) * HD)
            q_head = head_rows(qt, which)
            own = causal(nn(k_own, q_head))
            peak = jnp.max(own, 0, keepdims=True)
            if joined:
                prev = nn(k_prev, q_head)
                peak = jnp.maximum(peak, jnp.max(prev, 0, keepdims=True) + apart)
            own = jnp.exp(own - peak)
            total = jnp.sum(own, 0, keepdims=True)
            out = nn(vt_own[half], own.astype(BF16))
            if joined:
                prev = jnp.exp(prev - (peak - apart))
                total = total + jnp.sum(prev, 0, keepdims=True)
                out = out + nn(vt_prev[half], prev.astype(BF16))
            ctxt_ref[half, :] = (out * (1.0 / total)).astype(BF16)
            lse_ref[0, pair, which : which + 1, at] = peak + jnp.log(total)
        ctx_ref[0, at, feats] = ctxt_ref[...].T

    def first(pair, carry):
        attend(0, pair, False)
        return carry

    def other(n, carry):
        attend(n // (H // 2) + 1, lax.rem(n, H // 2), True)
        return carry

    lax.fori_loop(0, H // 2, first, 0)
    lax.fori_loop(0, (blocks - 1) * (H // 2), other, 0)

    @pl.when(row == rows - 1)
    def _():
        late.arrive()
        early.close()
        late.close()


def backward_attention(
    joined_ref, q_ref, qt_ref, k_ref, kt_ref, v_ref, lse_ref, grad_ref, first_ref, act_ref, pos_ref, weight_ref,
    input_ref, wgrad_ref, posgrad_ref, sums_ref,
    gradt_ref, dq_ref, dk_ref, dv_ref, wacc_ref,
):
    row = pl.program_id(0)
    rows = pl.num_programs(0)
    width = act_ref.shape[2]
    blocks = act_ref.shape[1] // WIN

    def turn(step, carry):
        at = pl.ds(pl.multiple_of(step * WIN, WIN), WIN)
        gradt_ref[:, at] = grad_ref[0, at, :].T
        return carry

    lax.fori_loop(0, blocks, turn, 0)

    def attend(block, pair, joined):
        at = pl.ds(pl.multiple_of(block * WIN, WIN), WIN)
        feats = pl.ds(pl.multiple_of(pair * PAIR, PAIR), PAIR)
        before = pl.ds(pl.multiple_of(jnp.maximum(block - 1, 0) * WIN, WIN), WIN)
        qt = qt_ref[0, feats, at]
        gt = gradt_ref[feats, at]
        q = q_ref[0, at, feats]
        g = grad_ref[0, at, feats]
        places = [at, before] if joined else [at]
        probs = [[], []]
        score_grads = [[], []]
        dq_halves = []
        for which in range(2):
            half = slice(which * HD, (which + 1) * HD)
            q_head = head_rows(qt, which)
            g_head = head_rows(gt, which)
            lse = lse_ref[0, pair, which : which + 1, at]
            part = []
            inner = None
            for n, place in enumerate(places):
                s = nn(k_ref[0, place, feats], q_head)
                if n == 0:
                    s = causal(s)
                p = jnp.exp(s - lse)
                dp = nn(v_ref[0, place, feats], g_head)
                part.append((p, dp))
                term = jnp.sum(p * dp, 0, keepdims=True)
                inner = term if inner is None else inner + term
            dq = None
            for n, place in enumerate(places):
                p, dp = part[n]
                ds = (p * (dp - inner)).astype(BF16)
                probs[n if len(places) > n else 0].append(p.astype(BF16))
                score_grads[n].append(ds)
                term = nn(kt_ref[0, feats, place][half], ds)
                dq = term if dq is None else dq + term
            dq_halves.append((dq * 0.125).astype(BF16))
        dq_ref[at, feats] = jnp.concatenate(dq_halves, 0).T
        g_both = jnp.concatenate([head_lanes(g, 0), head_lanes(g, 1)], 0)
        q_both = jnp.concatenate([head_lanes(q, 0), head_lanes(q, 1)], 0)
        for n, place in enumerate(places):
            dv = nn(jnp.concatenate(probs[n], 1), g_both)
            dk = nn(jnp.concatenate(score_grads[n], 1), q_both)
            if n == 0:
                dv_ref[place, feats] = dv
                dk_ref[place, feats] = dk
            else:
                dv_ref[place, feats] += dv
                dk_ref[place, feats] += dk

    def one_block(block, carry):
        together = joined_ref[row, block] == 1

        @pl.when(together)
        def _():
            lax.fori_loop(0, H // 2, lambda p, c: (attend(block, p, True), c)[1], 0)

        @pl.when(jnp.logical_not(together))
        def _():
            lax.fori_loop(0, H // 2, lambda p, c: (attend(block, p, False), c)[1], 0)

        return carry

    lax.fori_loop(0, blocks, one_block, 0)

    @pl.when(row == 0)
    def _():
        wacc_ref[...] = jnp.zeros_like(wacc_ref)
        sums_ref[...] = jnp.zeros_like(sums_ref)
        posgrad_ref[...] = jnp.zeros_like(posgrad_ref)

    tile = 2 * WIN

    def finish(step, carry):
        at = pl.ds(pl.multiple_of(step * tile, tile), tile)
        dq = dq_ref[at, :]
        dk = dk_ref[at, :].astype(BF16)
        dv = dv_ref[at, :].astype(BF16)
        every = jnp.concatenate([dq, dk, dv], 1)
        start_grad = first_ref[0, at, :] + nt(every, weight_ref[...])
        input_ref[0, at, :] = start_grad.astype(BF16)
        posgrad_ref[at, :] += start_grad
        low = (act_ref[0, at, :].astype(F32) + pos_ref[at, :].astype(F32)).astype(BF16)
        wacc_ref[...] += nn(low.T, every)
        sums_ref[0:1, :] += column_sum(dq)
        sums_ref[1:2, :] += column_sum(dv)
        return carry

    lax.fori_loop(0, act_ref.shape[1] // tile, finish, 0)

    @pl.when(row == rows - 1)
    def _():
        wgrad_ref[...] = wacc_ref[...].astype(wgrad_ref.dtype)


def feed_forward(
    ctx_ref, act_ref, pos_ref, cot_ref, late_ref, vec_ref, bias_ref,
    out_ref, first_ref, grad_ref, wog_ref, wig_ref, w2g_ref, sums_ref, bsum_ref,
    wo_acc, wi_acc, w2_acc, slope_ref, wo_ref, wi_ref, w2_ref,
):
    step = pl.program_id(0)
    width = ctx_ref.shape[1]
    dp, chips, _, _, c = late_ref.shape
    r = width // (2 * chips)
    hidden = bias_ref.shape[1]
    part = 512

    @pl.when(step == 0)
    def _():
        wo_acc[...] = jnp.zeros_like(wo_acc)
        wi_acc[...] = jnp.zeros_like(wi_acc)
        w2_acc[...] = jnp.zeros_like(w2_acc)
        sums_ref[...] = jnp.zeros_like(sums_ref)
        bsum_ref[...] = jnp.zeros_like(bsum_ref)
        parts = hidden // dp // c
        tall = hidden // (2 * chips)

        def unpack(chip, carry):
            for core in range(2):
                f = 2 * chip + core
                at = pl.ds(pl.multiple_of(f * r, r), r)
                block = lambda e, lo, n: late_ref[e, chip, core, lo : lo + n, :]
                wo_ref[at, :] = jnp.concatenate([block(e, 0, r) for e in range(dp)], 1)
                wi_ref[at, :] = jnp.concatenate(
                    [block(e, (1 + n) * r, r) for e in range(dp) for n in range(parts)], 1
                )
                w2_ref[pl.ds(pl.multiple_of(f * tall, tall), tall), :] = jnp.concatenate(
                    [block(e, (1 + parts) * r, tall) for e in range(dp)], 1
                )
            return carry

        lax.fori_loop(0, chips, unpack, 0)

    vec = lambda n: vec_ref[n : n + 1, :]
    ctx = ctx_ref[...]
    first_sum = act_ref[...].astype(F32) + pos_ref[...].astype(F32) + (nn(ctx, wo_ref[...]) + vec(2))
    center = first_sum - jnp.mean(first_sum, -1, keepdims=True)
    scale_one = lax.rsqrt(jnp.mean(center * center, -1, keepdims=True) + 1e-05)
    z_one = center * scale_one
    normed = z_one * vec(3) + vec(4)
    normed_low = normed.astype(BF16)
    branch = None
    acts = []
    for n in range(hidden // part):
        cols = slice(n * part, (n + 1) * part)
        pre = nn(normed_low, wi_ref[:, cols]) + bias_ref[:, cols]
        square = pre * pre
        t = jnp.tanh(pre * (0.7978845608028654 + (0.7978845608028654 * 0.044715) * square))
        half = 0.5 + 0.5 * t
        act = (pre * half).astype(BF16)
        slope_ref[:, cols] = half + (0.5 * pre) * (1.0 - t * t) * (
            0.7978845608028654 + (3.0 * 0.7978845608028654 * 0.044715) * square
        )
        acts.append(act)
        term = nn(act, w2_ref[cols, :])
        branch = term if branch is None else branch + term
    second_sum = normed + (branch + vec(5))
    center = second_sum - jnp.mean(second_sum, -1, keepdims=True)
    scale_two = lax.rsqrt(jnp.mean(center * center, -1, keepdims=True) + 1e-05)
    z_two = center * scale_two
    out_ref[...] = (z_two * vec(6) + vec(7)).astype(BF16)
    cot = cot_ref[...].astype(F32)
    sums_ref[6:7, :] += column_sum(cot * z_two)
    sums_ref[7:8, :] += column_sum(cot)
    e = cot * vec(6)
    second_grad = scale_two * (
        e - jnp.mean(e, -1, keepdims=True) - z_two * jnp.mean(e * z_two, -1, keepdims=True)
    )
    branch_grad = second_grad.astype(BF16)
    sums_ref[5:6, :] += column_sum(branch_grad)
    branch_t = branch_grad.T
    normed_t = normed_low.T
    normed_grad = second_grad
    for n in range(hidden // part):
        cols = slice(n * part, (n + 1) * part)
        pre_grad = nt(branch_grad, w2_ref[cols, :]) * slope_ref[:, cols]
        pre_low = pre_grad.astype(BF16)
        w2_acc[:, cols] += nn(branch_t, acts[n])
        wi_acc[:, cols] += nn(normed_t, pre_low)
        bsum_ref[:, cols] += column_sum(pre_low)
        normed_grad = normed_grad + nt(pre_low, wi_ref[:, cols])
    sums_ref[3:4, :] += column_sum(normed_grad * z_one)
    sums_ref[4:5, :] += column_sum(normed_grad)
    e = normed_grad * vec(3)
    first_grad = scale_one * (
        e - jnp.mean(e, -1, keepdims=True) - z_one * jnp.mean(e * z_one, -1, keepdims=True)
    )
    first_ref[...] = first_grad
    attn_grad = first_grad.astype(BF16)
    sums_ref[2:3, :] += column_sum(attn_grad)
    wo_acc[...] += nn(ctx.T, attn_grad)
    grad_ref[...] = nt(attn_grad, wo_ref[...]).astype(BF16)

    @pl.when(step == pl.num_programs(0) - 1)
    def _():
        wog_ref[...] = wo_acc[...].astype(wog_ref.dtype)
        wig_ref[...] = wi_acc[...].astype(wig_ref.dtype)
        w2g_ref[...] = w2_acc[...].astype(w2g_ref.dtype)


def whole(shape):
    return pl.BlockSpec(shape, lambda *_: (0,) * len(shape))


def run_forward(apart, act, wq, wk, wv, wo, wi, w2, table, place, line):
    rows, seq, width = act.shape
    dp, fsdp = lax.axis_size("dp"), lax.axis_size("fsdp")
    chips = fsdp // 2
    r, c = wq.shape
    hidden = wi.shape[1] * dp
    first_rows = 3 * r + place.shape[0] * place.shape[1] // c + SMALL
    late_rows = r + r * wi.shape[1] // c + w2.shape[0]
    row3 = lambda shape: pl.BlockSpec((1,) + shape, lambda i: (i,) + (0,) * len(shape))
    seqs = row3((seq, width))
    turned = row3((width, seq))
    st, tt = jax.ShapeDtypeStruct((rows, seq, width), BF16), jax.ShapeDtypeStruct((rows, width, seq), BF16)
    late = (dp, chips, 2, late_rows, c)
    small = [x.shape for x in (wq, wk, wv, wo, wi, w2, table, place, line)]
    return pl.pallas_call(
        forward_attention,
        grid=(rows,),
        in_specs=[pl.BlockSpec(memory_space=pltpu.SMEM), seqs] + [whole(x) for x in small],
        out_specs=[seqs, turned, seqs, turned, seqs, seqs, row3((H // 2, 2, seq)), whole((width, 3 * width)),
                   whole((seq, width)), whole((table.shape[0] * dp, width)), whole((1, hidden)),
                   pl.BlockSpec(memory_space=pl.ANY)],
        scratch_shapes=[
            pltpu.VMEM((width, seq), BF16),
            pltpu.VMEM((PAIR, WIN), BF16),
            pltpu.VMEM((dp, chips, 2, first_rows, c), BF16),
            pltpu.VMEM((late_rows, c), BF16),
            pltpu.SemaphoreType.DMA,
        ] + Gather.semaphores(dp, chips) * 2,
        out_shape=[
            st, tt, st, tt, st, st, jax.ShapeDtypeStruct((rows, H // 2, 2, seq), F32),
            jax.ShapeDtypeStruct((width, 3 * width), BF16),
            jax.ShapeDtypeStruct((seq, width), BF16),
            jax.ShapeDtypeStruct((table.shape[0] * dp, width), F32),
            jax.ShapeDtypeStruct((1, hidden), F32),
            jax.ShapeDtypeStruct(late, BF16),
        ],
        compiler_params=pltpu.CompilerParams(
            vmem_limit_bytes=VMEM_LIMIT, collective_id=0, has_side_effects=True
        ),
        name="forward_attention",
    )(apart, act, wq, wk, wv, wo, wi, w2, table, place, line)


def run_backward(joined, q, qt, k, kt, v, lse, grad, first, act, pos, weight):
    rows, seq, width = act.shape
    row3 = lambda shape: pl.BlockSpec((1,) + shape, lambda r, *_: (r,) + (0,) * len(shape))
    seqs = row3((seq, width))
    turned = row3((width, seq))
    return pl.pallas_call(
        backward_attention,
        grid_spec=pltpu.PrefetchScalarGridSpec(
            num_scalar_prefetch=1,
            grid=(rows,),
            in_specs=[seqs, turned, seqs, turned, seqs, row3((H // 2, 2, seq)), seqs, seqs, seqs,
                      whole((seq, width)), whole((width, 3 * width))],
            out_specs=[seqs, whole((width, 3 * width)), whole((seq, width)), whole((8, width))],
            scratch_shapes=[
                pltpu.VMEM((width, seq), BF16),
                pltpu.VMEM((seq, width), BF16),
                pltpu.VMEM((seq, width), F32),
                pltpu.VMEM((seq, width), F32),
                pltpu.VMEM((width, 3 * width), F32),
            ],
        ),
        out_shape=[
            jax.ShapeDtypeStruct((rows, seq, width), BF16),
            jax.ShapeDtypeStruct((width, 3 * width), BF16),
            jax.ShapeDtypeStruct((seq, width), F32),
            jax.ShapeDtypeStruct((8, width), F32),
        ],
        compiler_params=pltpu.CompilerParams(vmem_limit_bytes=VMEM_LIMIT),
        name="backward_attention",
    )(joined, q, qt, k, kt, v, lse, grad, first, act, pos, weight)


def run_feed_forward(ctx, act, pos, cot, late, vec, bias, tile=256):
    tokens, width = ctx.shape
    seq = pos.shape[0]
    hidden = bias.shape[1]
    per_row = seq // tile
    tok = pl.BlockSpec((tile, width), lambda t: (t, 0))
    once = lambda shape: pl.BlockSpec(shape, lambda *_: (0,) * len(shape), pipeline_mode=pl.Buffered(1))
    return pl.pallas_call(
        feed_forward,
        grid=(tokens // tile,),
        in_specs=[tok, tok, pl.BlockSpec((tile, width), lambda t: (t % per_row, 0)), tok,
                  once(late.shape), whole(vec.shape), whole(bias.shape)],
        out_specs=[tok, tok, tok, whole((width, width)), whole((width, hidden)), whole((width, hidden)),
                   whole((8, width)), whole((1, hidden))],
        scratch_shapes=[
            pltpu.VMEM((width, width), F32),
            pltpu.VMEM((width, hidden), F32),
            pltpu.VMEM((width, hidden), F32),
            pltpu.VMEM((tile, hidden), F32),
            pltpu.VMEM((width, width), BF16),
            pltpu.VMEM((width, hidden), BF16),
            pltpu.VMEM((hidden, width), BF16),
        ],
        out_shape=[
            jax.ShapeDtypeStruct((tokens, width), BF16),
            jax.ShapeDtypeStruct((tokens, width), F32),
            jax.ShapeDtypeStruct((tokens, width), BF16),
            jax.ShapeDtypeStruct((width, width), BF16),
            jax.ShapeDtypeStruct((width, hidden), BF16),
            jax.ShapeDtypeStruct((width, hidden), BF16),
            jax.ShapeDtypeStruct((8, width), F32),
            jax.ShapeDtypeStruct((1, hidden), F32),
        ],
        compiler_params=pltpu.CompilerParams(vmem_limit_bytes=VMEM_LIMIT),
        name="feed_forward",
    )(ctx, act, pos, cot, late, vec, bias)


def joined_blocks(window_lengths, seq):
    bounds = jnp.cumsum(window_lengths, -1)
    starts = jnp.arange(seq // WIN, dtype=jnp.int32) * WIN
    cut = jnp.any(bounds[:, None, :] == starts[None, :, None], -1)
    return jnp.where(cut | (starts == 0)[None], 0, 1).astype(jnp.int32)


def shards(
    activations, window_lengths, query_weight, key_weight, value_weight, output_weight, inner_weight, outer_weight,
    vectors, positions, inner_bias, output_cotangent,
):
    rows, seq, width = activations.shape
    dp, fsdp = lax.axis_size("dp"), lax.axis_size("fsdp")
    both = ("dp", "fsdp")

    joined = joined_blocks(window_lengths, seq)
    apart = jnp.where(joined == 1, 0.0, -1e30).astype(F32)
    q, qt, k, kt, v, ctx, lse, weight, pos, vec, bias, late = run_forward(
        apart, activations, query_weight, key_weight, value_weight, output_weight, inner_weight, outer_weight,
        vectors, positions, inner_bias.reshape(1, -1),
    )
    c = query_weight.shape[1]
    flat = lambda x: x.reshape(rows * seq, width)
    out, first, grad, wog, wig, w2g, sums, bsum = run_feed_forward(
        flat(ctx), flat(activations), pos, flat(output_cotangent), late, vec, bias
    )
    deep = lambda x: x.reshape(rows, seq, width)
    input_grad, wgrad, posgrad, more = run_backward(
        joined, q, qt, k, kt, v, lse, deep(grad), deep(first), activations, pos, weight
    )
    sums = jnp.concatenate([more[0:2], sums[2:]], 0)

    def scatter(x):
        return lax.psum_scatter(x, both, scatter_dimension=0, tiled=True)[0].astype(F32)

    def split_columns(x, r, c):
        return x.reshape(fsdp, r, dp, c).transpose(2, 0, 1, 3).reshape(dp * fsdp, r, c)

    r = query_weight.shape[0]
    own = [scatter(split_columns(g, r, c)) for g in (wgrad[:, :width], wgrad[:, width:2 * width], wgrad[:, 2 * width:], wog)]
    own.append(scatter(split_columns(wig, *inner_weight.shape)))
    own.append(scatter(split_columns(w2g.T, *outer_weight.shape)))
    split_rows = lambda x, s: x.reshape(dp, s[0], fsdp, s[1]).transpose(0, 2, 1, 3).reshape((dp * fsdp,) + s)
    own.append(scatter(split_rows(sums, vectors.shape)))
    own.append(scatter(split_rows(posgrad, positions.shape)))
    own.append(scatter(bsum.reshape(dp * fsdp, -1)))
    return (deep(out), input_grad) + tuple(own)


def solution(mesh):
    tokens = P(("dp", "fsdp"), None, None)
    matrix = P("fsdp", "dp")
    table = P("dp", "fsdp")
    line = P(("dp", "fsdp"))
    return jax.shard_map(
        shards,
        mesh=mesh,
        in_specs=(tokens, P(("dp", "fsdp"), None)) + (matrix,) * 6 + (table, table, line, tokens),
        out_specs=(tokens, tokens) + (matrix,) * 6 + (table, table, line),
        check_vma=False,
    )
```

time: 1170 us -> 1130 us (0.966)
  waiting for transfers between devices: 415 us -> 861 us
  matrix products: 301 us -> 0 us
  Pallas kernels: 0 us -> 171 us
  blocking collectives: 195 us -> 40.9 us
  local copies, waits for them, and re-layouts: 118 us -> 27.3 us
  other arithmetic: 92.8 us -> 11.2 us
  loops' own time: 27.7 us -> 0 us
    reduce_scatter x13 -> x7, waiting for transfers between devices: 394 us -> 861 us  [scatter(): lax.psum_scatter(x, both, scatter_dimension=0, tiled=True)[0].astype(F32)]
    dot_general x46 -> x0, matrix products: 301 us -> none  [the longest x8 70 us: block_pieces(): jnp.einsum('qhd,khd->hqk', query_block, key_block, preferred_element_type...]
    pallas_call x0 -> x3, Pallas kernels: none -> 171 us  [the longest x1 69.6 us: run_forward(): pl.pallas_call(forward_attention, grid=(rows,), in_specs=[pl.BlockSpec(me...]
    all_gather x14 -> x0, blocking collectives: 161 us -> none  [the longest x1 16.9 us: fetch_params(): lax.all_gather(positions, 'dp', axis=0, tiled=True)]
    convert_element_type x7 -> x6, other arithmetic: 49.8 us -> 8.34 us  [scatter(): lax.psum_scatter(x, both, scatter_dimension=0, tiled=True)[0].astype(F32)]
    reduce_sum x16 -> x0, other arithmetic: 37.3 us -> none  [the longest x4 17.5 us: one_block(): total = jnp.sum(expo, -1, keepdims=True)]
    while x42 -> x0, local copies, waits for them, and re-layouts: 30.7 us -> none
    unnamed x115 -> x8, local copies, waits for them, and re-layouts: 34.5 us -> 3.77 us
  transfers between devices with their start and end apart: 18 -> 7, of which waited for: 14 -> 7; matrix products, arithmetic and copies ran while one was open for 16% -> 3% of each run, Pallas kernels for 0% -> 0%
where the time goes in v1:
time: 1130 us
  waiting for transfers between devices  861 us (76%)
  Pallas kernels  171 us (15%)
  blocking collectives  40.9 us (4%)
  local copies, waits for them, and re-layouts  27.3 us (2%)
  between operations  14.3 us (1%)
    reduce_scatter x7, waiting for transfers between devices, scatter(): lax.psum_scatter(x, both, scatter_dimension=0, tiled=True)[0].astype(F32)  861 us
    pallas_call x1, Pallas kernels, run_forward(): pl.pallas_call(forward_attention, grid=(rows,), in_specs=[pl.BlockSpec(me...  69.6 us
    pallas_call x1, Pallas kernels, run_feed_forward(): pl.pallas_call(feed_forward, grid=(tokens // tile,), in_specs=[tok, tok,...  51.8 us
    pallas_call x1, Pallas kernels, run_backward(): pl.pallas_call(backward_attention, grid_spec=pltpu.PrefetchScalarGridSpec...  49.5 us
    unnamed x1, blocking collectives  40.9 us
  transfers between devices with their start and end apart: 7, of which 7 were waited for; matrix products, arithmetic and copies ran while one was open for 3% of the time, Pallas kernels for 0%

profile of v1, /device:TPU:0, one launch (start us, length us, event | category | flops | bytes accessed | tf_op | source)
XLA Modules:
  0.0 1125.6 jit_solution(12765482154353796424)
XLA Ops:
  7.2 0.9 reduce_window_sum.11
  9.4 1.5 copy.61.place_ref
  10.9 69.6 %forward_attention.1 = (bf16[2,1024,512]{2,1,0:T(8,128)(2,1)}, bf16[2,512,1024]{2,1,0:T(8,128)(2,1)}, bf16[2,1024,512]{2,1,0:T(8,128)(2,1)}, bf16[2,512,1024]{2,...) custom-call(f32[2,4]{1,0:T(2,128)} %compare_select_fusion.joined_ref, ...), custom_call_target="tpu_custom_call" | custom-call | tf_op jit(solution)/shard_map/forward_attention/pallas_call | solution.py:525
  80.5 51.8 %feed_forward.1 = (bf16[2048,512]{1,0:T(8,128)(2,1)}, f32[2048,512]{1,0:T(8,128)}, bf16[2048,512]{1,0:T(8,128)(2,1)}, bf16[512,512]{1,0:T(8,128)(2,1)}, bf16[512...) custom-call(bf16[2048,512]{1,0:T(8,128)(2,1)} %bitcast.64, ...), custom_call_target="tpu_custom_call" | custom-call | tf_op jit(solution)/shard_map/feed_forward/pallas_call | solution.py:593
  132.3 49.5 %backward_attention.1 = (bf16[2,1024,512]{2,1,0:T(8,128)(2,1)}, bf16[512,1536]{1,0:T(8,128)(2,1)}, f32[1024,512]{1,0:T(8,128)}, f32[8,512]{1,0:T(8,128)}) custom-call(s32[2,4]{1,0:T(2,128)} %or_select_fusion.joined_ref, bf16[2,1024,512]{2,1,0:T(8,128)(2,1)} %get-tuple-element.41.q_ref, bf16[2,512,1024]{2,1,0:T(8,128)(2,1)} %get-tuple-element.42.qt_ref, ...), custom_call_target="tpu_custom_call" | custom-call | tf_op jit(solution)/shard_map/backward_attention/pallas_call | solution.py:559
  181.8 1.5 fusion.1
  183.4 0.9 copy.64
  184.5 1.0 copy.63
  185.7 1.0 copy.62
  186.9 0.9 copy.65
  187.9 2.3 copy.71
  190.1 3.0 copy.67
  193.2 3.3 reshape.133
  196.5 1.8 copy.66
  198.4 1.9 copy.69
  200.3 2.0 reshape.139
  202.3 3.3 copy.70
  205.7 0.7 slice.18
  207.8 40.9 %all-reduce.2 = (f32[32,2,64]{2,1,0:T(2,128)S(1)}, f32[32,64]{1,0:T(8,128)S(1)}) all-reduce(f32[32,2,64]{2,1,0:T(2,128)S(1)} %bitcast.75, f32[32,64]{1,0:T(8,128)S(1)} %reshape.141), channel_id=8, replica_groups=mesh['dp'=4,'fsdp'=8] {'dp','fsdp'}, use_global_device_ids=true, to_apply=%region_8.9.clone | all-reduce | flops 6144 | bytes 49152
  249.8 68.5 %reduce-scatter.12.cloned.1.call-done = bf16[1,64,128]{2,1,0:T(8,128)(2,1)} async-done(((bf16[32,64,128]{2,1,0:T(8,128)(2,1)}), bf16[1,64,128]{2,1,0:T(8,128)(2,1)}) %reduce-scatter.12.cloned.1.call-update) | async-done | bytes 16400 | tf_op jit(solution)/shard_map/reduce_scatter | solution.py:657
  318.3 1.3 bitcast_convert_fusion.3
  319.6 130.7 %reduce-scatter.10.cloned.1.call-done = bf16[1,64,128]{2,1,0:T(8,128)(2,1)} async-done(((bf16[32,64,128]{2,1,0:T(8,128)(2,1)}), bf16[1,64,128]{2,1,0:T(8,128)(2,1)}) %reduce-scatter.10.cloned.1.call-update) | async-done | bytes 16400 | tf_op jit(solution)/shard_map/reduce_scatter | solution.py:657
  450.3 1.3 bitcast_convert_fusion.4
  451.7 130.5 %reduce-scatter.8.cloned.1.call-done = bf16[1,64,128]{2,1,0:T(8,128)(2,1)} async-done(((bf16[32,64,128]{2,1,0:T(8,128)(2,1)}), bf16[1,64,128]{2,1,0:T(8,128)(2,1)}) %reduce-scatter.8.cloned.1.call-update) | async-done | bytes 16400 | tf_op jit(solution)/shard_map/reduce_scatter | solution.py:657
  582.1 1.3 bitcast_convert_fusion.5
  583.5 130.4 %reduce-scatter.14.cloned.1.call-done = bf16[1,64,128]{2,1,0:T(8,128)(2,1)} async-done(((bf16[32,64,128]{2,1,0:T(8,128)(2,1)}), bf16[1,64,128]{2,1,0:T(8,128)(2,1)}) %reduce-scatter.14.cloned.1.call-update) | async-done | bytes 16400 | tf_op jit(solution)/shard_map/reduce_scatter | solution.py:657
  713.9 1.3 bitcast_convert_fusion.2
  715.2 133.4 %reduce-scatter.18.cloned.1.call-done = bf16[1,256,128]{2,1,0:T(8,128)(2,1)} async-done(((bf16[32,256,128]{2,1,0:T(8,128)(2,1)}), bf16[1,256,128]{2,1,0:T(8,128)(2,1)}) %reduce-scatter.18.cloned.1.call-update) | async-done | bytes 65552 | tf_op jit(solution)/shard_map/reduce_scatter | solution.py:657
  848.6 1.5 bitcast_convert_fusion
  850.2 133.3 %reduce-scatter.16.cloned.1.call-done = bf16[1,64,512]{2,1,0:T(8,128)(2,1)} async-done(((bf16[32,64,512]{2,1,0:T(8,128)(2,1)}), bf16[1,64,512]{2,1,0:T(8,128)(2,1)}) %reduce-scatter.16.cloned.1.call-update) | async-done | bytes 65552 | tf_op jit(solution)/shard_map/reduce_scatter | solution.py:657
  983.4 1.5 bitcast_convert_fusion.1
  984.9 133.8 %reduce-scatter.20.cloned.1.call-done = f32[1,256,64]{1,2,0:T(8,128)} async-done(((f32[32,256,64]{1,2,0:T(8,128)}), f32[1,256,64]{1,2,0:T(8,128)}) %reduce-scatter.20.cloned.1.call-update) | async-done | bytes 65552 | tf_op jit(solution)/shard_map/reduce_scatter | solution.py:657
  (38 shorter events, 4.7 us)
Async XLA Ops:
  7.2 311.1 %reduce-scatter.12.cloned.1.call-start = ((), (), s32[]{:S(2)}) async-start(), calls=%async_computation.9 | async-start | bytes 540672 | tf_op jit(solution)/shard_map/reduce_scatter | solution.py:657
  184.3 266.0 %reduce-scatter.10.cloned.1.call-start = ((), (), s32[]{:S(2)}) async-start(), calls=%async_computation.8 | async-start | bytes 540672 | tf_op jit(solution)/shard_map/reduce_scatter | solution.py:657
  184.5 2.2 copy-start
  185.5 396.6 %reduce-scatter.8.cloned.1.call-start = ((), (), s32[]{:S(2)}) async-start(), calls=%async_computation.7 | async-start | bytes 540672 | tf_op jit(solution)/shard_map/reduce_scatter | solution.py:657
  186.7 527.2 %reduce-scatter.14.cloned.1.call-start = ((), (), s32[]{:S(2)}) async-start(), calls=%async_computation.10 | async-start | bytes 540672 | tf_op jit(solution)/shard_map/reduce_scatter | solution.py:657
  187.8 660.8 %reduce-scatter.18.cloned.1.call-start = ((), (), s32[]{:S(2)}) async-start(), calls=%async_computation.12 | async-start | bytes 2162688 | tf_op jit(solution)/shard_map/reduce_scatter | solution.py:657
  193.1 790.3 %reduce-scatter.16.cloned.1.call-start = ((), (), s32[]{:S(2)}) async-start(), calls=%async_computation.11 | async-start | bytes 2162688 | tf_op jit(solution)/shard_map/reduce_scatter | solution.py:657
  198.3 920.4 %reduce-scatter.20.cloned.1.call-start = ((), (), s32[]{:S(2)}) async-start(), calls=%async_computation.13 | async-start | bytes 2162688 | tf_op jit(solution)/shard_map/reduce_scatter | solution.py:657
  205.7 0.8 copy-start.1
  205.7 1.4 copy-start.2
Sparse Core Ops, SparseCore 0:
  184.4 133.8 reduce-scatter.11
  320.6 129.6 reduce-scatter.9
  452.6 129.5 reduce-scatter.7
  584.3 129.5 reduce-scatter.13
  716.0 132.5 reduce-scatter.17
  850.9 132.5 reduce-scatter.15
  986.2 132.4 reduce-scatter.19

commit v2 on v1

--- a/solution.py
+++ b/solution.py
@@ -11,7 +11,7 @@
 HD = 64
 WIN = 256
 PAIR = 2 * HD
-VMEM_LIMIT = 60 * 1024 * 1024
+VMEM_LIMIT = 62 * 1024 * 1024
 F32 = jnp.float32
 BF16 = jnp.bfloat16
 MESH = pl.DeviceIdType.MESH
@@ -138,6 +138,100 @@
                 self.to_chip(o, p).wait_send()
         for p in range(self.chips):
             self.to_core(p).wait_send()
+
+
+class Reduce:
+    def __init__(self, part, scratch):
+        (self.part, (self.pair, self.plane, self.mine, self.line,
+                     self.cs, self.cr, self.xs, self.xr, self.zs, self.zr)) = part, scratch
+        self.d, self.chip, self.core, self.dp, self.chips = mesh_place()
+
+    @staticmethod
+    def scratch(dp, chips, rows, c):
+        dma = pltpu.SemaphoreType.DMA
+        return [
+            pltpu.VMEM((dp, chips, rows, c), BF16),
+            pltpu.VMEM((chips - 1, dp, rows, c), BF16),
+            pltpu.VMEM((dp, rows, c), BF16),
+            pltpu.VMEM((dp, rows, c), BF16),
+            dma((chips,)), dma((chips,)), dma((chips,)), dma((chips,)), dma((dp,)), dma((dp,)),
+        ]
+
+    COUNT = 10
+
+    def chip_at(self, p):
+        return lax.rem(self.chip + p + self.chips, self.chips)
+
+    def to_core(self, p):
+        at = self.chip_at(p)
+        return remote(
+            self.part.at[:, at, 1 - self.core], self.pair.at[:, at], self.cs.at[p], self.cr.at[p],
+            {"fsdp": self.chip * 2 + 1 - self.core},
+        )
+
+    def to_chip(self, p):
+        at = self.chip_at(p)
+        return remote(
+            self.pair.at[:, at], self.plane.at[p - 1], self.xs.at[p], self.xr.at[p], {"fsdp": at * 2 + self.core}
+        )
+
+    def along_dp(self, o):
+        to = lax.rem(self.d + o, self.dp)
+        return remote(self.mine.at[to], self.line.at[o], self.zs.at[o], self.zr.at[o], {"dp": to})
+
+    def order(self):
+        return list(range(1, self.chips)) + [0]
+
+    def begin(self):
+        for p in self.order():
+            self.to_core(p).start()
+
+    def across(self):
+        for p in self.order():
+            at = self.chip_at(p)
+            self.to_core(p).wait_recv()
+
+            def add(e, carry):
+                both = self.part[e, at, self.core].astype(F32) + self.pair[e, at].astype(F32)
+                self.pair[e, at] = both.astype(BF16)
+                return carry
+
+            lax.fori_loop(0, self.dp, add, 0)
+            if p:
+                self.to_chip(p).start()
+
+    def along(self):
+        for p in range(1, self.chips):
+            self.to_chip(p).wait_recv()
+
+        def add(n, carry):
+            e = lax.rem(self.d + 1 + n, self.dp)
+            total = self.pair[e, self.chip].astype(F32)
+            for p in range(1, self.chips):
+                total = total + self.plane[p - 1, e].astype(F32)
+            self.mine[e] = total.astype(BF16)
+            return carry
+
+        for n in range(self.dp):
+            add(n, 0)
+            if n < self.dp - 1:
+                self.along_dp(n + 1).start()
+
+    def result(self):
+        for o in range(1, self.dp):
+            self.along_dp(o).wait_recv()
+        total = self.mine[self.d].astype(F32)
+        for o in range(1, self.dp):
+            total = total + self.line[o].astype(F32)
+        return total
+
+    def close(self):
+        for p in range(self.chips):
+            self.to_core(p).wait_send()
+        for p in range(1, self.chips):
+            self.to_chip(p).wait_send()
+        for o in range(1, self.dp):
+            self.along_dp(o).wait_send()
 
 
 def forward_attention(
@@ -289,13 +383,31 @@
 
 def backward_attention(
     joined_ref, q_ref, qt_ref, k_ref, kt_ref, v_ref, lse_ref, grad_ref, first_ref, act_ref, pos_ref, weight_ref,
-    input_ref, wgrad_ref, posgrad_ref, sums_ref,
-    gradt_ref, dq_ref, dk_ref, dv_ref, wacc_ref,
+    late_ref, sums_ref, bsum_ref,
+    input_ref, wqg_ref, wkg_ref, wvg_ref, wog_ref, wig_ref, w2g_ref, table_ref, place_ref, line_ref,
+    gradt_ref, dq_ref, dk_ref, dv_ref, wacc_ref, posgrad_ref, total_ref, wpart_ref, ppart_ref, *scratch,
 ):
     row = pl.program_id(0)
     rows = pl.num_programs(0)
     width = act_ref.shape[2]
     blocks = act_ref.shape[1] // WIN
+    d, chip, core, dp, chips = mesh_place()
+    r, c = wqg_ref.shape
+    held, narrow = place_ref.shape
+    folds = c // narrow
+    per = held // folds
+    few = table_ref.shape[0]
+    single = line_ref.shape[1]
+    n = Reduce.COUNT
+    late = Reduce(late_ref, scratch[:n])
+    weights = Reduce(wpart_ref, scratch[n : 2 * n])
+    places = Reduce(ppart_ref, scratch[2 * n :])
+    members = [(a, b) for a in range(chips) for b in range(2)]
+
+    @pl.when(row == 0)
+    def _():
+        meet()
+        late.begin()
 
     def turn(step, carry):
         at = pl.ds(pl.multiple_of(step * WIN, WIN), WIN)
@@ -307,12 +419,14 @@
     def attend(block, pair, joined):
         at = pl.ds(pl.multiple_of(block * WIN, WIN), WIN)
         feats = pl.ds(pl.multiple_of(pair * PAIR, PAIR), PAIR)
-        before = pl.ds(pl.multiple_of(jnp.maximum(block - 1, 0) * WIN, WIN), WIN)
         qt = qt_ref[0, feats, at]
         gt = gradt_ref[feats, at]
         q = q_ref[0, at, feats]
         g = grad_ref[0, at, feats]
-        places = [at, before] if joined else [at]
+        spots = [at]
+        if joined:
+            spots.append(pl.ds(pl.multiple_of((block - 1) * WIN, WIN), WIN))
+            apart = joined_ref[row, block]
         probs = [[], []]
         score_grads = [[], []]
         dq_halves = []
@@ -323,91 +437,153 @@
             lse = lse_ref[0, pair, which : which + 1, at]
             part = []
             inner = None
-            for n, place in enumerate(places):
-                s = nn(k_ref[0, place, feats], q_head)
+            for n, spot in enumerate(spots):
+                s = nn(k_ref[0, spot, feats], q_head)
                 if n == 0:
-                    s = causal(s)
-                p = jnp.exp(s - lse)
-                dp = nn(v_ref[0, place, feats], g_head)
-                part.append((p, dp))
-                term = jnp.sum(p * dp, 0, keepdims=True)
+                    p = jnp.exp(causal(s) - lse)
+                else:
+                    p = jnp.exp(s - (lse - apart))
+                dp_ = nn(v_ref[0, spot, feats], g_head)
+                part.append((p, dp_))
+                term = jnp.sum(p * dp_, 0, keepdims=True)
                 inner = term if inner is None else inner + term
             dq = None
-            for n, place in enumerate(places):
-                p, dp = part[n]
-                ds = (p * (dp - inner)).astype(BF16)
-                probs[n if len(places) > n else 0].append(p.astype(BF16))
+            for n, spot in enumerate(spots):
+                p, dp_ = part[n]
+                ds = (p * (dp_ - inner)).astype(BF16)
+                probs[n].append(p.astype(BF16))
                 score_grads[n].append(ds)
-                term = nn(kt_ref[0, feats, place][half], ds)
+                term = nn(kt_ref[0, feats, spot][half], ds)
                 dq = term if dq is None else dq + term
             dq_halves.append((dq * 0.125).astype(BF16))
         dq_ref[at, feats] = jnp.concatenate(dq_halves, 0).T
         g_both = jnp.concatenate([head_lanes(g, 0), head_lanes(g, 1)], 0)
         q_both = jnp.concatenate([head_lanes(q, 0), head_lanes(q, 1)], 0)
-        for n, place in enumerate(places):
+        for n, spot in enumerate(spots):
             dv = nn(jnp.concatenate(probs[n], 1), g_both)
             dk = nn(jnp.concatenate(score_grads[n], 1), q_both)
             if n == 0:
-                dv_ref[place, feats] = dv
-                dk_ref[place, feats] = dk
+                dv_ref[spot, feats] = dv
+                dk_ref[spot, feats] = dk
             else:
-                dv_ref[place, feats] += dv
-                dk_ref[place, feats] += dk
-
-    def one_block(block, carry):
-        together = joined_ref[row, block] == 1
-
-        @pl.when(together)
-        def _():
-            lax.fori_loop(0, H // 2, lambda p, c: (attend(block, p, True), c)[1], 0)
-
-        @pl.when(jnp.logical_not(together))
-        def _():
-            lax.fori_loop(0, H // 2, lambda p, c: (attend(block, p, False), c)[1], 0)
-
+                dv_ref[spot, feats] += dv
+                dk_ref[spot, feats] += dk
+
+    def first(pair, carry):
+        attend(0, pair, False)
         return carry
 
-    lax.fori_loop(0, blocks, one_block, 0)
+    def other(n, carry):
+        attend(n // (H // 2) + 1, lax.rem(n, H // 2), True)
+        return carry
+
+    lax.fori_loop(0, H // 2, first, 0)
 
     @pl.when(row == 0)
     def _():
+        late.across()
+
+    @pl.when(row == rows - 1)
+    def _():
+        late.along()
+
+    lax.fori_loop(0, (blocks - 1) * (H // 2), other, 0)
+
+    @pl.when(row == 0)
+    def _():
         wacc_ref[...] = jnp.zeros_like(wacc_ref)
-        sums_ref[...] = jnp.zeros_like(sums_ref)
+        total_ref[...] = sums_ref[...]
         posgrad_ref[...] = jnp.zeros_like(posgrad_ref)
 
     tile = 2 * WIN
-
-    def finish(step, carry):
+    tiles = act_ref.shape[1] // tile
+
+    def gather_tile(step, carry):
         at = pl.ds(pl.multiple_of(step * tile, tile), tile)
         dq = dq_ref[at, :]
         dk = dk_ref[at, :].astype(BF16)
         dv = dv_ref[at, :].astype(BF16)
         every = jnp.concatenate([dq, dk, dv], 1)
+        low = (act_ref[0, at, :].astype(F32) + pos_ref[at, :].astype(F32)).astype(BF16)
+        wacc_ref[...] += nn(low.T, every)
+        total_ref[0:1, :] += column_sum(dq)
+        total_ref[1:2, :] += column_sum(dv)
+        return carry
+
+    lax.fori_loop(0, tiles, gather_tile, 0)
+
+    @pl.when(row == rows - 1)
+    def _():
+        packed = jnp.zeros((SMALL - few - 1, c), F32)
+        wide = lambda x: jnp.concatenate([x, jnp.zeros((x.shape[0], c - x.shape[1]), F32)], 1)
+        for e in range(dp):
+            for f, (a, b) in enumerate(members):
+                for n in range(3):
+                    lanes = slice(n * width + e * c, n * width + (e + 1) * c)
+                    wpart_ref[e, a, b, n * r : (n + 1) * r, :] = wacc_ref[f * r : (f + 1) * r, lanes].astype(BF16)
+                table = total_ref[e * few : (e + 1) * few, f * narrow : (f + 1) * narrow]
+                spot = (e * len(members) + f) * single
+                line = bsum_ref[:, spot : spot + single]
+                wpart_ref[e, a, b, 3 * r :, :] = jnp.concatenate([wide(table), wide(line), packed], 0).astype(BF16)
+        weights.begin()
+
+    def spread_tile(step, carry):
+        at = pl.ds(pl.multiple_of(step * tile, tile), tile)
+        every = jnp.concatenate([dq_ref[at, :], dk_ref[at, :].astype(BF16), dv_ref[at, :].astype(BF16)], 1)
         start_grad = first_ref[0, at, :] + nt(every, weight_ref[...])
         input_ref[0, at, :] = start_grad.astype(BF16)
         posgrad_ref[at, :] += start_grad
-        low = (act_ref[0, at, :].astype(F32) + pos_ref[at, :].astype(F32)).astype(BF16)
-        wacc_ref[...] += nn(low.T, every)
-        sums_ref[0:1, :] += column_sum(dq)
-        sums_ref[1:2, :] += column_sum(dv)
         return carry
 
-    lax.fori_loop(0, act_ref.shape[1] // tile, finish, 0)
+    lax.fori_loop(0, tiles, spread_tile, 0)
 
     @pl.when(row == rows - 1)
     def _():
-        wgrad_ref[...] = wacc_ref[...].astype(wgrad_ref.dtype)
+        weights.across()
+        for e in range(dp):
+            for f, (a, b) in enumerate(members):
+                lanes = slice(f * narrow, (f + 1) * narrow)
+                ppart_ref[e, a, b] = jnp.concatenate(
+                    [
+                        posgrad_ref[e * held + n * per : e * held + (n + 1) * per, lanes].astype(BF16)
+                        for n in range(folds)
+                    ],
+                    1,
+                )
+        places.begin()
+        owned = late.result()
+        wide_parts = wig_ref.shape[1] // c
+        wog_ref[...] = owned[:r]
+        for n in range(wide_parts):
+            wig_ref[:, n * c : (n + 1) * c] = owned[(1 + n) * r : (2 + n) * r]
+        w2g_ref[...] = owned[(1 + wide_parts) * r :]
+        places.across()
+        weights.along()
+        places.along()
+        owned = weights.result()
+        for n, ref in enumerate((wqg_ref, wkg_ref, wvg_ref)):
+            ref[...] = owned[n * r : (n + 1) * r]
+        table_ref[...] = owned[3 * r : 3 * r + few, :narrow]
+        line_ref[...] = owned[3 * r + few : 3 * r + few + 1, :single]
+        owned = places.result()
+        for n in range(folds):
+            place_ref[n * per : (n + 1) * per, :] = owned[:, n * narrow : (n + 1) * narrow]
+        late.close()
+        weights.close()
+        places.close()
 
 
 def feed_forward(
     ctx_ref, act_ref, pos_ref, cot_ref, late_ref, vec_ref, bias_ref,
-    out_ref, first_ref, grad_ref, wog_ref, wig_ref, w2g_ref, sums_ref, bsum_ref,
+    out_ref, first_ref, grad_ref, part_ref, sums_ref, bsum_ref,
     wo_acc, wi_acc, w2_acc, slope_ref, wo_ref, wi_ref, w2_ref,
 ):
     step = pl.program_id(0)
     width = ctx_ref.shape[1]
     dp, chips, _, _, c = late_ref.shape
     r = width // (2 * chips)
+    parts = bias_ref.shape[1] // dp // c
+    tall = bias_ref.shape[1] // (2 * chips)
     hidden = bias_ref.shape[1]
     part = 512
 
@@ -418,8 +594,6 @@
         w2_acc[...] = jnp.zeros_like(w2_acc)
         sums_ref[...] = jnp.zeros_like(sums_ref)
         bsum_ref[...] = jnp.zeros_like(bsum_ref)
-        parts = hidden // dp // c
-        tall = hidden // (2 * chips)
 
         def unpack(chip, carry):
             for core in range(2):
@@ -499,13 +673,25 @@
 
     @pl.when(step == pl.num_programs(0) - 1)
     def _():
-        wog_ref[...] = wo_acc[...].astype(wog_ref.dtype)
-        wig_ref[...] = wi_acc[...].astype(wig_ref.dtype)
-        w2g_ref[...] = w2_acc[...].astype(w2g_ref.dtype)
+        for e in range(dp):
+            lanes = slice(e * c, (e + 1) * c)
+            for f in range(2 * chips):
+                rows = slice(f * r, (f + 1) * r)
+                a, b = f // 2, f % 2
+                part_ref[e, a, b, :r, :] = wo_acc[rows, lanes].astype(BF16)
+                for n in range(parts):
+                    wide = slice((e * parts + n) * c, (e * parts + n + 1) * c)
+                    part_ref[e, a, b, (1 + n) * r : (2 + n) * r, :] = wi_acc[rows, wide].astype(BF16)
+                turned = w2_acc[lanes, f * tall : (f + 1) * tall].astype(BF16)
+                part_ref[e, a, b, (1 + parts) * r :, :] = turned.T
 
 
 def whole(shape):
     return pl.BlockSpec(shape, lambda *_: (0,) * len(shape))
+
+
+def once(shape):
+    return pl.BlockSpec(shape, lambda *_: (0,) * len(shape), pipeline_mode=pl.Buffered(1))
 
 
 def run_forward(apart, act, wq, wk, wv, wo, wi, w2, table, place, line):
@@ -551,36 +737,45 @@
     )(apart, act, wq, wk, wv, wo, wi, w2, table, place, line)
 
 
-def run_backward(joined, q, qt, k, kt, v, lse, grad, first, act, pos, weight):
+def run_backward(apart, q, qt, k, kt, v, lse, grad, first, act, pos, weight, late, sums, bsum, shapes):
     rows, seq, width = act.shape
-    row3 = lambda shape: pl.BlockSpec((1,) + shape, lambda r, *_: (r,) + (0,) * len(shape))
+    dp, fsdp = lax.axis_size("dp"), lax.axis_size("fsdp")
+    chips = fsdp // 2
+    r, c = shapes[0]
+    held, narrow = shapes[7]
+    first_rows = 3 * r + SMALL
+    place_rows = held * narrow // c
+    row3 = lambda shape: pl.BlockSpec((1,) + shape, lambda i: (i,) + (0,) * len(shape))
     seqs = row3((seq, width))
     turned = row3((width, seq))
+    lone = pl.BlockSpec((1, seq, width), lambda i: (i, 0, 0), pipeline_mode=pl.Buffered(1))
     return pl.pallas_call(
         backward_attention,
-        grid_spec=pltpu.PrefetchScalarGridSpec(
-            num_scalar_prefetch=1,
-            grid=(rows,),
-            in_specs=[seqs, turned, seqs, turned, seqs, row3((H // 2, 2, seq)), seqs, seqs, seqs,
-                      whole((seq, width)), whole((width, 3 * width))],
-            out_specs=[seqs, whole((width, 3 * width)), whole((seq, width)), whole((8, width))],
-            scratch_shapes=[
-                pltpu.VMEM((width, seq), BF16),
-                pltpu.VMEM((seq, width), BF16),
-                pltpu.VMEM((seq, width), F32),
-                pltpu.VMEM((seq, width), F32),
-                pltpu.VMEM((width, 3 * width), F32),
-            ],
+        grid=(rows,),
+        in_specs=[pl.BlockSpec(memory_space=pltpu.SMEM), seqs, turned, seqs, turned, seqs,
+                  row3((H // 2, 2, seq)), lone, lone, lone, once(pos.shape), once(weight.shape), once(late.shape),
+                  once(sums.shape), once(bsum.shape)],
+        out_specs=[seqs] + [whole(x) for x in shapes],
+        scratch_shapes=[
+            pltpu.VMEM((width, seq), BF16),
+            pltpu.VMEM((seq, width), BF16),
+            pltpu.VMEM((seq, width), F32),
+            pltpu.VMEM((seq, width), F32),
+            pltpu.VMEM((width, 3 * width), F32),
+            pltpu.VMEM((seq, width), F32),
+            pltpu.VMEM((8, width), F32),
+            pltpu.VMEM((dp, chips, 2, first_rows, c), BF16),
+            pltpu.VMEM((dp, chips, 2, place_rows, c), BF16),
+        ]
+        + Reduce.scratch(dp, chips, late.shape[3], c)
+        + Reduce.scratch(dp, chips, first_rows, c)
+        + Reduce.scratch(dp, chips, place_rows, c),
+        out_shape=[jax.ShapeDtypeStruct((rows, seq, width), BF16)] + [jax.ShapeDtypeStruct(x, F32) for x in shapes],
+        compiler_params=pltpu.CompilerParams(
+            vmem_limit_bytes=VMEM_LIMIT, collective_id=1, has_side_effects=True
         ),
-        out_shape=[
-            jax.ShapeDtypeStruct((rows, seq, width), BF16),
-            jax.ShapeDtypeStruct((width, 3 * width), BF16),
-            jax.ShapeDtypeStruct((seq, width), F32),
-            jax.ShapeDtypeStruct((8, width), F32),
-        ],
-        compiler_params=pltpu.CompilerParams(vmem_limit_bytes=VMEM_LIMIT),
         name="backward_attention",
-    )(joined, q, qt, k, kt, v, lse, grad, first, act, pos, weight)
+    )(apart, q, qt, k, kt, v, lse, grad, first, act, pos, weight, late, sums, bsum)
 
 
 def run_feed_forward(ctx, act, pos, cot, late, vec, bias, tile=256):
@@ -589,14 +784,12 @@
     hidden = bias.shape[1]
     per_row = seq // tile
     tok = pl.BlockSpec((tile, width), lambda t: (t, 0))
-    once = lambda shape: pl.BlockSpec(shape, lambda *_: (0,) * len(shape), pipeline_mode=pl.Buffered(1))
     return pl.pallas_call(
         feed_forward,
         grid=(tokens // tile,),
         in_specs=[tok, tok, pl.BlockSpec((tile, width), lambda t: (t % per_row, 0)), tok,
                   once(late.shape), whole(vec.shape), whole(bias.shape)],
-        out_specs=[tok, tok, tok, whole((width, width)), whole((width, hidden)), whole((width, hidden)),
-                   whole((8, width)), whole((1, hidden))],
+        out_specs=[tok, tok, tok, whole(late.shape), whole((8, width)), whole((1, hidden))],
         scratch_shapes=[
             pltpu.VMEM((width, width), F32),
             pltpu.VMEM((width, hidden), F32),
@@ -610,9 +803,7 @@
             jax.ShapeDtypeStruct((tokens, width), BF16),
             jax.ShapeDtypeStruct((tokens, width), F32),
             jax.ShapeDtypeStruct((tokens, width), BF16),
-            jax.ShapeDtypeStruct((width, width), BF16),
-            jax.ShapeDtypeStruct((width, hidden), BF16),
-            jax.ShapeDtypeStruct((width, hidden), BF16),
+            jax.ShapeDtypeStruct(late.shape, BF16),
             jax.ShapeDtypeStruct((8, width), F32),
             jax.ShapeDtypeStruct((1, hidden), F32),
         ],
@@ -633,41 +824,24 @@
     vectors, positions, inner_bias, output_cotangent,
 ):
     rows, seq, width = activations.shape
-    dp, fsdp = lax.axis_size("dp"), lax.axis_size("fsdp")
-    both = ("dp", "fsdp")
-
     joined = joined_blocks(window_lengths, seq)
     apart = jnp.where(joined == 1, 0.0, -1e30).astype(F32)
     q, qt, k, kt, v, ctx, lse, weight, pos, vec, bias, late = run_forward(
         apart, activations, query_weight, key_weight, value_weight, output_weight, inner_weight, outer_weight,
         vectors, positions, inner_bias.reshape(1, -1),
     )
-    c = query_weight.shape[1]
     flat = lambda x: x.reshape(rows * seq, width)
-    out, first, grad, wog, wig, w2g, sums, bsum = run_feed_forward(
+    deep = lambda x: x.reshape(rows, seq, width)
+    out, first, grad, part, sums, bsum = run_feed_forward(
         flat(ctx), flat(activations), pos, flat(output_cotangent), late, vec, bias
     )
-    deep = lambda x: x.reshape(rows, seq, width)
-    input_grad, wgrad, posgrad, more = run_backward(
-        joined, q, qt, k, kt, v, lse, deep(grad), deep(first), activations, pos, weight
+    shapes = [x.shape for x in (query_weight, key_weight, value_weight, output_weight, inner_weight, outer_weight,
+                                vectors, positions)] + [(1, inner_bias.shape[0])]
+    input_grad, *owned = run_backward(
+        apart, q, qt, k, kt, v, lse, deep(grad), deep(first), activations, pos, weight, part, sums, bsum, shapes
     )
-    sums = jnp.concatenate([more[0:2], sums[2:]], 0)
-
-    def scatter(x):
-        return lax.psum_scatter(x, both, scatter_dimension=0, tiled=True)[0].astype(F32)
-
-    def split_columns(x, r, c):
-        return x.reshape(fsdp, r, dp, c).transpose(2, 0, 1, 3).reshape(dp * fsdp, r, c)
-
-    r = query_weight.shape[0]
-    own = [scatter(split_columns(g, r, c)) for g in (wgrad[:, :width], wgrad[:, width:2 * width], wgrad[:, 2 * width:], wog)]
-    own.append(scatter(split_columns(wig, *inner_weight.shape)))
-    own.append(scatter(split_columns(w2g.T, *outer_weight.shape)))
-    split_rows = lambda x, s: x.reshape(dp, s[0], fsdp, s[1]).transpose(0, 2, 1, 3).reshape((dp * fsdp,) + s)
-    own.append(scatter(split_rows(sums, vectors.shape)))
-    own.append(scatter(split_rows(posgrad, positions.shape)))
-    own.append(scatter(bsum.reshape(dp * fsdp, -1)))
-    return (deep(out), input_grad) + tuple(own)
+    owned[8] = owned[8].reshape(-1)
+    return (deep(out), input_grad) + tuple(owned)
 
 
 def solution(mesh):

time: 1130 us -> 220 us (0.19)
  waiting for transfers between devices: 861 us -> 0 us
  blocking collectives: 40.9 us -> 0 us
  Pallas kernels: 171 us -> 206 us
  local copies, waits for them, and re-layouts: 27.3 us -> 11.1 us
  between operations: 14.3 us -> 0.72 us
    reduce_scatter x7 -> x0, waiting for transfers between devices: 861 us -> none  [scatter(): lax.psum_scatter(x, both, scatter_dimension=0, tiled=True)[0].astype(F32)]
    unnamed x1 -> x0, blocking collectives: 40.9 us -> none
    pallas_call x1, Pallas kernels: 49.5 us -> 84.5 us  [run_backward(): pl.pallas_call(backward_attention, grid=(rows,), in_specs=[pl.BlockSpec(m...]
    transpose x8 -> x0, local copies, waits for them, and re-layouts: 11.9 us -> none  [the longest x6 8.54 us: split_columns(): x.reshape(fsdp, r, dp, c).transpose(2, 0, 1, 3).reshape(dp * fsdp, r, c)]
  transfers between devices with their start and end apart: 7 -> 0, of which waited for: 7 -> 0; matrix products, arithmetic and copies ran while one was open for 3% -> 0% of each run, Pallas kernels for 0% -> 0%
where the time goes in v2:
time: 220 us; the launch traced here: 219 us
  Pallas kernels  206 us (94%)
  local copies, waits for them, and re-layouts  11.1 us (5%)
    pallas_call x1, Pallas kernels, run_backward(): pl.pallas_call(backward_attention, grid=(rows,), in_specs=[pl.BlockSpec(m...  84.5 us
    pallas_call x1, Pallas kernels, run_forward(): pl.pallas_call(forward_attention, grid=(rows,), in_specs=[pl.BlockSpec(me...  69.5 us
    pallas_call x1, Pallas kernels, run_feed_forward(): pl.pallas_call(feed_forward, grid=(tokens // tile,), in_specs=[tok, tok,...  51.9 us
    unnamed x27, local copies, waits for them, and re-layouts  11.1 us

profile of v2, /device:TPU:0, one launch (start us, length us, event | category | flops | bytes accessed | tf_op | source)
XLA Modules:
  0.0 219.4 jit_solution(3854115975370750577)
XLA Ops:
  0.7 0.9 reduce_window_sum.11
  1.5 0.2 compare_reduce_fusion
  1.7 0.6 compare_select_fusion.joined_ref
  2.3 1.5 copy.25.place_ref
  3.8 69.5 %forward_attention.1 = (bf16[2,1024,512]{2,1,0:T(8,128)(2,1)}, bf16[2,512,1024]{2,1,0:T(8,128)(2,1)}, bf16[2,1024,512]{2,1,0:T(8,128)(2,1)}, bf16[2,512,1024]{2,...) custom-call(f32[2,4]{1,0:T(2,128)} %compare_select_fusion.joined_ref, ...), custom_call_target="tpu_custom_call" | custom-call | tf_op jit(solution)/shard_map/forward_attention/pallas_call | solution.py:711
  73.3 51.9 %feed_forward.1 = (bf16[2048,512]{1,0:T(8,128)(2,1)}, f32[2048,512]{1,0:T(8,128)}, bf16[2048,512]{1,0:T(8,128)(2,1)}, bf16[4,4,2,576,128]{4,3,2,1,0:T(8,128)(2,1)}, f32[8,512]{1,0:T(8,128)}, /*index=5*/f32[1,2048]{1,0:T(1,128)}) custom-call(bf16[2048,512]{1,0:T(8,128)(2,1)} %bitcast.11, bf16[2048,512]{1,0:T(8,128)(2,1)} %bitcast.8, ...), custom_call_target="tpu_custom_call" | custom-call | tf_op jit(solution)/shard_map/feed_forward/pallas_call | solution.py:787
  125.2 84.5 %backward_attention.1 = (bf16[2,1024,512]{2,1,0:T(8,128)(2,1)}, f32[64,128]{1,0:T(8,128)}, f32[64,128]{1,0:T(8,128)}, f32[64,128]{1,0:T(8,128)}, f32[64,128]{1,0...) custom-call(f32[2,4]{1,0:T(2,128)} %compare_select_fusion.joined_ref, ...), custom_call_target="tpu_custom_call" | custom-call | tf_op jit(solution)/shard_map/backward_attention/pallas_call | solution.py:752
  209.7 1.6 copy.26
  211.3 0.0 copy-start.5
  211.3 0.0 copy-start.4
  211.3 0.0 copy-start.3
  211.3 0.0 copy-start.1
  211.3 0.0 copy-start
  211.3 0.0 copy-start.6
  211.4 0.0 copy-start.7
  211.4 3.1 %copy.36 = bf16[2,1024,512]{2,1,0:T(8,128)(2,1)} copy(bf16[2,1024,512]{2,1,0:T(8,128)(2,1)} %get-tuple-element.101) | data formatting | bytes 4194304
  214.5 0.0 copy-done.5
  214.5 0.6 copy.37
  215.1 0.0 copy-done.4
  215.1 0.6 copy.38
  215.7 0.0 copy-done.3
  215.7 0.6 copy.39
  216.3 0.0 copy-done.2
  216.3 0.6 copy.40
  217.0 0.0 copy-done.1
  217.0 0.7 copy.41
  217.6 0.0 copy-done
  217.6 0.7 copy.42
  218.3 0.0 copy-done.6
  218.3 0.6 copy.43
  218.8 0.0 copy-done.7
  218.8 0.5 copy.44
  (3 shorter events, 0.0 us)
Async XLA Ops:
  211.3 3.2 %copy-start.5 = (f32[64,128]{1,0:T(8,128)S(1)}, f32[64,128]{1,0:T(8,128)}, u32[]{:S(2)}) copy-start(f32[64,128]{1,0:T(8,128)} %get-tuple-element.102) | copy-start | bytes 98308
  211.3 3.8 %copy-start.4 = (f32[64,128]{1,0:T(8,128)S(1)}, f32[64,128]{1,0:T(8,128)}, u32[]{:S(2)}) copy-start(f32[64,128]{1,0:T(8,128)} %get-tuple-element.103) | copy-start | bytes 98308
  211.3 4.4 %copy-start.3 = (f32[64,128]{1,0:T(8,128)S(1)}, f32[64,128]{1,0:T(8,128)}, u32[]{:S(2)}) copy-start(f32[64,128]{1,0:T(8,128)} %get-tuple-element.104) | copy-start | bytes 98308
  211.3 5.0 %copy-start.2 = (f32[64,128]{1,0:T(8,128)S(1)}, f32[64,128]{1,0:T(8,128)}, u32[]{:S(2)}) copy-start(f32[64,128]{1,0:T(8,128)} %get-tuple-element.105) | copy-start | bytes 98308
  211.3 5.6 %copy-start.1 = (f32[64,512]{1,0:T(8,128)S(1)}, f32[64,512]{1,0:T(8,128)}, u32[]{:S(2)}) copy-start(f32[64,512]{1,0:T(8,128)} %get-tuple-element.106) | copy-start | bytes 393220
  211.3 6.3 %copy-start = (f32[256,128]{1,0:T(8,128)S(1)}, f32[256,128]{1,0:T(8,128)}, u32[]{:S(2)}) copy-start(f32[256,128]{1,0:T(8,128)} %get-tuple-element.107) | copy-start | bytes 393220
  211.3 6.9 %copy-start.6 = (f32[2,64]{1,0:T(2,128)S(1)}, f32[2,64]{1,0:T(2,128)}, u32[]{:S(2)}) copy-start(f32[2,64]{1,0:T(2,128)} %get-tuple-element.108) | copy-start | bytes 1540
  211.4 7.5 %copy-start.7 = (f32[1,64]{1,0:T(1,128)S(1)}, f32[1,64]{1,0:T(1,128)}, u32[]{:S(2)}) copy-start(f32[1,64]{1,0:T(1,128)} %get-tuple-element.66) | copy-start | bytes 772

commit v3 on v1

v3 whole, which is shorter than its diff:
```python
import functools

import jax
import jax.numpy as jnp
from jax import lax
from jax.experimental import pallas as pl
from jax.experimental.pallas import tpu as pltpu
from jax.sharding import PartitionSpec as P

H = 8
HD = 64
WIN = 256
PAIR = 2 * HD
VMEM_LIMIT = 62 * 1024 * 1024
F32 = jnp.float32
BF16 = jnp.bfloat16
MESH = pl.DeviceIdType.MESH
SMALL = 16


def nn(left, right):
    return lax.dot_general(left, right, (((1,), (0,)), ((), ())), preferred_element_type=F32)


def nt(left, right):
    return lax.dot_general(left, right, (((1,), (1,)), ((), ())), preferred_element_type=F32)


def tn(left, right):
    return lax.dot_general(left, right, (((0,), (0,)), ((), ())), preferred_element_type=F32)


def column_sum(value):
    return jnp.sum(value.astype(F32), 0, keepdims=True)


def head_rows(pair, which):
    zeros = jnp.zeros((HD, pair.shape[1]), pair.dtype)
    if which == 0:
        return jnp.concatenate([pair[:HD], zeros], 0)
    return jnp.concatenate([zeros, pair[HD:]], 0)


def head_lanes(pair, which):
    lane = lax.broadcasted_iota(jnp.int32, pair.shape, 1)
    keep = (lane < HD) if which == 0 else (lane >= HD)
    return jnp.where(keep, pair, jnp.zeros_like(pair))


def causal(scores):
    key = lax.broadcasted_iota(jnp.int32, scores.shape, 0)
    query = lax.broadcasted_iota(jnp.int32, scores.shape, 1)
    return jnp.where(key <= query, scores, -1e30)


def block_of(block):
    return slice(block * WIN, (block + 1) * WIN)


def spots_of(block):
    return [block_of(n) for n in (block, block - 1) if n >= 0]


def pair_of(head):
    return slice(head // 2 * PAIR, (head // 2 + 1) * PAIR)


def staggered(tasks, stages):
    held = {}
    for step in range(len(tasks) + len(stages) - 1):
        for n, stage in enumerate(stages):
            task = step - n
            if 0 <= task < len(tasks):
                args = (held.pop(task),) if n else ()
                held[task] = stage(*tasks[task], *args)


class Place:
    def __init__(self):
        fsdp = lax.axis_index("fsdp")
        self.d, self.dp = lax.axis_index("dp"), lax.axis_size("dp")
        self.side = side_of(lax.axis_size("fsdp"))
        self.chip, self.core = fsdp // 2, lax.rem(fsdp, 2)
        y, x = self.chip // self.side, lax.rem(self.chip, self.side)
        self.a = y + self.core * (x - y)
        self.b = x + self.core * (y - x)

    def device(self, a, b):
        straight, turned = a * self.side + b, b * self.side + a
        return {"fsdp": (straight + self.core * (turned - straight)) * 2 + self.core}

    def sibling(self):
        return {"fsdp": self.chip * 2 + 1 - self.core}

    def at_a(self, n):
        return lax.rem(self.a + n + self.side, self.side)

    def at_b(self, n):
        return lax.rem(self.b + n + self.side, self.side)

    def at_dp(self, n):
        return lax.rem(self.d + n + self.dp, self.dp)


def side_of(fsdp):
    side = 1
    while side * side * 2 < fsdp:
        side += 1
    assert side * side * 2 == fsdp
    return side


def members(side):
    found = []
    for f in range(2 * side * side):
        y, x = f // 2 // side, f // 2 % side
        found.append((x, y, 1) if f % 2 else (y, x, 0))
    return found


def remote(src, dst, send, recv, device):
    return pltpu.make_async_remote_copy(
        src_ref=src, dst_ref=dst, send_sem=send, recv_sem=recv, device_id=device, device_id_type=MESH
    )


def meet(at):
    barrier = pltpu.get_barrier_semaphore()
    others = [{"dp": at.at_dp(n)} for n in range(1, at.dp)]
    others += [at.device(at.a, at.at_b(n)) for n in range(1, at.side)]
    others += [at.device(at.at_a(n), at.b) for n in range(1, at.side)]
    others.append(at.sibling())
    for other in others:
        pl.semaphore_signal(barrier, inc=1, device_id=other, device_id_type=MESH)
    pl.semaphore_wait(barrier, len(others))


class Gather:
    COUNT = 8

    def __init__(self, buf, sems, at):
        self.buf, self.at = buf, at
        self.zs, self.zr, self.bs, self.br, self.sa, self.ra, self.cs, self.cr = sems

    @staticmethod
    def semaphores(dp, side):
        dma = pltpu.SemaphoreType.DMA
        shapes = [(dp,), (dp, side), (dp, side, side), (side, side)]
        return [dma(x) for x in shapes for _ in range(2)]

    def along_dp(self, o):
        at = self.at
        block = self.buf.at[at.d, at.a, at.b, at.core]
        return remote(block, block, self.zs.at[o], self.zr.at[o], {"dp": at.at_dp(o)})

    def along_b(self, o, p):
        at = self.at
        block = self.buf.at[at.at_dp(-o), at.a, at.b, at.core]
        return remote(block, block, self.bs.at[o, p], self.br.at[o, p], at.device(at.a, at.at_b(p)))

    def along_a(self, o, p, q):
        at = self.at
        block = self.buf.at[at.at_dp(-o), at.a, at.at_b(-p), at.core]
        return remote(block, block, self.sa.at[o, p, q], self.ra.at[o, p, q], at.device(at.at_a(q), at.b))

    def to_core(self, q, p):
        at = self.at
        block = self.buf.at[:, at.at_a(-q), at.at_b(-p), at.core]
        return remote(block, block, self.cs.at[q, p], self.cr.at[q, p], at.sibling())

    def begin(self):
        for o in range(1, self.at.dp):
            self.along_dp(o).start()
        self.pass_on(0)

    def pass_on(self, o):
        for p in range(1, self.at.side):
            self.along_b(o, p).start()
        for q in range(1, self.at.side):
            self.along_a(o, 0, q).start()

    def spread(self, o):
        self.along_dp(o).wait_recv()
        self.pass_on(o)

    def relay(self, o):
        for p in range(1, self.at.side):
            self.along_b(o, p).wait_recv()
            for q in range(1, self.at.side):
                self.along_a(o, p, q).start()

    def near(self):
        for p in range(self.at.side):
            self.to_core(0, p).start()

    def share(self):
        for p in range(self.at.side):
            for q in range(1, self.at.side):
                for o in range(self.at.dp):
                    self.along_a(o, p, q).wait_recv()
                self.to_core(q, p).start()

    def arrive(self):
        for q in range(self.at.side):
            for p in range(self.at.side):
                self.to_core(q, p).wait_recv()

    def close(self):
        for o in range(1, self.at.dp):
            self.along_dp(o).wait_send()
        for o in range(self.at.dp):
            for p in range(1, self.at.side):
                self.along_b(o, p).wait_send()
            for p in range(self.at.side):
                for q in range(1, self.at.side):
                    self.along_a(o, p, q).wait_send()
        for q in range(self.at.side):
            for p in range(self.at.side):
                self.to_core(q, p).wait_send()


def add_up(terms):
    if len(terms) == 2:
        return terms[0] + terms[1]
    return sum(x.astype(F32) for x in terms).astype(BF16)


class Reduce:
    COUNT = 13

    def __init__(self, part, scratch, at, own=None):
        self.part, self.at = part, at
        self.own, self.own_sem = own or (None, None)
        (self.pair, self.plane, self.row, self.mine, self.line,
         self.cs, self.cr, self.sa, self.ra, self.bs, self.br, self.zs, self.zr) = scratch

    @staticmethod
    def scratch(dp, side, rows, c):
        dma = pltpu.SemaphoreType.DMA
        return [
            pltpu.VMEM((dp, side, side, rows, c), BF16),
            pltpu.VMEM((side - 1, dp, side, rows, c), BF16),
            pltpu.VMEM((side - 1, dp, rows, c), BF16),
            pltpu.VMEM((dp, rows, c), BF16),
            pltpu.VMEM((dp - 1, rows, c), BF16),
        ] + [dma((dp,))] * 2 + [dma((dp, side))] * 4 + [dma((dp,))] * 2

    def to_core(self, e):
        at = self.at
        return remote(self.part.at[e, :, :, 1 - at.core], self.pair.at[e], self.cs.at[e], self.cr.at[e], at.sibling())

    def along_a(self, e, q):
        at = self.at
        to = at.at_a(q)
        return remote(
            self.pair.at[e, to], self.plane.at[q - 1, e], self.sa.at[e, q], self.ra.at[e, q], at.device(to, at.b)
        )

    def along_b(self, e, p):
        at = self.at
        to = at.at_b(p)
        return remote(
            self.pair.at[e, at.a, to], self.row.at[p - 1, e], self.bs.at[e, p], self.br.at[e, p], at.device(at.a, to)
        )

    def along_dp(self, o):
        at = self.at
        to = at.at_dp(o)
        return remote(self.mine.at[to], self.line.at[o - 1], self.zs.at[o], self.zr.at[o], {"dp": to})

    def own_half(self):
        return pltpu.make_async_copy(self.part.at[:, :, :, self.at.core], self.own, self.own_sem)

    def begin(self, e):
        self.to_core(e).start()

    def across(self, e):
        at = self.at
        self.to_core(e).wait_recv()
        for n in list(range(1, at.side)) + [0]:
            a = at.at_a(n)
            for b in range(at.side):
                own = self.part[e, a, b, at.core] if self.own is None else self.own[e, a, b]
                self.pair[e, a, b] = add_up([own, self.pair[e, a, b]])
            if n:
                self.along_a(e, n).start()

    def middle(self, e):
        at = self.at
        for q in range(1, at.side):
            self.along_a(e, q).wait_recv()
        for n in list(range(1, at.side)) + [0]:
            b = at.at_b(n)
            terms = [self.pair[e, at.a, b]] + [self.plane[q - 1, e, b] for q in range(1, at.side)]
            self.pair[e, at.a, b] = add_up(terms)
            if n:
                self.along_b(e, n).start()

    def along(self, e):
        at = self.at
        for p in range(1, at.side):
            self.along_b(e, p).wait_recv()
        self.mine[e] = add_up([self.pair[e, at.a, at.b]] + [self.row[p - 1, e] for p in range(1, at.side)])

        @pl.when(e != at.d)
        def _():
            self.along_dp(lax.rem(e - at.d + at.dp, at.dp)).start()

    def result(self):
        at = self.at
        for o in range(1, at.dp):
            self.along_dp(o).wait_recv()
        total = self.mine[at.d].astype(F32)
        for o in range(1, at.dp):
            total = total + self.line[o - 1].astype(F32)
        return total

    def close(self):
        at = self.at
        for e in range(at.dp):
            self.to_core(e).wait_send()
            for n in range(1, at.side):
                self.along_a(e, n).wait_send()
                self.along_b(e, n).wait_send()
        for o in range(1, at.dp):
            self.along_dp(o).wait_send()


def apart(lengths_ref, row, block):
    total = jnp.int32(0)
    cut = jnp.bool_(False)
    for n in range(lengths_ref.shape[1]):
        total = total + lengths_ref[row, n]
        cut = cut | (total == block * WIN)
    return jnp.where(cut, jnp.float32(-1e30), jnp.float32(0.0))


def forward_attention(
    lengths_ref, act_ref, wq_ref, wk_ref, wv_ref, wo_ref, wi_ref, w2_ref, table_ref, place_ref, line_ref,
    q_ref, qt_ref, k_ref, kt_ref, v_ref, ctx_ref, lse_ref, weight_ref, pos_ref, vec_ref, bias_ref, late_ref,
    vt_ref, ctxt_ref, early_ref, own_ref, own_sem, *sems,
):
    row = pl.program_id(0)
    rows = pl.num_programs(0)
    width = act_ref.shape[2]
    blocks = act_ref.shape[1] // WIN
    at = Place()
    dp = at.dp
    here = (at.d, at.a, at.b, at.core)
    r, c = wq_ref.shape
    narrow, held = place_ref.shape
    folds = c // narrow
    per = held // folds
    early = Gather(early_ref, sems[: Gather.COUNT], at)
    late = Gather(late_ref, sems[Gather.COUNT :], at)

    def own_copy():
        return pltpu.make_async_copy(own_ref, late_ref.at[here], own_sem)

    @pl.when(row == 0)
    def _():
        for n, ref in enumerate((wq_ref, wk_ref, wv_ref)):
            early_ref[here + (slice(n * r, (n + 1) * r),)] = ref[...]
        place = place_ref[...].T
        early_ref[here + (slice(3 * r, 3 * r + per),)] = jnp.concatenate(
            [place[n * per : (n + 1) * per] for n in range(folds)], 1
        )
        wide = lambda x: jnp.concatenate([x, jnp.zeros((x.shape[0], c - x.shape[1]), F32)], 1)
        table = wide(table_ref[...].astype(F32))
        line = wide(line_ref[...].astype(F32))
        few = table.shape[0]
        small = jnp.concatenate([table, line, jnp.zeros((SMALL - few - 1, c), F32)], 0)
        early_ref[here + (slice(3 * r + per, None),)] = small.astype(BF16)
        own_ref[:r, :] = wo_ref[...]
        wide_parts = wi_ref.shape[1] // c
        for n in range(wide_parts):
            own_ref[(1 + n) * r : (2 + n) * r, :] = wi_ref[:, n * c : (n + 1) * c]
        own_ref[(1 + wide_parts) * r :, :] = w2_ref[...]
        own_copy().start()
        meet(at)
        early.begin()
        early.relay(0)
        for o in range(1, dp):
            early.spread(o)
        for o in range(1, dp):
            early.relay(o)
        early.near()
        own_copy().wait()
        late.begin()
        early.share()
        early.arrive()
        group = members(at.side)
        for f, (a, b, core) in enumerate(group):
            for n in range(3):
                weight_ref[f * r : (f + 1) * r, n * width : (n + 1) * width] = jnp.concatenate(
                    [early_ref[e, a, b, core, n * r : (n + 1) * r, :] for e in range(dp)], 1
                )
        tables = []
        lines = []
        for e in range(dp):
            for n in range(folds):
                spot = slice(e * held + n * per, e * held + (n + 1) * per)
                pos_ref[spot, :] = jnp.concatenate(
                    [
                        early_ref[e, a, b, core, 3 * r : 3 * r + per, :][:, n * narrow : (n + 1) * narrow]
                        for a, b, core in group
                    ],
                    1,
                )
            smalls = [early_ref[e, a, b, core, 3 * r + per :, :].astype(F32) for a, b, core in group]
            tables.append(jnp.concatenate([x[:few, :narrow] for x in smalls], 1))
            lines.extend(x[few : few + 1, : line_ref.shape[1]] for x in smalls)
        vec_ref[...] = jnp.concatenate(tables, 0)
        bias_ref[...] = jnp.concatenate(lines, 1)

    def project(step, carry):
        spot = pl.ds(pl.multiple_of(step * WIN, WIN), WIN)
        low = (act_ref[0, spot, :].astype(F32) + pos_ref[spot, :].astype(F32)).astype(BF16)
        every = nn(low, weight_ref[...])
        q = (every[:, :width] + vec_ref[0:1, :]).astype(BF16)
        q = (q.astype(F32) * 0.125).astype(BF16)
        k = every[:, width : 2 * width].astype(BF16)
        v = (every[:, 2 * width :] + vec_ref[1:2, :]).astype(BF16)
        q_ref[0, spot, :] = q
        k_ref[0, spot, :] = k
        v_ref[0, spot, :] = v
        qt_ref[0, :, spot] = q.T
        kt_ref[0, :, spot] = k.T
        vt_ref[:, spot] = v.T
        return carry

    lax.fori_loop(0, blocks, project, 0)

    @pl.when(row == 0)
    def _():
        late.relay(0)

    @pl.when(row == rows - 1)
    def _():
        for o in range(dp // 2, dp):
            late.relay(o)
        late.near()

    def score(block, head):
        q_head = head_rows(qt_ref[0, pair_of(head), block_of(block)], head % 2)
        return [nn(k_ref[0, spot, pair_of(head)], q_head) for spot in spots_of(block)]

    def soften(block, head, scores):
        scores[0] = causal(scores[0])
        peaks = [jnp.max(x, 0, keepdims=True) for x in scores]
        peak = peaks[0]
        if block:
            peak = jnp.maximum(peak, peaks[1] + apart(lengths_ref, row, block))
        expo = [jnp.exp(scores[0] - peak)]
        if block:
            expo.append(jnp.exp(scores[1] - (peak - apart(lengths_ref, row, block))))
        total = sum(jnp.sum(x, 0, keepdims=True) for x in expo)
        lse_ref[0, head // 2, head % 2 : head % 2 + 1, block_of(block)] = peak + jnp.log(total)
        return [x.astype(BF16) for x in expo], total

    def combine(block, head, soft):
        expo, total = soft
        half = slice(head * HD, (head + 1) * HD)
        out = sum(nn(vt_ref[half, spot], x) for spot, x in zip(spots_of(block), expo))
        ctxt_ref[block % 2, half, :] = (out * (1.0 / total)).astype(BF16)
        if head == H - 1:
            ctx_ref[0, block_of(block), :] = ctxt_ref[block % 2].T

    stages = (score, soften, combine)
    tasks = [(block, head) for block in range(blocks) for head in range(H)]
    quarter = len(tasks) // 4
    staggered(tasks[:quarter], stages)

    @pl.when(row == 0)
    def _():
        for o in range(1, dp // 2):
            late.spread(o)

    staggered(tasks[quarter : 2 * quarter], stages)

    @pl.when(row == 0)
    def _():
        for o in range(dp // 2, dp):
            late.spread(o)

    @pl.when(row == rows - 1)
    def _():
        late.share()

    staggered(tasks[2 * quarter : 3 * quarter], stages)

    @pl.when(row == 0)
    def _():
        for o in range(1, dp // 2):
            late.relay(o)

    staggered(tasks[3 * quarter :], stages)

    @pl.when(row == rows - 1)
    def _():
        late.arrive()
        early.close()
        late.close()


def backward_attention(
    lengths_ref, q_ref, qt_ref, k_ref, kt_ref, v_ref, lse_ref, grad_ref, first_ref, act_ref, pos_ref, weight_ref,
    late_ref, sums_ref, bsum_ref,
    input_ref, late_sum_ref, weight_sum_ref, place_sum_ref,
    lowt_ref, gradt_ref, dqt_ref, dk_ref, dv_ref, every_ref, start_ref, total_ref, wpart_ref, ppart_ref, own_ref,
    own_sem, first_sem, *scratch,
):
    step = pl.program_id(0)
    last = H // 2 - 1
    rows, seq, width = act_ref.shape
    blocks = seq // WIN
    at = Place()
    dp = at.dp
    group = members(at.side)
    r = width // len(group)
    c = width // dp
    narrow = r
    held = seq // dp
    folds = c // narrow
    per = held // folds
    few = sums_ref.shape[0] // dp
    single = bsum_ref.shape[1] // (dp * len(group))
    shared = dp // (H // 2)
    count = Reduce.COUNT
    late = Reduce(late_ref, scratch[:count], at, (own_ref, own_sem))
    weights = Reduce(wpart_ref, scratch[count : 2 * count], at)
    places = Reduce(ppart_ref, scratch[2 * count :], at)
    first_copy = pltpu.make_async_copy(first_ref, start_ref, first_sem)
    pieces = lambda j: [j * shared + n for n in range(shared)]
    nearest = [at.at_dp(n + 1) for n in range(dp)]

    @pl.when(step == 0)
    def _():
        first_copy.start()
        late.own_half().start()
        meet(at)
        for e in nearest:
            late.begin(e)
        total_ref[...] = sums_ref[...]
        for row in range(rows):
            for block in range(blocks):
                spot = block_of(block)
                low = (act_ref[row, spot, :].astype(F32) + pos_ref[spot, :].astype(F32)).astype(BF16)
                lowt_ref[:, row * seq + block * WIN : row * seq + (block + 1) * WIN] = low.T

    for row in range(rows):
        for block in range(blocks):
            gradt_ref[row, :, block_of(block)] = grad_ref[row, block_of(block), :].T

    def score(row, block, head):
        q_head = head_rows(qt_ref[row, :, block_of(block)], head)
        g_head = head_rows(gradt_ref[row, :, block_of(block)], head)
        scores = [nn(k_ref[row, spot, :], q_head) for spot in spots_of(block)]
        return scores, [nn(v_ref[row, spot, :], g_head) for spot in spots_of(block)]

    def soften(row, block, head, products):
        scores, prob_grads = products
        lse = lse_ref[row, 0, head : head + 1, block_of(block)]
        probs = [jnp.exp(causal(scores[0]) - lse)]
        if block:
            probs.append(jnp.exp(scores[1] - (lse - apart(lengths_ref, row, block))))
        inner = sum(jnp.sum(p * g, 0, keepdims=True) for p, g in zip(probs, prob_grads))
        score_grads = [(p * (g - inner)).astype(BF16) for p, g in zip(probs, prob_grads)]
        return [p.astype(BF16) for p in probs], score_grads

    waiting = {}

    def combine(row, block, head, soft):
        half = slice(head * HD, (head + 1) * HD)
        dq = sum(nn(kt_ref[row, half, spot], x) for spot, x in zip(spots_of(block), soft[1]))
        dqt_ref[row, half, block_of(block)] = (dq * 0.125).astype(BF16)
        if head == 0:
            waiting[row, block] = soft
            return
        even = waiting.pop((row, block))
        g = grad_ref[row, block_of(block), :]
        q = q_ref[row, block_of(block), :]
        g_both = jnp.concatenate([head_lanes(g, 0), head_lanes(g, 1)], 0)
        q_both = jnp.concatenate([head_lanes(q, 0), head_lanes(q, 1)], 0)
        for n, spot in enumerate(spots_of(block)):
            dv = nn(jnp.concatenate([even[0][n], soft[0][n]], 1), g_both)
            dk = nn(jnp.concatenate([even[1][n], soft[1][n]], 1), q_both)
            if n == 0:
                dv_ref[row, spot, :] = dv
                dk_ref[row, spot, :] = dk
            else:
                dv_ref[row, spot, :] += dv
                dk_ref[row, spot, :] += dk

    def attend(row):
        staggered([(row, block, head) for block in range(blocks) for head in range(2)], (score, soften, combine))

    for row in range(rows - 1):
        attend(row)

    @pl.when(step == 0)
    def _():
        late.own_half().wait()
        for e in nearest:
            late.across(e)

    @pl.when(step == 2)
    def _():
        for e in nearest:
            late.middle(e)

    @pl.when(step == last)
    def _():
        for e in nearest:
            late.along(e)
        for e in pieces(last - 3):
            weights.along(e)

    @pl.when(step > 0)
    def _():
        for e in pieces(step - 1):
            weights.across(e)

    attend(rows - 1)

    feats = pl.ds(pl.multiple_of(step * PAIR, PAIR), PAIR)
    for row in range(rows):
        for block in range(blocks):
            spot = block_of(block)
            every = [dqt_ref[row, :, spot].T, dk_ref[row, spot, :].astype(BF16), dv_ref[row, spot, :].astype(BF16)]
            every_ref[row * seq + block * WIN : row * seq + (block + 1) * WIN, :] = jnp.concatenate(every, 1)
    total_ref[0:1, feats] = column_sum(every_ref[:, :PAIR])
    total_ref[1:2, feats] = column_sum(every_ref[:, 2 * PAIR :])
    owned = nn(lowt_ref[...], every_ref[...])
    for i, e in enumerate(pieces(step)):
        for f, (a, b, core) in enumerate(group):
            for n in range(3):
                lanes = slice(n * PAIR + i * c, n * PAIR + (i + 1) * c)
                wpart_ref[e, a, b, core, n * r : (n + 1) * r, :] = owned[f * r : (f + 1) * r, lanes].astype(BF16)
        weights.begin(e)

    @pl.when(step > 1)
    def _():
        for e in pieces(step - 2):
            weights.middle(e)

    column = jnp.concatenate(
        [weight_ref[:, pl.ds(pl.multiple_of(n * width + step * PAIR, PAIR), PAIR)] for n in range(3)], 1
    )

    @pl.when(step == 0)
    def _():
        first_copy.wait()

    @pl.when(step < last)
    def _():
        tile = 2 * WIN
        for row in range(rows):
            for n in range(seq // tile):
                spot = slice(n * tile, (n + 1) * tile)
                start_ref[row, spot, :] += nt(every_ref[row * seq + n * tile : row * seq + (n + 1) * tile, :], column)

    @pl.when(step == last)
    def _():
        wide = lambda x: jnp.concatenate([x, jnp.zeros((x.shape[0], c - x.shape[1]), F32)], 1)

        def finish(e):
            total = None
            for row in range(rows):
                spot = slice(e * held, (e + 1) * held)
                grad = start_ref[row, spot, :] + nt(every_ref[row * seq + e * held : row * seq + (e + 1) * held, :], column)
                input_ref[row, spot, :] = grad.astype(BF16)
                total = grad if total is None else total + grad
            total = total.astype(BF16)
            for f, (a, b, core) in enumerate(group):
                lanes = slice(f * narrow, (f + 1) * narrow)
                ppart_ref[e, a, b, core, :per, :] = jnp.concatenate(
                    [total[n * per : (n + 1) * per, lanes] for n in range(folds)], 1
                )
                table = total_ref[e * few : (e + 1) * few, lanes]
                spot = (e * len(group) + f) * single
                line = bsum_ref[:, spot : spot + single]
                filler = jnp.zeros((SMALL - few - 1, c), F32)
                ppart_ref[e, a, b, core, per:, :] = jnp.concatenate([wide(table), wide(line), filler], 0).astype(BF16)
            places.begin(e)

        for n in range(dp + 3):
            if n < dp:
                finish(n)
            if n == 0:
                for e in pieces(last):
                    weights.across(e)
                for e in pieces(last - 1):
                    weights.middle(e)
                for e in pieces(last - 2):
                    weights.along(e)
            if n == 1:
                for e in pieces(last):
                    weights.middle(e)
                for e in pieces(last - 1):
                    weights.along(e)
            if n == 2:
                for e in pieces(last):
                    weights.along(e)
            if n == 3:
                late_sum_ref[...] = late.result()
            if 0 <= n - 1 < dp:
                places.across(n - 1)
            if 0 <= n - 2 < dp:
                places.middle(n - 2)
            if 0 <= n - 3 < dp:
                places.along(n - 3)
        weight_sum_ref[...] = weights.result()
        place_sum_ref[...] = places.result()
        late.close()
        weights.close()
        places.close()


def hand_out(
    late_ref, weight_ref, place_ref, input_ref,
    out_ref, wq_ref, wk_ref, wv_ref, wo_ref, wi_ref, w2_ref, table_ref, placet_ref, line_ref,
):
    @pl.when(pl.program_id(0) >= 0)
    def _():
        out_ref[...] = input_ref[...]

    r, c = wq_ref.shape
    few, narrow = table_ref.shape
    held = placet_ref.shape[1]
    folds = c // narrow
    per = held // folds
    for n, ref in enumerate((wq_ref, wk_ref, wv_ref)):
        ref[...] = weight_ref[n * r : (n + 1) * r, :]
    wide_parts = wi_ref.shape[1] // c
    wo_ref[...] = late_ref[:r, :]
    for n in range(wide_parts):
        wi_ref[:, n * c : (n + 1) * c] = late_ref[(1 + n) * r : (2 + n) * r, :]
    w2_ref[...] = late_ref[(1 + wide_parts) * r :, :]
    place = place_ref[:per, :]
    placet_ref[...] = jnp.concatenate([place[:, n * narrow : (n + 1) * narrow] for n in range(folds)], 0).T
    table_ref[...] = place_ref[per : per + few, :narrow]
    line_ref[...] = place_ref[per + few : per + few + 1, : line_ref.shape[1]]


def feed_forward(
    ctx_ref, act_ref, pos_ref, cot_ref, late_ref, vec_ref, bias_ref,
    out_ref, first_ref, grad_ref, part_ref, sums_ref, bsum_ref,
    wo_acc, wi_acc, w2_acc, slope_ref, wo_ref, wi_ref, w2_ref,
):
    step = pl.program_id(0)
    width = ctx_ref.shape[1]
    dp, side, _, _, _, c = late_ref.shape
    group = members(side)
    r = width // len(group)
    parts = bias_ref.shape[1] // dp // c
    tall = bias_ref.shape[1] // len(group)
    hidden = bias_ref.shape[1]
    part = 512

    @pl.when(step == 0)
    def _():
        wo_acc[...] = jnp.zeros_like(wo_acc)
        wi_acc[...] = jnp.zeros_like(wi_acc)
        w2_acc[...] = jnp.zeros_like(w2_acc)
        sums_ref[...] = jnp.zeros_like(sums_ref)
        bsum_ref[...] = jnp.zeros_like(bsum_ref)
        for f, (a, b, core) in enumerate(group):
            rows = slice(f * r, (f + 1) * r)
            block = lambda e, lo, n: late_ref[e, a, b, core, lo : lo + n, :]
            wo_ref[rows, :] = jnp.concatenate([block(e, 0, r) for e in range(dp)], 1)
            wi_ref[rows, :] = jnp.concatenate([block(e, (1 + n) * r, r) for e in range(dp) for n in range(parts)], 1)
            w2_ref[f * tall : (f + 1) * tall, :] = jnp.concatenate(
                [block(e, (1 + parts) * r, tall) for e in range(dp)], 1
            )

    vec = lambda n: vec_ref[n : n + 1, :]
    ctx = ctx_ref[...]
    first_sum = act_ref[...].astype(F32) + pos_ref[...].astype(F32) + (nn(ctx, wo_ref[...]) + vec(2))
    center = first_sum - jnp.mean(first_sum, -1, keepdims=True)
    scale_one = lax.rsqrt(jnp.mean(center * center, -1, keepdims=True) + 1e-05)
    z_one = center * scale_one
    normed = z_one * vec(3) + vec(4)
    normed_low = normed.astype(BF16)
    branch = None
    acts = []
    C = hidden // part
    cols = [slice(n * part, (n + 1) * part) for n in range(C)]
    pre_next = nn(normed_low, wi_ref[:, cols[0]])
    for n in range(C):
        pre = pre_next + bias_ref[:, cols[n]]
        if n + 1 < C:
            pre_next = nn(normed_low, wi_ref[:, cols[n + 1]])
        if n >= 1:
            term = nn(acts[n - 1], w2_ref[cols[n - 1], :])
            branch = term if branch is None else branch + term
        square = pre * pre
        t = jnp.tanh(pre * (0.7978845608028654 + (0.7978845608028654 * 0.044715) * square))
        half = 0.5 + 0.5 * t
        acts.append((pre * half).astype(BF16))
        slope_ref[:, cols[n]] = half + (0.5 * pre) * (1.0 - t * t) * (
            0.7978845608028654 + (3.0 * 0.7978845608028654 * 0.044715) * square
        )
    term = nn(acts[C - 1], w2_ref[cols[C - 1], :])
    branch = term if branch is None else branch + term
    second_sum = normed + (branch + vec(5))
    center = second_sum - jnp.mean(second_sum, -1, keepdims=True)
    scale_two = lax.rsqrt(jnp.mean(center * center, -1, keepdims=True) + 1e-05)
    z_two = center * scale_two
    out_ref[...] = (z_two * vec(6) + vec(7)).astype(BF16)
    cot = cot_ref[...].astype(F32)
    sums_ref[6:7, :] += column_sum(cot * z_two)
    sums_ref[7:8, :] += column_sum(cot)
    e = cot * vec(6)
    second_grad = scale_two * (
        e - jnp.mean(e, -1, keepdims=True) - z_two * jnp.mean(e * z_two, -1, keepdims=True)
    )
    branch_grad = second_grad.astype(BF16)
    sums_ref[5:6, :] += column_sum(branch_grad)
    branch_t = branch_grad.T
    normed_t = normed_low.T
    normed_grad = second_grad
    grad_next = nt(branch_grad, w2_ref[cols[0], :])
    lows = []

    def weights(n):
        wi_acc[:, cols[n]] += nn(normed_t, lows[n])
        return nt(lows[n], wi_ref[:, cols[n]])

    for n in range(C):
        pre_grad = grad_next * slope_ref[:, cols[n]]
        if n + 1 < C:
            grad_next = nt(branch_grad, w2_ref[cols[n + 1], :])
        w2_acc[:, cols[n]] += nn(branch_t, acts[n])
        if n >= 1:
            normed_grad = normed_grad + weights(n - 1)
        lows.append(pre_grad.astype(BF16))
        bsum_ref[:, cols[n]] += column_sum(lows[n])
    normed_grad = normed_grad + weights(C - 1)
    sums_ref[3:4, :] += column_sum(normed_grad * z_one)
    sums_ref[4:5, :] += column_sum(normed_grad)
    e = normed_grad * vec(3)
    first_grad = scale_one * (
        e - jnp.mean(e, -1, keepdims=True) - z_one * jnp.mean(e * z_one, -1, keepdims=True)
    )
    first_ref[...] = first_grad
    attn_grad = first_grad.astype(BF16)
    sums_ref[2:3, :] += column_sum(attn_grad)
    wo_acc[...] += nn(ctx.T, attn_grad)
    grad_ref[...] = nt(attn_grad, wo_ref[...]).astype(BF16)

    @pl.when(step == pl.num_programs(0) - 1)
    def _():
        for e in range(dp):
            lanes = slice(e * c, (e + 1) * c)
            for f, (a, b, core) in enumerate(group):
                rows = slice(f * r, (f + 1) * r)
                part_ref[e, a, b, core, :r, :] = wo_acc[rows, lanes].astype(BF16)
                for n in range(parts):
                    wide = slice((e * parts + n) * c, (e * parts + n + 1) * c)
                    part_ref[e, a, b, core, (1 + n) * r : (2 + n) * r, :] = wi_acc[rows, wide].astype(BF16)
                turned = w2_acc[lanes, f * tall : (f + 1) * tall].astype(BF16)
                part_ref[e, a, b, core, (1 + parts) * r :, :] = turned.T


def whole(shape):
    return pl.BlockSpec(shape, lambda *_: (0,) * len(shape))


def once(shape):
    return pl.BlockSpec(shape, lambda *_: (0,) * len(shape), pipeline_mode=pl.Buffered(1))


def run_forward(lengths, act, wq, wk, wv, wo, wi, w2, table, place, line):
    rows, seq, width = act.shape
    dp, side = lax.axis_size("dp"), side_of(lax.axis_size("fsdp"))
    r, c = wq.shape
    hidden = wi.shape[1] * dp
    first_rows = 3 * r + place.shape[0] * place.shape[1] // c + SMALL
    late_rows = r + r * wi.shape[1] // c + w2.shape[0]
    row3 = lambda shape: pl.BlockSpec((1,) + shape, lambda i: (i,) + (0,) * len(shape))
    seqs = row3((seq, width))
    turned = row3((width, seq))
    st, tt = jax.ShapeDtypeStruct((rows, seq, width), BF16), jax.ShapeDtypeStruct((rows, width, seq), BF16)
    small = [x.shape for x in (wq, wk, wv, wo, wi, w2, table, place, line)]
    return pl.pallas_call(
        forward_attention,
        grid=(rows,),
        in_specs=[pl.BlockSpec(memory_space=pltpu.SMEM), seqs] + [whole(x) for x in small],
        out_specs=[seqs, turned, seqs, turned, seqs, seqs, row3((H // 2, 2, seq)), whole((width, 3 * width)),
                   whole((seq, width)), whole((table.shape[0] * dp, width)), whole((1, hidden)),
                   pl.BlockSpec(memory_space=pl.ANY)],
        scratch_shapes=[
            pltpu.VMEM((width, seq), BF16),
            pltpu.VMEM((2, width, WIN), BF16),
            pltpu.VMEM((dp, side, side, 2, first_rows, c), BF16),
            pltpu.VMEM((late_rows, c), BF16),
            pltpu.SemaphoreType.DMA,
        ]
        + Gather.semaphores(dp, side) * 2,
        out_shape=[
            st, tt, st, tt, st, st, jax.ShapeDtypeStruct((rows, H // 2, 2, seq), F32),
            jax.ShapeDtypeStruct((width, 3 * width), BF16),
            jax.ShapeDtypeStruct((seq, width), BF16),
            jax.ShapeDtypeStruct((table.shape[0] * dp, width), F32),
            jax.ShapeDtypeStruct((1, hidden), F32),
            jax.ShapeDtypeStruct((dp, side, side, 2, late_rows, c), BF16),
        ],
        compiler_params=pltpu.CompilerParams(
            vmem_limit_bytes=VMEM_LIMIT, collective_id=0, has_side_effects=True
        ),
        name="forward_attention",
    )(lengths, act, wq, wk, wv, wo, wi, w2, table, place, line)


def run_backward(lengths, q, qt, k, kt, v, lse, grad, first, act, pos, weight, late, sums, bsum):
    rows, seq, width = act.shape
    dp, side = late.shape[:2]
    late_rows, c = late.shape[4:]
    r = width // (2 * side * side)
    weight_rows = 3 * r
    place_rows = (seq // dp) * r // c + SMALL
    lanes = pl.BlockSpec((rows, seq, PAIR), lambda j: (0, 0, j))
    turned = pl.BlockSpec((rows, PAIR, seq), lambda j: (0, j, 0))
    anywhere = pl.BlockSpec(memory_space=pl.ANY)
    totals = [(n, c) for n in (late_rows, weight_rows, place_rows)]
    return pl.pallas_call(
        backward_attention,
        grid=(H // 2,),
        in_specs=[pl.BlockSpec(memory_space=pltpu.SMEM), lanes, turned, lanes, turned, lanes,
                  pl.BlockSpec((rows, 1, 2, seq), lambda j: (0, j, 0, 0)), lanes, anywhere, once(act.shape),
                  once(pos.shape), once(weight.shape), anywhere, once(sums.shape), once(bsum.shape)],
        out_specs=[whole(act.shape)] + [whole(x) for x in totals],
        scratch_shapes=[
            pltpu.VMEM((width, rows * seq), BF16),
            pltpu.VMEM((rows, PAIR, seq), BF16),
            pltpu.VMEM((rows, PAIR, seq), BF16),
            pltpu.VMEM((rows, seq, PAIR), F32),
            pltpu.VMEM((rows, seq, PAIR), F32),
            pltpu.VMEM((rows * seq, 3 * PAIR), BF16),
            pltpu.VMEM((rows, seq, width), F32),
            pltpu.VMEM(sums.shape, F32),
            pltpu.VMEM((dp, side, side, 2, weight_rows, c), BF16),
            pltpu.VMEM((dp, side, side, 2, place_rows, c), BF16),
            pltpu.VMEM((dp, side, side, late_rows, c), BF16),
            pltpu.SemaphoreType.DMA,
            pltpu.SemaphoreType.DMA,
        ]
        + Reduce.scratch(dp, side, late_rows, c)
        + Reduce.scratch(dp, side, weight_rows, c)
        + Reduce.scratch(dp, side, place_rows, c),
        out_shape=[jax.ShapeDtypeStruct(act.shape, BF16)] + [jax.ShapeDtypeStruct(x, F32) for x in totals],
        compiler_params=pltpu.CompilerParams(
            vmem_limit_bytes=VMEM_LIMIT, collective_id=1, has_side_effects=True
        ),
        name="backward_attention",
    )(lengths, q, qt, k, kt, v, lse, grad, first, act, pos, weight, late, sums, bsum)


def run_hand_out(late, weight, place, grad, shapes):
    steps = 4
    block = pl.BlockSpec((1, grad.shape[0] * grad.shape[1] // steps, grad.shape[2]), lambda i: (i, 0, 0))
    rows = grad.reshape(steps, -1, grad.shape[2])
    return pl.pallas_call(
        hand_out,
        grid=(steps,),
        in_specs=[whole(x.shape) for x in (late, weight, place)] + [block],
        out_specs=[block] + [whole(x) for x in shapes],
        out_shape=[jax.ShapeDtypeStruct(rows.shape, BF16)] + [jax.ShapeDtypeStruct(x, F32) for x in shapes],
        name="hand_out",
    )(late, weight, place, rows)


def run_feed_forward(ctx, act, pos, cot, late, vec, bias, tile=512):
    tokens, width = ctx.shape
    seq = pos.shape[0]
    hidden = bias.shape[1]
    per_row = seq // tile
    tok = pl.BlockSpec((tile, width), lambda t: (t, 0))
    return pl.pallas_call(
        feed_forward,
        grid=(tokens // tile,),
        in_specs=[tok, tok, pl.BlockSpec((tile, width), lambda t: (t % per_row, 0)), tok,
                  once(late.shape), whole(vec.shape), whole(bias.shape)],
        out_specs=[tok, tok, tok, whole(late.shape), whole((8, width)), whole((1, hidden))],
        scratch_shapes=[
            pltpu.VMEM((width, width), F32),
            pltpu.VMEM((width, hidden), F32),
            pltpu.VMEM((width, hidden), F32),
            pltpu.VMEM((tile, hidden), F32),
            pltpu.VMEM((width, width), BF16),
            pltpu.VMEM((width, hidden), BF16),
            pltpu.VMEM((hidden, width), BF16),
        ],
        out_shape=[
            jax.ShapeDtypeStruct((tokens, width), BF16),
            jax.ShapeDtypeStruct((tokens, width), F32),
            jax.ShapeDtypeStruct((tokens, width), BF16),
            jax.ShapeDtypeStruct(late.shape, BF16),
            jax.ShapeDtypeStruct((8, width), F32),
            jax.ShapeDtypeStruct((1, hidden), F32),
        ],
        compiler_params=pltpu.CompilerParams(vmem_limit_bytes=VMEM_LIMIT),
        name="feed_forward",
    )(ctx, act, pos, cot, late, vec, bias)


def shards(
    activations, window_lengths, query_weight, key_weight, value_weight, output_weight, inner_weight, outer_weight,
    vectors, positions, inner_bias, output_cotangent,
):
    rows, seq, width = activations.shape
    q, qt, k, kt, v, ctx, lse, weight, pos, vec, bias, late = run_forward(
        window_lengths, activations, query_weight, key_weight, value_weight, output_weight, inner_weight, outer_weight,
        vectors, positions.T, inner_bias.reshape(1, -1),
    )
    flat = lambda x: x.reshape(rows * seq, width)
    deep = lambda x: x.reshape(rows, seq, width)
    out, first, grad, part, sums, bsum = run_feed_forward(
        flat(ctx), flat(activations), pos, flat(output_cotangent), late, vec, bias
    )
    input_grad, *sums = run_backward(
        window_lengths, q, qt, k, kt, v, lse, deep(grad), deep(first), activations, pos, weight, part, sums, bsum
    )
    shapes = [x.shape for x in (query_weight, key_weight, value_weight, output_weight, inner_weight, outer_weight,
                                vectors, positions.T)] + [(1, inner_bias.shape[0])]
    owned = run_hand_out(*sums, input_grad, shapes)
    return (deep(out), owned[0].reshape(input_grad.shape)) + tuple(owned[1:8]) + (owned[8].T, owned[9].reshape(-1))


def solution(mesh):
    tokens = P(("dp", "fsdp"), None, None)
    matrix = P("fsdp", "dp")
    table = P("dp", "fsdp")
    line = P(("dp", "fsdp"))
    return jax.shard_map(
        shards,
        mesh=mesh,
        in_specs=(tokens, P(("dp", "fsdp"), None)) + (matrix,) * 6 + (table, table, line, tokens),
        out_specs=(tokens, tokens) + (matrix,) * 6 + (table, table, line),
        check_vma=False,
    )
```

time: 1130 us -> 170 us (0.15)
  waiting for transfers between devices: 861 us -> 0 us
  blocking collectives: 40.9 us -> 0 us
  local copies, waits for them, and re-layouts: 27.3 us -> 0 us
  between operations: 14.3 us -> 0.84 us
    reduce_scatter x7 -> x0, waiting for transfers between devices: 861 us -> none  [scatter(): lax.psum_scatter(x, both, scatter_dimension=0, tiled=True)[0].astype(F32)]
    unnamed x1 -> x0, blocking collectives: 40.9 us -> none
    pallas_call x1 -> x2, Pallas kernels: 49.5 us -> 69 us  [the longest x1 64.9 us: run_backward(): pl.pallas_call(backward_attention, grid=(H // 2,), in_specs=[pl.BlockSpec...]
    pallas_call x1, Pallas kernels: 69.6 us -> 53.4 us  [run_forward(): pl.pallas_call(forward_attention, grid=(rows,), in_specs=[pl.BlockSpec(me...]
    transpose x8 -> x0, local copies, waits for them, and re-layouts: 11.9 us -> none  [the longest x6 8.54 us: split_columns(): x.reshape(fsdp, r, dp, c).transpose(2, 0, 1, 3).reshape(dp * fsdp, r, c)]
  transfers between devices with their start and end apart: 7 -> 0, of which waited for: 7 -> 0; matrix products, arithmetic and copies ran while one was open for 3% -> 0% of each run, Pallas kernels for 0% -> 0%
where the time goes in v3:
time: 170 us
  Pallas kernels  169 us (99%)
    pallas_call x1, Pallas kernels, run_backward(): pl.pallas_call(backward_attention, grid=(H // 2,), in_specs=[pl.BlockSpec...  64.9 us
    pallas_call x1, Pallas kernels, run_forward(): pl.pallas_call(forward_attention, grid=(rows,), in_specs=[pl.BlockSpec(me...  53.4 us
    pallas_call x1, Pallas kernels, run_feed_forward(): pl.pallas_call(feed_forward, grid=(tokens // tile,), in_specs=[tok, tok,...  46.9 us
    pallas_call x1, Pallas kernels, run_hand_out(): pl.pallas_call(hand_out, grid=(steps,), in_specs=[whole(x.shape) for x in...  4.08 us

profile of v3, /device:TPU:0, one launch (start us, length us, event | category | flops | bytes accessed | tf_op | source)
XLA Modules:
  0.0 170.1 jit_solution(11043212054767525706)
XLA Ops:
  0.6 53.4 %forward_attention.1 = (bf16[2,1024,512]{2,1,0:T(8,128)(2,1)}, bf16[2,512,1024]{2,1,0:T(8,128)(2,1)}, bf16[2,1024,512]{2,1,0:T(8,128)(2,1)}, bf16[2,512,1024]{2,...) custom-call(s32[2,4]{1,0:T(2,128)} %lengths_ref.3, ...), custom_call_target="tpu_custom_call" | custom-call | tf_op jit(solution)/shard_map/forward_attention/pallas_call | solution.py:886
  54.1 46.9 %feed_forward.1 = (bf16[2048,512]{1,0:T(8,128)(2,1)}, f32[2048,512]{1,0:T(8,128)}, bf16[2048,512]{1,0:T(8,128)(2,1)}, bf16[4,2,2,2,576,128]{5,4,3,2,1,0:T(8,128)...) custom-call(bf16[2048,512]{1,0:T(8,128)(2,1)} %bitcast.15, bf16[2048,512]{1,0:T(8,128)(2,1)} %bitcast.12, ...), custom_call_target="tpu_custom_call" | custom-call | tf_op jit(solution)/shard_map/feed_forward/pallas_call | solution.py:980
  101.0 64.9 %backward_attention.1 = (bf16[2,1024,512]{2,1,0:T(8,128)(2,1)}, f32[576,128]{1,0:T(8,128)}, f32[192,128]{1,0:T(8,128)}, f32[144,128]{1,0:T(8,128)}) custom-call(s32[2,4]{1,0:T(2,128)} %lengths_ref.3, bf16[2,1024,512]{2,1,0:T(8,128)(2,1)} %get-tuple-element.49.q_ref, bf16[2,512,1024]{2,1,0:T(8,128)(2,1)} %get-tuple-element.50.qt_ref, ...), custom_call_target="tpu_custom_call" | custom-call | tf_op jit(solution)/shard_map/backward_attention/pallas_call | solution.py:927
  165.9 4.1 %hand_out.1 = (bf16[4,512,512]{2,1,0:T(8,128)(2,1)}, f32[64,128]{1,0:T(8,128)}, f32[64,128]{1,0:T(8,128)}, f32[64,128]{1,0:T(8,128)}, f32[64,128]{1,0:T(8,128)},...) custom-call(f32[576,128]{1,0:T(8,128)} %get-tuple-element.61.late_ref, ...), custom_call_target="tpu_custom_call" | custom-call | tf_op jit(solution)/shard_map/hand_out/pallas_call | solution.py:964

commit v4 on v3

--- a/solution.py
+++ b/solution.py
@@ -124,7 +124,7 @@
     )
 
 
-def meet(at):
+def greet(at):
     barrier = pltpu.get_barrier_semaphore()
     others = [{"dp": at.at_dp(n)} for n in range(1, at.dp)]
     others += [at.device(at.a, at.at_b(n)) for n in range(1, at.side)]
@@ -132,7 +132,11 @@
     others.append(at.sibling())
     for other in others:
         pl.semaphore_signal(barrier, inc=1, device_id=other, device_id_type=MESH)
-    pl.semaphore_wait(barrier, len(others))
+    return len(others)
+
+
+def meet(count):
+    pl.semaphore_wait(pltpu.get_barrier_semaphore(), count)
 
 
 class Gather:
@@ -171,11 +175,12 @@
     def begin(self):
         for o in range(1, self.at.dp):
             self.along_dp(o).start()
-        self.pass_on(0)
 
     def pass_on(self, o):
         for p in range(1, self.at.side):
             self.along_b(o, p).start()
+
+    def far(self, o):
         for q in range(1, self.at.side):
             self.along_a(o, 0, q).start()
 
@@ -337,7 +342,8 @@
 
 def forward_attention(
     lengths_ref, act_ref, wq_ref, wk_ref, wv_ref, wo_ref, wi_ref, w2_ref, table_ref, place_ref, line_ref,
-    q_ref, qt_ref, k_ref, kt_ref, v_ref, ctx_ref, lse_ref, weight_ref, pos_ref, vec_ref, bias_ref, late_ref,
+    q_out, qt_out, k_out, kt_out, v_out, lowt_out, ctx_ref, lse_ref, weight_out, pos_out, vec_ref, bias_ref, late_ref,
+    q_ref, qt_ref, k_ref, kt_ref, v_ref, lowt_ref, weight_ref, pos_ref, out_sems,
     vt_ref, ctxt_ref, early_ref, own_ref, own_sem, *sems,
 ):
     row = pl.program_id(0)
@@ -357,8 +363,20 @@
     def own_copy():
         return pltpu.make_async_copy(own_ref, late_ref.at[here], own_sem)
 
+    def row_copies(of_row):
+        pairs = ((q_ref, q_out), (qt_ref, qt_out), (k_ref, k_out), (kt_ref, kt_out), (v_ref, v_out),
+                 (lowt_ref, lowt_out))
+        return [
+            pltpu.make_async_copy(src.at[0], dst.at[of_row], out_sems.at[n]) for n, (src, dst) in enumerate(pairs)
+        ]
+
+    def table_copies():
+        pairs = ((weight_ref, weight_out), (pos_ref, pos_out))
+        return [pltpu.make_async_copy(src, dst, out_sems.at[6 + n]) for n, (src, dst) in enumerate(pairs)]
+
     @pl.when(row == 0)
     def _():
+        count = greet(at)
         for n, ref in enumerate((wq_ref, wk_ref, wv_ref)):
             early_ref[here + (slice(n * r, (n + 1) * r),)] = ref[...]
         place = place_ref[...].T
@@ -377,17 +395,25 @@
             own_ref[(1 + n) * r : (2 + n) * r, :] = wi_ref[:, n * c : (n + 1) * c]
         own_ref[(1 + wide_parts) * r :, :] = w2_ref[...]
         own_copy().start()
-        meet(at)
+        meet(count)
         early.begin()
+        early.pass_on(0)
+        early.far(0)
         early.relay(0)
         for o in range(1, dp):
             early.spread(o)
+        own_copy().wait()
+        late.begin()
         for o in range(1, dp):
             early.relay(o)
+            early.far(o)
         early.near()
-        own_copy().wait()
-        late.begin()
+        late.pass_on(0)
+        late.far(0)
         early.share()
+        late.relay(0)
+        late.spread(1)
+        late.far(1)
         early.arrive()
         group = members(at.side)
         for f, (a, b, core) in enumerate(group):
@@ -412,10 +438,18 @@
             lines.extend(x[few : few + 1, : line_ref.shape[1]] for x in smalls)
         vec_ref[...] = jnp.concatenate(tables, 0)
         bias_ref[...] = jnp.concatenate(lines, 1)
+        for copy in table_copies():
+            copy.start()
+
+    @pl.when(row > 0)
+    def _():
+        for copy in row_copies(row - 1):
+            copy.wait()
 
     def project(step, carry):
         spot = pl.ds(pl.multiple_of(step * WIN, WIN), WIN)
         low = (act_ref[0, spot, :].astype(F32) + pos_ref[spot, :].astype(F32)).astype(BF16)
+        lowt_ref[0, :, spot] = low.T
         every = nn(low, weight_ref[...])
         q = (every[:, :width] + vec_ref[0:1, :]).astype(BF16)
         q = (q.astype(F32) * 0.125).astype(BF16)
@@ -430,16 +464,15 @@
         return carry
 
     lax.fori_loop(0, blocks, project, 0)
+    for copy in row_copies(row):
+        copy.start()
 
     @pl.when(row == 0)
     def _():
-        late.relay(0)
-
-    @pl.when(row == rows - 1)
-    def _():
-        for o in range(dp // 2, dp):
-            late.relay(o)
-        late.near()
+        for o in range(2, dp // 2 + 1):
+            late.spread(o)
+            late.far(o)
+        late.relay(1)
 
     def score(block, head):
         q_head = head_rows(qt_ref[0, pair_of(head), block_of(block)], head % 2)
@@ -473,46 +506,47 @@
 
     @pl.when(row == 0)
     def _():
-        for o in range(1, dp // 2):
+        for o in range(dp // 2 + 1, dp):
             late.spread(o)
+            late.far(o)
 
     staggered(tasks[quarter : 2 * quarter], stages)
 
     @pl.when(row == 0)
     def _():
-        for o in range(dp // 2, dp):
-            late.spread(o)
+        for o in range(2, dp - 1):
+            late.relay(o)
 
     @pl.when(row == rows - 1)
     def _():
         late.share()
 
-    staggered(tasks[2 * quarter : 3 * quarter], stages)
+    staggered(tasks[2 * quarter :], stages)
 
     @pl.when(row == 0)
     def _():
-        for o in range(1, dp // 2):
-            late.relay(o)
-
-    staggered(tasks[3 * quarter :], stages)
+        late.relay(dp - 1)
+        late.near()
 
     @pl.when(row == rows - 1)
     def _():
         late.arrive()
         early.close()
         late.close()
+        for copy in row_copies(row) + table_copies():
+            copy.wait()
 
 
 def backward_attention(
-    lengths_ref, q_ref, qt_ref, k_ref, kt_ref, v_ref, lse_ref, grad_ref, first_ref, act_ref, pos_ref, weight_ref,
+    lengths_ref, q_ref, qt_ref, k_ref, kt_ref, v_ref, lse_ref, grad_ref, first_ref, lowt_in, weight_in,
     late_ref, sums_ref, bsum_ref,
-    input_ref, late_sum_ref, weight_sum_ref, place_sum_ref,
-    lowt_ref, gradt_ref, dqt_ref, dk_ref, dv_ref, every_ref, start_ref, total_ref, wpart_ref, ppart_ref, own_ref,
+    input_out, late_sum_ref, weight_sum_ref, place_sum_ref,
+    weight_ref, input_ref, load_sems, input_sems, lowt_ref, gradt_ref, dqt_ref, dk_ref, dv_ref, every_ref, start_ref, total_ref, wpart_ref, ppart_ref, own_ref,
     own_sem, first_sem, *scratch,
 ):
     step = pl.program_id(0)
     last = H // 2 - 1
-    rows, seq, width = act_ref.shape
+    rows, width, seq = lowt_in.shape
     blocks = seq // WIN
     at = Place()
     dp = at.dp
@@ -531,26 +565,37 @@
     weights = Reduce(wpart_ref, scratch[count : 2 * count], at)
     places = Reduce(ppart_ref, scratch[2 * count :], at)
     first_copy = pltpu.make_async_copy(first_ref, start_ref, first_sem)
+    loads = [
+        pltpu.make_async_copy(lowt_in.at[row], lowt_ref.at[:, row * seq : (row + 1) * seq], load_sems.at[row])
+        for row in range(rows)
+    ]
+    loads.append(pltpu.make_async_copy(weight_in, weight_ref, load_sems.at[rows]))
+    arriving = loads + [first_copy]
+
+    def input_copy(e):
+        spot = (slice(None), slice(e * held, (e + 1) * held))
+        return pltpu.make_async_copy(input_ref.at[spot], input_out.at[spot], input_sems.at[e])
+
     pieces = lambda j: [j * shared + n for n in range(shared)]
     nearest = [at.at_dp(n + 1) for n in range(dp)]
 
     @pl.when(step == 0)
     def _():
-        first_copy.start()
+        greet(at)
+        for load in arriving:
+            load.start()
         late.own_half().start()
-        meet(at)
-        for e in nearest:
-            late.begin(e)
         total_ref[...] = sums_ref[...]
-        for row in range(rows):
-            for block in range(blocks):
-                spot = block_of(block)
-                low = (act_ref[row, spot, :].astype(F32) + pos_ref[spot, :].astype(F32)).astype(BF16)
-                lowt_ref[:, row * seq + block * WIN : row * seq + (block + 1) * WIN] = low.T
 
     for row in range(rows):
         for block in range(blocks):
             gradt_ref[row, :, block_of(block)] = grad_ref[row, block_of(block), :].T
+
+    @pl.when(step == 0)
+    def _():
+        meet(dp + 2 * at.side - 2)
+        for e in nearest:
+            late.begin(e)
 
     def score(row, block, head):
         q_head = head_rows(qt_ref[row, :, block_of(block)], head)
@@ -585,90 +630,114 @@
         for n, spot in enumerate(spots_of(block)):
             dv = nn(jnp.concatenate([even[0][n], soft[0][n]], 1), g_both)
             dk = nn(jnp.concatenate([even[1][n], soft[1][n]], 1), q_both)
-            if n == 0:
+            if n or block == blocks - 1:
                 dv_ref[row, spot, :] = dv
                 dk_ref[row, spot, :] = dk
             else:
                 dv_ref[row, spot, :] += dv
                 dk_ref[row, spot, :] += dk
 
-    def attend(row):
-        staggered([(row, block, head) for block in range(blocks) for head in range(2)], (score, soften, combine))
-
-    for row in range(rows - 1):
-        attend(row)
-
-    @pl.when(step == 0)
-    def _():
-        late.own_half().wait()
-        for e in nearest:
-            late.across(e)
-
-    @pl.when(step == 2)
-    def _():
-        for e in nearest:
-            late.middle(e)
-
-    @pl.when(step == last)
-    def _():
-        for e in nearest:
-            late.along(e)
-        for e in pieces(last - 3):
-            weights.along(e)
-
-    @pl.when(step > 0)
-    def _():
-        for e in pieces(step - 1):
-            weights.across(e)
-
-    attend(rows - 1)
-
+    def attend(*chosen):
+        tasks = [(row, block, head) for block in chosen for row in range(rows) for head in range(2)]
+        staggered(tasks, (score, soften, combine))
+        for row in range(rows):
+            for block in chosen:
+                spot = block_of(block)
+                every = [dqt_ref[row, :, spot].T, dk_ref[row, spot, :].astype(BF16), dv_ref[row, spot, :].astype(BF16)]
+                every_ref[row * seq + block * WIN : row * seq + (block + 1) * WIN, :] = jnp.concatenate(every, 1)
+
+    half = dp // 2
+    downward = list(range(blocks))[::-1]
     feats = pl.ds(pl.multiple_of(step * PAIR, PAIR), PAIR)
-    for row in range(rows):
-        for block in range(blocks):
-            spot = block_of(block)
-            every = [dqt_ref[row, :, spot].T, dk_ref[row, spot, :].astype(BF16), dv_ref[row, spot, :].astype(BF16)]
-            every_ref[row * seq + block * WIN : row * seq + (block + 1) * WIN, :] = jnp.concatenate(every, 1)
-    total_ref[0:1, feats] = column_sum(every_ref[:, :PAIR])
-    total_ref[1:2, feats] = column_sum(every_ref[:, 2 * PAIR :])
-    owned = nn(lowt_ref[...], every_ref[...])
-    for i, e in enumerate(pieces(step)):
-        for f, (a, b, core) in enumerate(group):
-            for n in range(3):
-                lanes = slice(n * PAIR + i * c, n * PAIR + (i + 1) * c)
-                wpart_ref[e, a, b, core, n * r : (n + 1) * r, :] = owned[f * r : (f + 1) * r, lanes].astype(BF16)
-        weights.begin(e)
-
-    @pl.when(step > 1)
-    def _():
-        for e in pieces(step - 2):
-            weights.middle(e)
-
-    column = jnp.concatenate(
-        [weight_ref[:, pl.ds(pl.multiple_of(n * width + step * PAIR, PAIR), PAIR)] for n in range(3)], 1
-    )
-
-    @pl.when(step == 0)
-    def _():
-        first_copy.wait()
+
+    def sum_tokens():
+        total_ref[0:1, feats] = column_sum(every_ref[:, :PAIR])
+        total_ref[1:2, feats] = column_sum(every_ref[:, 2 * PAIR :])
+
+    def send_weights():
+        owned = nn(lowt_ref[...], every_ref[...])
+        for i, e in enumerate(pieces(step)):
+            for f, (a, b, core) in enumerate(group):
+                for n in range(3):
+                    lanes = slice(n * PAIR + i * c, n * PAIR + (i + 1) * c)
+                    wpart_ref[e, a, b, core, n * r : (n + 1) * r, :] = owned[f * r : (f + 1) * r, lanes].astype(BF16)
+            weights.begin(e)
+
+    def column():
+        return jnp.concatenate(
+            [weight_ref[:, pl.ds(pl.multiple_of(n * width + step * PAIR, PAIR), PAIR)] for n in range(3)], 1
+        )
+
+    def weights_on():
+        @pl.when(step > 0)
+        def _():
+            for e in pieces(step - 1):
+                weights.across(e)
 
     @pl.when(step < last)
     def _():
+        attend(*downward[: blocks // 2])
+
+        @pl.when(step == 0)
+        def _():
+            late.own_half().wait()
+            for e in nearest:
+                late.across(e)
+
+        @pl.when(step == 1)
+        def _():
+            for e in nearest[: half // 2]:
+                late.middle(e)
+
+        @pl.when(step == 2)
+        def _():
+            for e in nearest[half : half + half // 2]:
+                late.middle(e)
+            for e in nearest[: half // 2]:
+                late.along(e)
+
+        weights_on()
+        attend(*downward[blocks // 2 :])
+
+        @pl.when(step == 0)
+        def _():
+            for load in arriving:
+                load.wait()
+
+        sum_tokens()
+        send_weights()
+
+        @pl.when(step == 1)
+        def _():
+            for e in nearest[half // 2 : half]:
+                late.middle(e)
+
+        @pl.when(step == 2)
+        def _():
+            for e in nearest[half + half // 2 :]:
+                late.middle(e)
+            for e in nearest[half // 2 : half]:
+                late.along(e)
+            for e in pieces(0):
+                weights.middle(e)
+
         tile = 2 * WIN
+        turned = column()
         for row in range(rows):
             for n in range(seq // tile):
                 spot = slice(n * tile, (n + 1) * tile)
-                start_ref[row, spot, :] += nt(every_ref[row * seq + n * tile : row * seq + (n + 1) * tile, :], column)
+                start_ref[row, spot, :] += nt(every_ref[row * seq + n * tile : row * seq + (n + 1) * tile, :], turned)
 
     @pl.when(step == last)
     def _():
         wide = lambda x: jnp.concatenate([x, jnp.zeros((x.shape[0], c - x.shape[1]), F32)], 1)
+        turned = column()
 
         def finish(e):
             total = None
             for row in range(rows):
                 spot = slice(e * held, (e + 1) * held)
-                grad = start_ref[row, spot, :] + nt(every_ref[row * seq + e * held : row * seq + (e + 1) * held, :], column)
+                grad = start_ref[row, spot, :] + nt(every_ref[row * seq + e * held : row * seq + (e + 1) * held, :], turned)
                 input_ref[row, spot, :] = grad.astype(BF16)
                 total = grad if total is None else total + grad
             total = total.astype(BF16)
@@ -683,48 +752,72 @@
                 filler = jnp.zeros((SMALL - few - 1, c), F32)
                 ppart_ref[e, a, b, core, per:, :] = jnp.concatenate([wide(table), wide(line), filler], 0).astype(BF16)
             places.begin(e)
-
-        for n in range(dp + 3):
-            if n < dp:
-                finish(n)
-            if n == 0:
-                for e in pieces(last):
-                    weights.across(e)
-                for e in pieces(last - 1):
-                    weights.middle(e)
-                for e in pieces(last - 2):
-                    weights.along(e)
-            if n == 1:
-                for e in pieces(last):
-                    weights.middle(e)
-                for e in pieces(last - 1):
-                    weights.along(e)
-            if n == 2:
-                for e in pieces(last):
-                    weights.along(e)
-            if n == 3:
-                late_sum_ref[...] = late.result()
-            if 0 <= n - 1 < dp:
-                places.across(n - 1)
-            if 0 <= n - 2 < dp:
-                places.middle(n - 2)
-            if 0 <= n - 3 < dp:
-                places.along(n - 3)
+            input_copy(e).start()
+
+        def places_of(block):
+            return [e for e in range(dp) if e * held // WIN == block]
+
+        def on(step_of, *chosen):
+            for block in chosen:
+                for e in places_of(block):
+                    step_of(e)
+
+        attend(*downward[: blocks // 2])
+        for e in nearest[half:]:
+            late.along(e)
+        weights_on()
+        on(finish, *downward[: blocks // 2])
+        attend(*downward[blocks // 2 : -1])
+        on(finish, *downward[blocks // 2 : -1])
+        for e in pieces(last - 2):
+            weights.middle(e)
+        for e in pieces(last - 3):
+            weights.along(e)
+        on(places.across, *downward[: blocks // 2])
+        attend(downward[-1])
+        sum_tokens()
+        on(finish, downward[-1])
+        on(places.across, *downward[blocks // 2 : -1])
+        send_weights()
+        for e in pieces(last - 1):
+            weights.middle(e)
+        on(places.middle, *downward[: blocks // 2])
+        on(places.across, downward[-1])
+        for e in pieces(last):
+            weights.across(e)
+        on(places.middle, *downward[blocks // 2 : -1])
+        on(places.along, *downward[: blocks // 2])
+        for e in pieces(last - 2) + pieces(last - 1):
+            weights.along(e)
+        on(places.middle, downward[-1])
+        on(places.along, *downward[blocks // 2 : -1])
+        for e in pieces(last):
+            weights.middle(e)
+        late_sum_ref[...] = late.result()
+        on(places.along, downward[-1])
+        for e in pieces(last):
+            weights.along(e)
+        place_sum_ref[...] = places.result()
         weight_sum_ref[...] = weights.result()
-        place_sum_ref[...] = places.result()
         late.close()
         weights.close()
         places.close()
+        for e in range(dp):
+            input_copy(e).wait()
 
 
 def hand_out(
     late_ref, weight_ref, place_ref, input_ref,
     out_ref, wq_ref, wk_ref, wv_ref, wo_ref, wi_ref, w2_ref, table_ref, placet_ref, line_ref,
+    held_ref, in_sems, out_sems,
 ):
-    @pl.when(pl.program_id(0) >= 0)
-    def _():
-        out_ref[...] = input_ref[...]
-
+    pieces = in_sems.shape[0]
+    some = input_ref.shape[0] // pieces
+    spots = [slice(n * some, (n + 1) * some) for n in range(pieces)]
+    loads = [pltpu.make_async_copy(input_ref.at[x], held_ref.at[x], in_sems.at[n]) for n, x in enumerate(spots)]
+    stores = [pltpu.make_async_copy(held_ref.at[x], out_ref.at[x], out_sems.at[n]) for n, x in enumerate(spots)]
+    for load in loads:
+        load.start()
     r, c = wq_ref.shape
     few, narrow = table_ref.shape
     held = placet_ref.shape[1]
@@ -741,12 +834,17 @@
     placet_ref[...] = jnp.concatenate([place[:, n * narrow : (n + 1) * narrow] for n in range(folds)], 0).T
     table_ref[...] = place_ref[per : per + few, :narrow]
     line_ref[...] = place_ref[per + few : per + few + 1, : line_ref.shape[1]]
+    for load, store in zip(loads, stores):
+        load.wait()
+        store.start()
+    for store in stores:
+        store.wait()
 
 
 def feed_forward(
     ctx_ref, act_ref, pos_ref, cot_ref, late_ref, vec_ref, bias_ref,
-    out_ref, first_ref, grad_ref, part_ref, sums_ref, bsum_ref,
-    wo_acc, wi_acc, w2_acc, slope_ref, wo_ref, wi_ref, w2_ref,
+    out_ref, first_ref, grad_ref, part_out, sums_ref, bsum_ref,
+    wo_acc, wi_acc, w2_acc, slope_ref, wo_ref, wi_ref, w2_ref, part_ref, sems,
 ):
     step = pl.program_id(0)
     width = ctx_ref.shape[1]
@@ -755,23 +853,41 @@
     r = width // len(group)
     parts = bias_ref.shape[1] // dp // c
     tall = bias_ref.shape[1] // len(group)
+    spans = [slice(0, r), slice(r, (1 + parts) * r), slice((1 + parts) * r, (1 + parts) * r + tall)]
+    everywhere = (slice(None),) * 4
+
+    def fetch(n):
+        at = everywhere + (spans[n],)
+        return pltpu.make_async_copy(late_ref.at[at], part_ref.at[at], sems.at[n])
+
+    def deliver(n):
+        at = everywhere + (spans[n],)
+        return pltpu.make_async_copy(part_ref.at[at], part_out.at[at], sems.at[3 + n])
+
     hidden = bias_ref.shape[1]
     part = 512
 
     @pl.when(step == 0)
     def _():
+        for n in range(3):
+            fetch(n).start()
         wo_acc[...] = jnp.zeros_like(wo_acc)
         wi_acc[...] = jnp.zeros_like(wi_acc)
         w2_acc[...] = jnp.zeros_like(w2_acc)
         sums_ref[...] = jnp.zeros_like(sums_ref)
         bsum_ref[...] = jnp.zeros_like(bsum_ref)
+        fetch(0).wait()
         for f, (a, b, core) in enumerate(group):
-            rows = slice(f * r, (f + 1) * r)
-            block = lambda e, lo, n: late_ref[e, a, b, core, lo : lo + n, :]
-            wo_ref[rows, :] = jnp.concatenate([block(e, 0, r) for e in range(dp)], 1)
-            wi_ref[rows, :] = jnp.concatenate([block(e, (1 + n) * r, r) for e in range(dp) for n in range(parts)], 1)
+            wo_ref[f * r : (f + 1) * r, :] = jnp.concatenate([part_ref[e, a, b, core, :r, :] for e in range(dp)], 1)
+        fetch(1).wait()
+        for f, (a, b, core) in enumerate(group):
+            wi_ref[f * r : (f + 1) * r, :] = jnp.concatenate(
+                [part_ref[e, a, b, core, (1 + n) * r : (2 + n) * r, :] for e in range(dp) for n in range(parts)], 1
+            )
+        fetch(2).wait()
+        for f, (a, b, core) in enumerate(group):
             w2_ref[f * tall : (f + 1) * tall, :] = jnp.concatenate(
-                [block(e, (1 + parts) * r, tall) for e in range(dp)], 1
+                [part_ref[e, a, b, core, (1 + parts) * r :, :] for e in range(dp)], 1
             )
 
     vec = lambda n: vec_ref[n : n + 1, :]
@@ -852,15 +968,23 @@
     @pl.when(step == pl.num_programs(0) - 1)
     def _():
         for e in range(dp):
-            lanes = slice(e * c, (e + 1) * c)
             for f, (a, b, core) in enumerate(group):
-                rows = slice(f * r, (f + 1) * r)
-                part_ref[e, a, b, core, :r, :] = wo_acc[rows, lanes].astype(BF16)
                 for n in range(parts):
                     wide = slice((e * parts + n) * c, (e * parts + n + 1) * c)
-                    part_ref[e, a, b, core, (1 + n) * r : (2 + n) * r, :] = wi_acc[rows, wide].astype(BF16)
-                turned = w2_acc[lanes, f * tall : (f + 1) * tall].astype(BF16)
+                    rows = slice((1 + n) * r, (2 + n) * r)
+                    part_ref[e, a, b, core, rows, :] = wi_acc[f * r : (f + 1) * r, wide].astype(BF16)
+        deliver(1).start()
+        for e in range(dp):
+            for f, (a, b, core) in enumerate(group):
+                turned = w2_acc[e * c : (e + 1) * c, f * tall : (f + 1) * tall].astype(BF16)
                 part_ref[e, a, b, core, (1 + parts) * r :, :] = turned.T
+        deliver(2).start()
+        for e in range(dp):
+            for f, (a, b, core) in enumerate(group):
+                part_ref[e, a, b, core, :r, :] = wo_acc[f * r : (f + 1) * r, e * c : (e + 1) * c].astype(BF16)
+        deliver(0).start()
+        for n in range(3):
+            deliver(n).wait()
 
 
 def whole(shape):
@@ -880,17 +1004,25 @@
     late_rows = r + r * wi.shape[1] // c + w2.shape[0]
     row3 = lambda shape: pl.BlockSpec((1,) + shape, lambda i: (i,) + (0,) * len(shape))
     seqs = row3((seq, width))
-    turned = row3((width, seq))
     st, tt = jax.ShapeDtypeStruct((rows, seq, width), BF16), jax.ShapeDtypeStruct((rows, width, seq), BF16)
     small = [x.shape for x in (wq, wk, wv, wo, wi, w2, table, place, line)]
+    anywhere = pl.BlockSpec(memory_space=pl.ANY)
     return pl.pallas_call(
         forward_attention,
         grid=(rows,),
         in_specs=[pl.BlockSpec(memory_space=pltpu.SMEM), seqs] + [whole(x) for x in small],
-        out_specs=[seqs, turned, seqs, turned, seqs, seqs, row3((H // 2, 2, seq)), whole((width, 3 * width)),
-                   whole((seq, width)), whole((table.shape[0] * dp, width)), whole((1, hidden)),
-                   pl.BlockSpec(memory_space=pl.ANY)],
+        out_specs=[anywhere] * 6 + [seqs, row3((H // 2, 2, seq)), anywhere, anywhere,
+                                    whole((table.shape[0] * dp, width)), whole((1, hidden)), anywhere],
         scratch_shapes=[
+            pltpu.VMEM((1, seq, width), BF16),
+            pltpu.VMEM((1, width, seq), BF16),
+            pltpu.VMEM((1, seq, width), BF16),
+            pltpu.VMEM((1, width, seq), BF16),
+            pltpu.VMEM((1, seq, width), BF16),
+            pltpu.VMEM((1, width, seq), BF16),
+            pltpu.VMEM((width, 3 * width), BF16),
+            pltpu.VMEM((seq, width), BF16),
+            pltpu.SemaphoreType.DMA((8,)),
             pltpu.VMEM((width, seq), BF16),
             pltpu.VMEM((2, width, WIN), BF16),
             pltpu.VMEM((dp, side, side, 2, first_rows, c), BF16),
@@ -899,7 +1031,7 @@
         ]
         + Gather.semaphores(dp, side) * 2,
         out_shape=[
-            st, tt, st, tt, st, st, jax.ShapeDtypeStruct((rows, H // 2, 2, seq), F32),
+            st, tt, st, tt, st, tt, st, jax.ShapeDtypeStruct((rows, H // 2, 2, seq), F32),
             jax.ShapeDtypeStruct((width, 3 * width), BF16),
             jax.ShapeDtypeStruct((seq, width), BF16),
             jax.ShapeDtypeStruct((table.shape[0] * dp, width), F32),
@@ -913,8 +1045,8 @@
     )(lengths, act, wq, wk, wv, wo, wi, w2, table, place, line)
 
 
-def run_backward(lengths, q, qt, k, kt, v, lse, grad, first, act, pos, weight, late, sums, bsum):
-    rows, seq, width = act.shape
+def run_backward(lengths, q, qt, k, kt, v, lse, grad, first, lowt, weight, late, sums, bsum):
+    rows, seq, width = grad.shape
     dp, side = late.shape[:2]
     late_rows, c = late.shape[4:]
     r = width // (2 * side * side)
@@ -928,10 +1060,14 @@
         backward_attention,
         grid=(H // 2,),
         in_specs=[pl.BlockSpec(memory_space=pltpu.SMEM), lanes, turned, lanes, turned, lanes,
-                  pl.BlockSpec((rows, 1, 2, seq), lambda j: (0, j, 0, 0)), lanes, anywhere, once(act.shape),
-                  once(pos.shape), once(weight.shape), anywhere, once(sums.shape), once(bsum.shape)],
-        out_specs=[whole(act.shape)] + [whole(x) for x in totals],
+                  pl.BlockSpec((rows, 1, 2, seq), lambda j: (0, j, 0, 0)), lanes, anywhere, anywhere, anywhere,
+                  anywhere, once(sums.shape), once(bsum.shape)],
+        out_specs=[anywhere] + [whole(x) for x in totals],
         scratch_shapes=[
+            pltpu.VMEM(weight.shape, BF16),
+            pltpu.VMEM(grad.shape, BF16),
+            pltpu.SemaphoreType.DMA((rows + 1,)),
+            pltpu.SemaphoreType.DMA((dp,)),
             pltpu.VMEM((width, rows * seq), BF16),
             pltpu.VMEM((rows, PAIR, seq), BF16),
             pltpu.VMEM((rows, PAIR, seq), BF16),
@@ -949,26 +1085,27 @@
         + Reduce.scratch(dp, side, late_rows, c)
         + Reduce.scratch(dp, side, weight_rows, c)
         + Reduce.scratch(dp, side, place_rows, c),
-        out_shape=[jax.ShapeDtypeStruct(act.shape, BF16)] + [jax.ShapeDtypeStruct(x, F32) for x in totals],
+        out_shape=[jax.ShapeDtypeStruct(grad.shape, BF16)] + [jax.ShapeDtypeStruct(x, F32) for x in totals],
         compiler_params=pltpu.CompilerParams(
             vmem_limit_bytes=VMEM_LIMIT, collective_id=1, has_side_effects=True
         ),
         name="backward_attention",
-    )(lengths, q, qt, k, kt, v, lse, grad, first, act, pos, weight, late, sums, bsum)
+    )(lengths, q, qt, k, kt, v, lse, grad, first, lowt, weight, late, sums, bsum)
 
 
 def run_hand_out(late, weight, place, grad, shapes):
-    steps = 4
-    block = pl.BlockSpec((1, grad.shape[0] * grad.shape[1] // steps, grad.shape[2]), lambda i: (i, 0, 0))
-    rows = grad.reshape(steps, -1, grad.shape[2])
+    vmem, anywhere = pl.BlockSpec(memory_space=pltpu.VMEM), pl.BlockSpec(memory_space=pl.ANY)
+    tokens = grad.reshape(-1, grad.shape[-1])
     return pl.pallas_call(
         hand_out,
-        grid=(steps,),
-        in_specs=[whole(x.shape) for x in (late, weight, place)] + [block],
-        out_specs=[block] + [whole(x) for x in shapes],
-        out_shape=[jax.ShapeDtypeStruct(rows.shape, BF16)] + [jax.ShapeDtypeStruct(x, F32) for x in shapes],
+        in_specs=[vmem, vmem, vmem, anywhere],
+        out_specs=[anywhere] + [vmem] * len(shapes),
+        out_shape=[jax.ShapeDtypeStruct(tokens.shape, BF16)] + [jax.ShapeDtypeStruct(x, F32) for x in shapes],
+        scratch_shapes=[
+            pltpu.VMEM(tokens.shape, BF16), pltpu.SemaphoreType.DMA((4,)), pltpu.SemaphoreType.DMA((4,)),
+        ],
         name="hand_out",
-    )(late, weight, place, rows)
+    )(late, weight, place, tokens)
 
 
 def run_feed_forward(ctx, act, pos, cot, late, vec, bias, tile=512):
@@ -981,8 +1118,9 @@
         feed_forward,
         grid=(tokens // tile,),
         in_specs=[tok, tok, pl.BlockSpec((tile, width), lambda t: (t % per_row, 0)), tok,
-                  once(late.shape), whole(vec.shape), whole(bias.shape)],
-        out_specs=[tok, tok, tok, whole(late.shape), whole((8, width)), whole((1, hidden))],
+                  pl.BlockSpec(memory_space=pl.ANY), whole(vec.shape), whole(bias.shape)],
+        out_specs=[tok, tok, tok, pl.BlockSpec(memory_space=pl.ANY), whole((8, width)),
+                   whole((1, hidden))],
         scratch_shapes=[
             pltpu.VMEM((width, width), F32),
             pltpu.VMEM((width, hidden), F32),
@@ -991,6 +1129,8 @@
             pltpu.VMEM((width, width), BF16),
             pltpu.VMEM((width, hidden), BF16),
             pltpu.VMEM((hidden, width), BF16),
+            pltpu.VMEM(late.shape, BF16),
+            pltpu.SemaphoreType.DMA((6,)),
         ],
         out_shape=[
             jax.ShapeDtypeStruct((tokens, width), BF16),
@@ -1010,7 +1150,7 @@
     vectors, positions, inner_bias, output_cotangent,
 ):
     rows, seq, width = activations.shape
-    q, qt, k, kt, v, ctx, lse, weight, pos, vec, bias, late = run_forward(
+    q, qt, k, kt, v, lowt, ctx, lse, weight, pos, vec, bias, late = run_forward(
         window_lengths, activations, query_weight, key_weight, value_weight, output_weight, inner_weight, outer_weight,
         vectors, positions.T, inner_bias.reshape(1, -1),
     )
@@ -1020,7 +1160,7 @@
         flat(ctx), flat(activations), pos, flat(output_cotangent), late, vec, bias
     )
     input_grad, *sums = run_backward(
-        window_lengths, q, qt, k, kt, v, lse, deep(grad), deep(first), activations, pos, weight, part, sums, bsum
+        window_lengths, q, qt, k, kt, v, lse, deep(grad), deep(first), lowt, weight, part, sums, bsum
     )
     shapes = [x.shape for x in (query_weight, key_weight, value_weight, output_weight, inner_weight, outer_weight,
                                 vectors, positions.T)] + [(1, inner_bias.shape[0])]

time: 170 us -> 158 us (0.929)
  Pallas kernels: 169 us -> 157 us
    pallas_call x1, Pallas kernels: 64.9 us -> 56.3 us  [run_backward(): pl.pallas_call(backward_attention, grid=(H // 2,), in_specs=[pl.BlockSpec...]
    pallas_call x1, Pallas kernels: 53.4 us -> 49.2 us  [run_forward(): pl.pallas_call(forward_attention, grid=(rows,), in_specs=[pl.BlockSpec(me...]
where the time goes in v4:
time: 158 us
  Pallas kernels  157 us (99%)
    pallas_call x1, Pallas kernels, run_backward(): pl.pallas_call(backward_attention, grid=(H // 2,), in_specs=[pl.BlockSpec...  56.3 us
    pallas_call x1, Pallas kernels, run_forward(): pl.pallas_call(forward_attention, grid=(rows,), in_specs=[pl.BlockSpec(me...  49.2 us
    pallas_call x1, Pallas kernels, run_feed_forward(): pl.pallas_call(feed_forward, grid=(tokens // tile,), in_specs=[tok, tok,...  47 us
    pallas_call x1, Pallas kernels, run_hand_out(): pl.pallas_call(hand_out, in_specs=[vmem, vmem, vmem, anywhere], out_specs...  4.21 us

profile of v4, /device:TPU:0, one launch (start us, length us, event | category | flops | bytes accessed | tf_op | source)
XLA Modules:
  0.0 157.6 jit_solution(1285458275894146026)
XLA Ops:
  0.6 49.2 %forward_attention.1 = (bf16[2,1024,512]{2,1,0:T(8,128)(2,1)}, bf16[2,512,1024]{2,1,0:T(8,128)(2,1)}, bf16[2,1024,512]{2,1,0:T(8,128)(2,1)}, bf16[2,512,1024]{2,...) custom-call(s32[2,4]{1,0:T(2,128)} %lengths_ref.3, ...), custom_call_target="tpu_custom_call" | custom-call | tf_op jit(solution)/shard_map/forward_attention/pallas_call | solution.py:1010
  49.9 47.0 %feed_forward.1 = (bf16[2048,512]{1,0:T(8,128)(2,1)}, f32[2048,512]{1,0:T(8,128)}, bf16[2048,512]{1,0:T(8,128)(2,1)}, bf16[4,2,2,2,576,128]{5,4,3,2,1,0:T(8,128)...) custom-call(bf16[2048,512]{1,0:T(8,128)(2,1)} %bitcast.15, bf16[2048,512]{1,0:T(8,128)(2,1)} %bitcast.12, ...), custom_call_target="tpu_custom_call" | custom-call | tf_op jit(solution)/shard_map/feed_forward/pallas_call | solution.py:1117
  96.9 56.3 %backward_attention.1 = (bf16[2,1024,512]{2,1,0:T(8,128)(2,1)}, f32[576,128]{1,0:T(8,128)}, f32[192,128]{1,0:T(8,128)}, f32[144,128]{1,0:T(8,128)}) custom-call(s32[2,4]{1,0:T(2,128)} %lengths_ref.3, bf16[2,1024,512]{2,1,0:T(8,128)(2,1)} %get-tuple-element.50.q_ref, bf16[2,512,1024]{2,1,0:T(8,128)(2,1)} %get-tuple-element.51.qt_ref, ...), custom_call_target="tpu_custom_call" | custom-call | tf_op jit(solution)/shard_map/backward_attention/pallas_call | solution.py:1059
  153.2 4.2 %hand_out.1 = (bf16[2048,512]{1,0:T(8,128)(2,1)}, f32[64,128]{1,0:T(8,128)}, f32[64,128]{1,0:T(8,128)}, f32[64,128]{1,0:T(8,128)}, f32[64,128]{1,0:T(8,128)}, /*...) custom-call(f32[576,128]{1,0:T(8,128)} %get-tuple-element.63.late_ref, ...), custom_call_target="tpu_custom_call" | custom-call | tf_op jit(solution)/shard_map/hand_out/pallas_call | solution.py:1099

commit v5 on v4

--- a/solution.py
+++ b/solution.py
@@ -16,6 +16,7 @@
 BF16 = jnp.bfloat16
 MESH = pl.DeviceIdType.MESH
 SMALL = 16
+LATER = 2
 
 
 def nn(left, right):
@@ -341,15 +342,15 @@
 
 
 def forward_attention(
-    lengths_ref, act_ref, wq_ref, wk_ref, wv_ref, wo_ref, wi_ref, w2_ref, table_ref, place_ref, line_ref,
+    lengths_ref, act_in, wq_ref, wk_ref, wv_ref, wo_ref, wi_ref, w2_ref, table_ref, place_ref, line_ref,
     q_out, qt_out, k_out, kt_out, v_out, lowt_out, ctx_ref, lse_ref, weight_out, pos_out, vec_ref, bias_ref, late_ref,
-    q_ref, qt_ref, k_ref, kt_ref, v_ref, lowt_ref, weight_ref, pos_ref, out_sems,
+    act_ref, act_sems, q_ref, qt_ref, k_ref, kt_ref, v_ref, lowt_ref, weight_ref, pos_ref, out_sems,
     vt_ref, ctxt_ref, early_ref, own_ref, own_sem, *sems,
 ):
     row = pl.program_id(0)
     rows = pl.num_programs(0)
-    width = act_ref.shape[2]
-    blocks = act_ref.shape[1] // WIN
+    width = act_in.shape[2]
+    blocks = act_in.shape[1] // WIN
     at = Place()
     dp = at.dp
     here = (at.d, at.a, at.b, at.core)
@@ -363,6 +364,9 @@
     def own_copy():
         return pltpu.make_async_copy(own_ref, late_ref.at[here], own_sem)
 
+    def act_copy(of_row):
+        return pltpu.make_async_copy(act_in.at[of_row], act_ref.at[of_row], act_sems.at[of_row])
+
     def row_copies(of_row):
         pairs = ((q_ref, q_out), (qt_ref, qt_out), (k_ref, k_out), (kt_ref, kt_out), (v_ref, v_out),
                  (lowt_ref, lowt_out))
@@ -377,6 +381,8 @@
     @pl.when(row == 0)
     def _():
         count = greet(at)
+        for n in range(act_in.shape[0]):
+            act_copy(n).start()
         for n, ref in enumerate((wq_ref, wk_ref, wv_ref)):
             early_ref[here + (slice(n * r, (n + 1) * r),)] = ref[...]
         place = place_ref[...].T
@@ -446,9 +452,11 @@
         for copy in row_copies(row - 1):
             copy.wait()
 
+    act_copy(row).wait()
+
     def project(step, carry):
         spot = pl.ds(pl.multiple_of(step * WIN, WIN), WIN)
-        low = (act_ref[0, spot, :].astype(F32) + pos_ref[spot, :].astype(F32)).astype(BF16)
+        low = (act_ref[row, spot, :].astype(F32) + pos_ref[spot, :].astype(F32)).astype(BF16)
         lowt_ref[0, :, spot] = low.T
         every = nn(low, weight_ref[...])
         q = (every[:, :width] + vec_ref[0:1, :]).astype(BF16)
@@ -591,12 +599,6 @@
         for block in range(blocks):
             gradt_ref[row, :, block_of(block)] = grad_ref[row, block_of(block), :].T
 
-    @pl.when(step == 0)
-    def _():
-        meet(dp + 2 * at.side - 2)
-        for e in nearest:
-            late.begin(e)
-
     def score(row, block, head):
         q_head = head_rows(qt_ref[row, :, block_of(block)], head)
         g_head = head_rows(gradt_ref[row, :, block_of(block)], head)
@@ -680,9 +682,9 @@
 
         @pl.when(step == 0)
         def _():
-            late.own_half().wait()
+            meet(dp + 2 * at.side - 2)
             for e in nearest:
-                late.across(e)
+                late.begin(e)
 
         @pl.when(step == 1)
         def _():
@@ -701,6 +703,9 @@
 
         @pl.when(step == 0)
         def _():
+            late.own_half().wait()
+            for e in nearest:
+                late.across(e)
             for load in arriving:
                 load.wait()
 
@@ -768,12 +773,12 @@
         weights_on()
         on(finish, *downward[: blocks // 2])
         attend(*downward[blocks // 2 : -1])
+        on(places.across, *downward[: blocks // 2])
         on(finish, *downward[blocks // 2 : -1])
         for e in pieces(last - 2):
             weights.middle(e)
         for e in pieces(last - 3):
             weights.along(e)
-        on(places.across, *downward[: blocks // 2])
         attend(downward[-1])
         sum_tokens()
         on(finish, downward[-1])
@@ -806,16 +811,20 @@
             input_copy(e).wait()
 
 
-def hand_out(
-    late_ref, weight_ref, place_ref, input_ref,
-    out_ref, wq_ref, wk_ref, wv_ref, wo_ref, wi_ref, w2_ref, table_ref, placet_ref, line_ref,
-    held_ref, in_sems, out_sems,
-):
-    pieces = in_sems.shape[0]
-    some = input_ref.shape[0] // pieces
+def hand_out(late_in, weight_in, place_in, input_in, *refs):
+    count = (len(refs) - 7) // 2
+    outs, (late_ref, weight_ref, place_ref, input_ref), stages = refs[: count + 1], refs[count + 1 : count + 5], refs[count + 5 : -2]
+    load_sems, store_sems = refs[-2:]
+    wq_ref, wk_ref, wv_ref, wo_ref, wi_ref, w2_ref, table_ref, placet_ref, line_ref = stages
+    copy = pltpu.make_async_copy
+    small = [(late_in, late_ref), (weight_in, weight_ref), (place_in, place_ref)]
+    loads = [copy(src, dst, load_sems.at[n]) for n, (src, dst) in enumerate(small)]
+    pieces = load_sems.shape[0] - len(small)
+    some = input_in.shape[0] // pieces
     spots = [slice(n * some, (n + 1) * some) for n in range(pieces)]
-    loads = [pltpu.make_async_copy(input_ref.at[x], held_ref.at[x], in_sems.at[n]) for n, x in enumerate(spots)]
-    stores = [pltpu.make_async_copy(held_ref.at[x], out_ref.at[x], out_sems.at[n]) for n, x in enumerate(spots)]
+    loads += [copy(input_in.at[x], input_ref.at[x], load_sems.at[3 + n]) for n, x in enumerate(spots)]
+    stores = [copy(src, dst, store_sems.at[n]) for n, (src, dst) in enumerate(zip(stages, outs[1:]))]
+    stores += [copy(input_ref.at[x], outs[0].at[x], store_sems.at[count + n]) for n, x in enumerate(spots)]
     for load in loads:
         load.start()
     r, c = wq_ref.shape
@@ -823,6 +832,8 @@
     held = placet_ref.shape[1]
     folds = c // narrow
     per = held // folds
+    for load in loads[:3]:
+        load.wait()
     for n, ref in enumerate((wq_ref, wk_ref, wv_ref)):
         ref[...] = weight_ref[n * r : (n + 1) * r, :]
     wide_parts = wi_ref.shape[1] // c
@@ -834,9 +845,11 @@
     placet_ref[...] = jnp.concatenate([place[:, n * narrow : (n + 1) * narrow] for n in range(folds)], 0).T
     table_ref[...] = place_ref[per : per + few, :narrow]
     line_ref[...] = place_ref[per + few : per + few + 1, : line_ref.shape[1]]
-    for load, store in zip(loads, stores):
-        load.wait()
+    for store in stores[:count]:
         store.start()
+    for n in range(pieces):
+        loads[3 + n].wait()
+        stores[count + n].start()
     for store in stores:
         store.wait()
 
@@ -867,122 +880,161 @@
     hidden = bias_ref.shape[1]
     part = 512
 
+    last = pl.num_programs(0) - 1
+    vec = lambda n: vec_ref[n : n + 1, :]
+    C = hidden // part
+    cols = [slice(n * part, (n + 1) * part) for n in range(C)]
+
+    def unpack(n):
+        fetch(n).wait()
+        for f, (a, b, core) in enumerate(group):
+            block = lambda e, lo, n: part_ref[e, a, b, core, lo : lo + n, :]
+            if n == 0:
+                wo_ref[f * r : (f + 1) * r, :] = jnp.concatenate([block(e, 0, r) for e in range(dp)], 1)
+            elif n == 1:
+                wi_ref[f * r : (f + 1) * r, :] = jnp.concatenate(
+                    [block(e, (1 + m) * r, r) for e in range(dp) for m in range(parts)], 1
+                )
+            else:
+                w2_ref[f * tall : (f + 1) * tall, :] = jnp.concatenate(
+                    [block(e, (1 + parts) * r, tall) for e in range(dp)], 1
+                )
+
+    def pack(n):
+        for e in range(dp):
+            for f, (a, b, core) in enumerate(group):
+                rows = slice(f * r, (f + 1) * r)
+                if n == 0:
+                    part_ref[e, a, b, core, :r, :] = wo_acc[rows, e * c : (e + 1) * c].astype(BF16)
+                elif n == 1:
+                    for m in range(parts):
+                        wide = slice((e * parts + m) * c, (e * parts + m + 1) * c)
+                        part_ref[e, a, b, core, (1 + m) * r : (2 + m) * r, :] = wi_acc[rows, wide].astype(BF16)
+                else:
+                    turned = w2_acc[e * c : (e + 1) * c, f * tall : (f + 1) * tall].astype(BF16)
+                    part_ref[e, a, b, core, (1 + parts) * r :, :] = turned.T
+        deliver(n).start()
+
+    def body(first, final):
+        def add(ref, at, value):
+            if first:
+                ref[at] = value
+            else:
+                ref[at] += value
+
+        def add_row(n, value):
+            add(sums_ref, (slice(n, n + 1), slice(None)), value)
+
+        if first:
+            for n in range(3):
+                fetch(n).start()
+            sums_ref[0:2, :] = jnp.zeros((2, width), F32)
+            unpack(0)
+        ctx = ctx_ref[...]
+        first_sum = act_ref[...].astype(F32) + pos_ref[...].astype(F32) + (nn(ctx, wo_ref[...]) + vec(2))
+        center = first_sum - jnp.mean(first_sum, -1, keepdims=True)
+        scale_one = lax.rsqrt(jnp.mean(center * center, -1, keepdims=True) + 1e-05)
+        z_one = center * scale_one
+        normed = z_one * vec(3) + vec(4)
+        normed_low = normed.astype(BF16)
+        if first:
+            unpack(1)
+        branch = None
+        acts = []
+        pre_next = nn(normed_low, wi_ref[:, cols[0]])
+        for n in range(C):
+            pre = pre_next + bias_ref[:, cols[n]]
+            if n + 1 < C:
+                pre_next = nn(normed_low, wi_ref[:, cols[n + 1]])
+            if n >= 1:
+                if first and n == 1:
+                    unpack(2)
+                term = nn(acts[n - 1], w2_ref[cols[n - 1], :])
+                branch = term if branch is None else branch + term
+            square = pre * pre
+            t = jnp.tanh(pre * (0.7978845608028654 + (0.7978845608028654 * 0.044715) * square))
+            half = 0.5 + 0.5 * t
+            acts.append((pre * half).astype(BF16))
+            slope_ref[:, cols[n]] = half + (0.5 * pre) * (1.0 - t * t) * (
+                0.7978845608028654 + (3.0 * 0.7978845608028654 * 0.044715) * square
+            )
+        branch = branch + nn(acts[C - 1], w2_ref[cols[C - 1], :])
+        second_sum = normed + (branch + vec(5))
+        center = second_sum - jnp.mean(second_sum, -1, keepdims=True)
+        scale_two = lax.rsqrt(jnp.mean(center * center, -1, keepdims=True) + 1e-05)
+        z_two = center * scale_two
+        out_ref[...] = (z_two * vec(6) + vec(7)).astype(BF16)
+        cot = cot_ref[...].astype(F32)
+        add_row(6, column_sum(cot * z_two))
+        add_row(7, column_sum(cot))
+        e = cot * vec(6)
+        second_grad = scale_two * (
+            e - jnp.mean(e, -1, keepdims=True) - z_two * jnp.mean(e * z_two, -1, keepdims=True)
+        )
+        branch_grad = second_grad.astype(BF16)
+        add_row(5, column_sum(branch_grad))
+        branch_t = branch_grad.T
+        normed_t = normed_low.T
+        normed_grad = second_grad
+        grad_next = nt(branch_grad, w2_ref[cols[0], :])
+        lows = []
+        everything = slice(None)
+
+        def inner(n):
+            add(wi_acc, (everything, cols[n]), nn(normed_t, lows[n]))
+
+        def outer(n):
+            add(w2_acc, (everything, cols[n]), nn(branch_t, acts[n]))
+
+        for n in range(C):
+            pre_grad = grad_next * slope_ref[:, cols[n]]
+            if n + 1 < C:
+                grad_next = nt(branch_grad, w2_ref[cols[n + 1], :])
+            if n < LATER:
+                outer(n)
+            if n >= 1:
+                inner(n - 1)
+                normed_grad = normed_grad + nt(lows[n - 1], wi_ref[:, cols[n - 1]])
+            lows.append(pre_grad.astype(BF16))
+            add(bsum_ref, (everything, cols[n]), column_sum(lows[n]))
+        normed_grad = normed_grad + nt(lows[C - 1], wi_ref[:, cols[C - 1]])
+        inner(C - 1)
+        add_row(3, column_sum(normed_grad * z_one))
+        add_row(4, column_sum(normed_grad))
+        e = normed_grad * vec(3)
+        level = jnp.mean(e, -1, keepdims=True)
+        slant = jnp.mean(e * z_one, -1, keepdims=True)
+        for n in range(LATER, C):
+            outer(n)
+        if final:
+            pack(1)
+            pack(2)
+        first_grad = scale_one * (e - level - z_one * slant)
+        first_ref[...] = first_grad
+        attn_grad = first_grad.astype(BF16)
+        add_row(2, column_sum(attn_grad))
+        add(wo_acc, (everything, everything), nn(ctx.T, attn_grad))
+        grad_ref[...] = nt(attn_grad, wo_ref[...]).astype(BF16)
+        if final:
+            pack(0)
+            for n in range(3):
+                deliver(n).wait()
+
     @pl.when(step == 0)
     def _():
         for n in range(3):
             fetch(n).start()
-        wo_acc[...] = jnp.zeros_like(wo_acc)
-        wi_acc[...] = jnp.zeros_like(wi_acc)
-        w2_acc[...] = jnp.zeros_like(w2_acc)
-        sums_ref[...] = jnp.zeros_like(sums_ref)
-        bsum_ref[...] = jnp.zeros_like(bsum_ref)
-        fetch(0).wait()
-        for f, (a, b, core) in enumerate(group):
-            wo_ref[f * r : (f + 1) * r, :] = jnp.concatenate([part_ref[e, a, b, core, :r, :] for e in range(dp)], 1)
-        fetch(1).wait()
-        for f, (a, b, core) in enumerate(group):
-            wi_ref[f * r : (f + 1) * r, :] = jnp.concatenate(
-                [part_ref[e, a, b, core, (1 + n) * r : (2 + n) * r, :] for e in range(dp) for n in range(parts)], 1
-            )
-        fetch(2).wait()
-        for f, (a, b, core) in enumerate(group):
-            w2_ref[f * tall : (f + 1) * tall, :] = jnp.concatenate(
-                [part_ref[e, a, b, core, (1 + parts) * r :, :] for e in range(dp)], 1
-            )
-
-    vec = lambda n: vec_ref[n : n + 1, :]
-    ctx = ctx_ref[...]
-    first_sum = act_ref[...].astype(F32) + pos_ref[...].astype(F32) + (nn(ctx, wo_ref[...]) + vec(2))
-    center = first_sum - jnp.mean(first_sum, -1, keepdims=True)
-    scale_one = lax.rsqrt(jnp.mean(center * center, -1, keepdims=True) + 1e-05)
-    z_one = center * scale_one
-    normed = z_one * vec(3) + vec(4)
-    normed_low = normed.astype(BF16)
-    branch = None
-    acts = []
-    C = hidden // part
-    cols = [slice(n * part, (n + 1) * part) for n in range(C)]
-    pre_next = nn(normed_low, wi_ref[:, cols[0]])
-    for n in range(C):
-        pre = pre_next + bias_ref[:, cols[n]]
-        if n + 1 < C:
-            pre_next = nn(normed_low, wi_ref[:, cols[n + 1]])
-        if n >= 1:
-            term = nn(acts[n - 1], w2_ref[cols[n - 1], :])
-            branch = term if branch is None else branch + term
-        square = pre * pre
-        t = jnp.tanh(pre * (0.7978845608028654 + (0.7978845608028654 * 0.044715) * square))
-        half = 0.5 + 0.5 * t
-        acts.append((pre * half).astype(BF16))
-        slope_ref[:, cols[n]] = half + (0.5 * pre) * (1.0 - t * t) * (
-            0.7978845608028654 + (3.0 * 0.7978845608028654 * 0.044715) * square
-        )
-    term = nn(acts[C - 1], w2_ref[cols[C - 1], :])
-    branch = term if branch is None else branch + term
-    second_sum = normed + (branch + vec(5))
-    center = second_sum - jnp.mean(second_sum, -1, keepdims=True)
-    scale_two = lax.rsqrt(jnp.mean(center * center, -1, keepdims=True) + 1e-05)
-    z_two = center * scale_two
-    out_ref[...] = (z_two * vec(6) + vec(7)).astype(BF16)
-    cot = cot_ref[...].astype(F32)
-    sums_ref[6:7, :] += column_sum(cot * z_two)
-    sums_ref[7:8, :] += column_sum(cot)
-    e = cot * vec(6)
-    second_grad = scale_two * (
-        e - jnp.mean(e, -1, keepdims=True) - z_two * jnp.mean(e * z_two, -1, keepdims=True)
-    )
-    branch_grad = second_grad.astype(BF16)
-    sums_ref[5:6, :] += column_sum(branch_grad)
-    branch_t = branch_grad.T
-    normed_t = normed_low.T
-    normed_grad = second_grad
-    grad_next = nt(branch_grad, w2_ref[cols[0], :])
-    lows = []
-
-    def weights(n):
-        wi_acc[:, cols[n]] += nn(normed_t, lows[n])
-        return nt(lows[n], wi_ref[:, cols[n]])
-
-    for n in range(C):
-        pre_grad = grad_next * slope_ref[:, cols[n]]
-        if n + 1 < C:
-            grad_next = nt(branch_grad, w2_ref[cols[n + 1], :])
-        w2_acc[:, cols[n]] += nn(branch_t, acts[n])
-        if n >= 1:
-            normed_grad = normed_grad + weights(n - 1)
-        lows.append(pre_grad.astype(BF16))
-        bsum_ref[:, cols[n]] += column_sum(lows[n])
-    normed_grad = normed_grad + weights(C - 1)
-    sums_ref[3:4, :] += column_sum(normed_grad * z_one)
-    sums_ref[4:5, :] += column_sum(normed_grad)
-    e = normed_grad * vec(3)
-    first_grad = scale_one * (
-        e - jnp.mean(e, -1, keepdims=True) - z_one * jnp.mean(e * z_one, -1, keepdims=True)
-    )
-    first_ref[...] = first_grad
-    attn_grad = first_grad.astype(BF16)
-    sums_ref[2:3, :] += column_sum(attn_grad)
-    wo_acc[...] += nn(ctx.T, attn_grad)
-    grad_ref[...] = nt(attn_grad, wo_ref[...]).astype(BF16)
-
-    @pl.when(step == pl.num_programs(0) - 1)
+        for ref in (wo_acc, wi_acc, w2_acc, sums_ref, bsum_ref):
+            ref[...] = jnp.zeros_like(ref)
+        for n in range(3):
+            unpack(n)
+
+    body(False, False)
+
+    @pl.when(step == last)
     def _():
-        for e in range(dp):
-            for f, (a, b, core) in enumerate(group):
-                for n in range(parts):
-                    wide = slice((e * parts + n) * c, (e * parts + n + 1) * c)
-                    rows = slice((1 + n) * r, (2 + n) * r)
-                    part_ref[e, a, b, core, rows, :] = wi_acc[f * r : (f + 1) * r, wide].astype(BF16)
-        deliver(1).start()
-        for e in range(dp):
-            for f, (a, b, core) in enumerate(group):
-                turned = w2_acc[e * c : (e + 1) * c, f * tall : (f + 1) * tall].astype(BF16)
-                part_ref[e, a, b, core, (1 + parts) * r :, :] = turned.T
-        deliver(2).start()
-        for e in range(dp):
-            for f, (a, b, core) in enumerate(group):
-                part_ref[e, a, b, core, :r, :] = wo_acc[f * r : (f + 1) * r, e * c : (e + 1) * c].astype(BF16)
-        deliver(0).start()
+        for n in (1, 2, 0):
+            pack(n)
         for n in range(3):
             deliver(n).wait()
 
@@ -1010,10 +1062,12 @@
     return pl.pallas_call(
         forward_attention,
         grid=(rows,),
-        in_specs=[pl.BlockSpec(memory_space=pltpu.SMEM), seqs] + [whole(x) for x in small],
+        in_specs=[pl.BlockSpec(memory_space=pltpu.SMEM), anywhere] + [whole(x) for x in small],
         out_specs=[anywhere] * 6 + [seqs, row3((H // 2, 2, seq)), anywhere, anywhere,
                                     whole((table.shape[0] * dp, width)), whole((1, hidden)), anywhere],
         scratch_shapes=[
+            pltpu.VMEM(act.shape, BF16),
+            pltpu.SemaphoreType.DMA((rows,)),
             pltpu.VMEM((1, seq, width), BF16),
             pltpu.VMEM((1, width, seq), BF16),
             pltpu.VMEM((1, seq, width), BF16),
@@ -1094,16 +1148,18 @@
 
 
 def run_hand_out(late, weight, place, grad, shapes):
-    vmem, anywhere = pl.BlockSpec(memory_space=pltpu.VMEM), pl.BlockSpec(memory_space=pl.ANY)
+    anywhere = pl.BlockSpec(memory_space=pl.ANY)
     tokens = grad.reshape(-1, grad.shape[-1])
+    dma = pltpu.SemaphoreType.DMA
+    pieces = 4
     return pl.pallas_call(
         hand_out,
-        in_specs=[vmem, vmem, vmem, anywhere],
-        out_specs=[anywhere] + [vmem] * len(shapes),
+        in_specs=[anywhere] * 4,
+        out_specs=[anywhere] * (1 + len(shapes)),
         out_shape=[jax.ShapeDtypeStruct(tokens.shape, BF16)] + [jax.ShapeDtypeStruct(x, F32) for x in shapes],
-        scratch_shapes=[
-            pltpu.VMEM(tokens.shape, BF16), pltpu.SemaphoreType.DMA((4,)), pltpu.SemaphoreType.DMA((4,)),
-        ],
+        scratch_shapes=[pltpu.VMEM(x.shape, x.dtype) for x in (late, weight, place, tokens)]
+        + [pltpu.VMEM(x, F32) for x in shapes]
+        + [dma((3 + pieces,)), dma((len(shapes) + pieces,))],
         name="hand_out",
     )(late, weight, place, tokens)
 

time: 158 us -> 155 us (0.981)
  Pallas kernels: 157 us -> 154 us
where the time goes in v5:
time: 155 us
  Pallas kernels  154 us (99%)
    pallas_call x1, Pallas kernels, run_backward(): pl.pallas_call(backward_attention, grid=(H // 2,), in_specs=[pl.BlockSpec...  56.2 us
    pallas_call x1, Pallas kernels, run_forward(): pl.pallas_call(forward_attention, grid=(rows,), in_specs=[pl.BlockSpec(me...  49 us
    pallas_call x1, Pallas kernels, run_feed_forward(): pl.pallas_call(feed_forward, grid=(tokens // tile,), in_specs=[tok, tok,...  46.2 us

profile of v5, /device:TPU:0, one launch (start us, length us, event | category | flops | bytes accessed | tf_op | source)
XLA Modules:
  0.0 155.0 jit_solution(11595871762267264143)
XLA Ops:
  0.6 49.0 %forward_attention.1 = (bf16[2,1024,512]{2,1,0:T(8,128)(2,1)}, bf16[2,512,1024]{2,1,0:T(8,128)(2,1)}, bf16[2,1024,512]{2,1,0:T(8,128)(2,1)}, bf16[2,512,1024]{2,...) custom-call(s32[2,4]{1,0:T(2,128)} %lengths_ref.3, ...), custom_call_target="tpu_custom_call" | custom-call | tf_op jit(solution)/shard_map/forward_attention/pallas_call | solution.py:1062
  49.6 46.2 %feed_forward.1 = (bf16[2048,512]{1,0:T(8,128)(2,1)}, f32[2048,512]{1,0:T(8,128)}, bf16[2048,512]{1,0:T(8,128)(2,1)}, bf16[4,2,2,2,576,128]{5,4,3,2,1,0:T(8,128)...) custom-call(bf16[2048,512]{1,0:T(8,128)(2,1)} %bitcast.15, bf16[2048,512]{1,0:T(8,128)(2,1)} %bitcast.12, ...), custom_call_target="tpu_custom_call" | custom-call | tf_op jit(solution)/shard_map/feed_forward/pallas_call | solution.py:1173
  95.9 56.2 %backward_attention.1 = (bf16[2,1024,512]{2,1,0:T(8,128)(2,1)}, f32[576,128]{1,0:T(8,128)}, f32[192,128]{1,0:T(8,128)}, f32[144,128]{1,0:T(8,128)}) custom-call(s32[2,4]{1,0:T(2,128)} %lengths_ref.3, bf16[2,1024,512]{2,1,0:T(8,128)(2,1)} %get-tuple-element.50.q_ref, bf16[2,512,1024]{2,1,0:T(8,128)(2,1)} %get-tuple-element.51.qt_ref, ...), custom_call_target="tpu_custom_call" | custom-call | tf_op jit(solution)/shard_map/backward_attention/pallas_call | solution.py:1113
  152.1 2.7 %hand_out.1 = (bf16[2048,512]{1,0:T(8,128)(2,1)}, f32[64,128]{1,0:T(8,128)}, f32[64,128]{1,0:T(8,128)}, f32[64,128]{1,0:T(8,128)}, f32[64,128]{1,0:T(8,128)}, /*...) custom-call(f32[576,128]{1,0:T(8,128)} %get-tuple-element.63.late_in, ...), custom_call_target="tpu_custom_call" | custom-call | tf_op jit(solution)/shard_map/hand_out/pallas_call | solution.py:1155

commit v6 on v5

--- a/solution.py
+++ b/solution.py
@@ -783,23 +783,25 @@
         sum_tokens()
         on(finish, downward[-1])
         on(places.across, *downward[blocks // 2 : -1])
+        on(places.across, downward[-1])
         send_weights()
         for e in pieces(last - 1):
             weights.middle(e)
         on(places.middle, *downward[: blocks // 2])
-        on(places.across, downward[-1])
+        on(places.middle, *downward[blocks // 2 : -1])
+        on(places.middle, downward[-1])
         for e in pieces(last):
             weights.across(e)
-        on(places.middle, *downward[blocks // 2 : -1])
         on(places.along, *downward[: blocks // 2])
-        for e in pieces(last - 2) + pieces(last - 1):
+        on(places.along, *downward[blocks // 2 : -1])
+        on(places.along, downward[-1])
+        for e in pieces(last - 2):
             weights.along(e)
-        on(places.middle, downward[-1])
-        on(places.along, *downward[blocks // 2 : -1])
+        for e in pieces(last - 1):
+            weights.along(e)
         for e in pieces(last):
             weights.middle(e)
         late_sum_ref[...] = late.result()
-        on(places.along, downward[-1])
         for e in pieces(last):
             weights.along(e)
         place_sum_ref[...] = places.result()

time: 155 us -> 154 us (level)
  Pallas kernels: 154 us -> 152 us
    pallas_call x1, Pallas kernels: 56.2 us -> 54.6 us  [run_backward(): pl.pallas_call(backward_attention, grid=(H // 2,), in_specs=[pl.BlockSpec...]
where the time goes in v6:
time: 154 us; the launch traced here: 153 us
  Pallas kernels  152 us (99%)
    pallas_call x1, Pallas kernels, run_backward(): pl.pallas_call(backward_attention, grid=(H // 2,), in_specs=[pl.BlockSpec...  54.6 us
    pallas_call x1, Pallas kernels, run_forward(): pl.pallas_call(forward_attention, grid=(rows,), in_specs=[pl.BlockSpec(me...  49 us
    pallas_call x1, Pallas kernels, run_feed_forward(): pl.pallas_call(feed_forward, grid=(tokens // tile,), in_specs=[tok, tok,...  46.2 us

profile of v6, /device:TPU:0, one launch (start us, length us, event | category | flops | bytes accessed | tf_op | source)
XLA Modules:
  0.0 153.3 jit_solution(16985921199768977249)
XLA Ops:
  0.6 49.0 %forward_attention.1 = (bf16[2,1024,512]{2,1,0:T(8,128)(2,1)}, bf16[2,512,1024]{2,1,0:T(8,128)(2,1)}, bf16[2,1024,512]{2,1,0:T(8,128)(2,1)}, bf16[2,512,1024]{2,...) custom-call(s32[2,4]{1,0:T(2,128)} %lengths_ref.3, ...), custom_call_target="tpu_custom_call" | custom-call | tf_op jit(solution)/shard_map/forward_attention/pallas_call | solution.py:1064
  49.6 46.2 %feed_forward.1 = (bf16[2048,512]{1,0:T(8,128)(2,1)}, f32[2048,512]{1,0:T(8,128)}, bf16[2048,512]{1,0:T(8,128)(2,1)}, bf16[4,2,2,2,576,128]{5,4,3,2,1,0:T(8,128)...) custom-call(bf16[2048,512]{1,0:T(8,128)(2,1)} %bitcast.15, bf16[2048,512]{1,0:T(8,128)(2,1)} %bitcast.12, ...), custom_call_target="tpu_custom_call" | custom-call | tf_op jit(solution)/shard_map/feed_forward/pallas_call | solution.py:1175
  95.9 54.6 %backward_attention.1 = (bf16[2,1024,512]{2,1,0:T(8,128)(2,1)}, f32[576,128]{1,0:T(8,128)}, f32[192,128]{1,0:T(8,128)}, f32[144,128]{1,0:T(8,128)}) custom-call(s32[2,4]{1,0:T(2,128)} %lengths_ref.3, bf16[2,1024,512]{2,1,0:T(8,128)(2,1)} %get-tuple-element.50.q_ref, bf16[2,512,1024]{2,1,0:T(8,128)(2,1)} %get-tuple-element.51.qt_ref, ...), custom_call_target="tpu_custom_call" | custom-call | tf_op jit(solution)/shard_map/backward_attention/pallas_call | solution.py:1115
  150.4 2.7 %hand_out.1 = (bf16[2048,512]{1,0:T(8,128)(2,1)}, f32[64,128]{1,0:T(8,128)}, f32[64,128]{1,0:T(8,128)}, f32[64,128]{1,0:T(8,128)}, f32[64,128]{1,0:T(8,128)}, /*...) custom-call(f32[576,128]{1,0:T(8,128)} %get-tuple-element.63.late_in, ...), custom_call_target="tpu_custom_call" | custom-call | tf_op jit(solution)/shard_map/hand_out/pallas_call | solution.py:1157

commit v7 on v6

--- a/solution.py
+++ b/solution.py
@@ -406,13 +406,15 @@
         early.pass_on(0)
         early.far(0)
         early.relay(0)
-        for o in range(1, dp):
+        early.spread(1)
+        early.far(1)
+        for o in range(2, dp):
             early.spread(o)
+            early.relay(o - 1)
+            early.far(o)
         own_copy().wait()
         late.begin()
-        for o in range(1, dp):
-            early.relay(o)
-            early.far(o)
+        early.relay(dp - 1)
         early.near()
         late.pass_on(0)
         late.far(0)
@@ -784,9 +786,9 @@
         on(finish, downward[-1])
         on(places.across, *downward[blocks // 2 : -1])
         on(places.across, downward[-1])
-        send_weights()
         for e in pieces(last - 1):
             weights.middle(e)
+        send_weights()
         on(places.middle, *downward[: blocks // 2])
         on(places.middle, *downward[blocks // 2 : -1])
         on(places.middle, downward[-1])

time: 154 us -> 153 us (level)
  no operation moved by 1% of the time
where the time goes in v7:
time: 153 us
  Pallas kernels  152 us (99%)
    pallas_call x1, Pallas kernels, run_backward(): pl.pallas_call(backward_attention, grid=(H // 2,), in_specs=[pl.BlockSpec...  55 us
    pallas_call x1, Pallas kernels, run_forward(): pl.pallas_call(forward_attention, grid=(rows,), in_specs=[pl.BlockSpec(me...  48.3 us
    pallas_call x1, Pallas kernels, run_feed_forward(): pl.pallas_call(feed_forward, grid=(tokens // tile,), in_specs=[tok, tok,...  46.2 us

profile of v7, /device:TPU:0, one launch (start us, length us, event | category | flops | bytes accessed | tf_op | source)
XLA Modules:
  0.0 153.0 jit_solution(12032190965941763028)
XLA Ops:
  0.6 48.3 %forward_attention.1 = (bf16[2,1024,512]{2,1,0:T(8,128)(2,1)}, bf16[2,512,1024]{2,1,0:T(8,128)(2,1)}, bf16[2,1024,512]{2,1,0:T(8,128)(2,1)}, bf16[2,512,1024]{2,...) custom-call(s32[2,4]{1,0:T(2,128)} %lengths_ref.3, ...), custom_call_target="tpu_custom_call" | custom-call | tf_op jit(solution)/shard_map/forward_attention/pallas_call | solution.py:1066
  48.9 46.2 %feed_forward.1 = (bf16[2048,512]{1,0:T(8,128)(2,1)}, f32[2048,512]{1,0:T(8,128)}, bf16[2048,512]{1,0:T(8,128)(2,1)}, bf16[4,2,2,2,576,128]{5,4,3,2,1,0:T(8,128)...) custom-call(bf16[2048,512]{1,0:T(8,128)(2,1)} %bitcast.15, bf16[2048,512]{1,0:T(8,128)(2,1)} %bitcast.12, ...), custom_call_target="tpu_custom_call" | custom-call | tf_op jit(solution)/shard_map/feed_forward/pallas_call | solution.py:1177
  95.1 55.0 %backward_attention.1 = (bf16[2,1024,512]{2,1,0:T(8,128)(2,1)}, f32[576,128]{1,0:T(8,128)}, f32[192,128]{1,0:T(8,128)}, f32[144,128]{1,0:T(8,128)}) custom-call(s32[2,4]{1,0:T(2,128)} %lengths_ref.3, bf16[2,1024,512]{2,1,0:T(8,128)(2,1)} %get-tuple-element.50.q_ref, bf16[2,512,1024]{2,1,0:T(8,128)(2,1)} %get-tuple-element.51.qt_ref, ...), custom_call_target="tpu_custom_call" | custom-call | tf_op jit(solution)/shard_map/backward_attention/pallas_call | solution.py:1117
  150.1 2.7 %hand_out.1 = (bf16[2048,512]{1,0:T(8,128)(2,1)}, f32[64,128]{1,0:T(8,128)}, f32[64,128]{1,0:T(8,128)}, f32[64,128]{1,0:T(8,128)}, f32[64,128]{1,0:T(8,128)}, /*...) custom-call(f32[576,128]{1,0:T(8,128)} %get-tuple-element.63.late_in, ...), custom_call_target="tpu_custom_call" | custom-call | tf_op jit(solution)/shard_map/hand_out/pallas_call | solution.py:1159
